TPU v7x, 32 devices: a whole 2x2x4 slice. The times are simulated.
32 devices in a mesh: head: 8 (over z, x), ctx: 2 (over y), dp: 2 (over core).
Axes of the slice: x: 2, y: 2, z: 4, core: 2. Of those that a mesh axis runs over, the one named last changes fastest.
Arguments:
- query_nope: bfloat16 [2, 256, 128, 128], P('dp', 'ctx', 'head'), may hold values from -6 to 6
- query_rope: bfloat16 [2, 256, 128, 64], P('dp', 'ctx', 'head'), may hold values from -10 to 10
- query_pos: int32 [2, 256], P('dp', 'ctx'), may hold values from 64 to 255
- latent_cache: bfloat16 [2, 4, 64, 576], P('dp', 'ctx'), may hold values from -6 to 6
- block_table: int32 [2, 4], P('dp'), may hold values from 0 to 3, each once within a row
- key_up: bfloat16 [128, 128, 512], P('head'), may hold values from -0.5 to 0.5
- value_up: bfloat16 [128, 512, 128], P('head'), may hold values from -0.25 to 0.25
- grad_out: bfloat16 [2, 256, 128, 128], P('dp', 'ctx', 'head'), may hold values from -6 to 6
Outputs:
- grad_query_nope: float32 [2, 256, 128, 128], P('dp', 'ctx', 'head')
- grad_query_rope: float32 [2, 256, 128, 64], P('dp', 'ctx', 'head')
- grad_cache: float32 [2, 4, 64, 576], P('dp', 'ctx')
- grad_key_up: float32 [128, 128, 512], P('head', ('ctx', 'dp'))
- grad_value_up: float32 [128, 512, 128], P('head', ('ctx', 'dp'))
Inputs may be any that keep to these rules, and one draw needn't show every extreme that they name: Each row is a permutation: logical block b of sequence s lies in physical block block_table[s, b].
All inputs are finite; a program needn't handle non-finite values.
Results may differ from a plain program's by a relative error of at most 0.025.
Values may be sent and summed in bfloat16 or wider, within the bound.
No kernel may reach another device: no remote copies, remote signals or barrier semaphores. Data moves between devices by JAX's collectives and lax.ppermute only.
A program may use at most 64 MiB of HBM per device.

v0:
```python
import jax
import jax.numpy as jnp
from jax import lax
from jax.sharding import PartitionSpec as P

softmax_scale = 192.0 ** (-0.5)
neg_big = -1e30


def on_device(
    query_nope, query_rope, query_pos, latent_cache, block_table, key_up, value_up, grad_out
):
    latent_width = key_up.shape[2]
    page_rows = latent_cache.shape[2]
    row_width = latent_cache.shape[3]
    query_latent = jnp.einsum(
        "qhn,hnl->hql", query_nope[0], key_up, preferred_element_type=jnp.float32
    ).astype(jnp.bfloat16)
    query_rows = jnp.concatenate([query_latent, jnp.swapaxes(query_rope[0], 0, 1)], axis=2)
    grad_latent = jnp.einsum(
        "qhv,hlv->hql", grad_out[0], value_up, preferred_element_type=jnp.float32
    ).astype(jnp.bfloat16)
    query_position = query_pos[0]
    slot_table = block_table[0]
    own_rows = latent_cache[0].reshape(-1, row_width)
    head_rows = query_rows.shape[0]
    query_count = query_rows.shape[1]

    def positions(row_count):
        row_index = jnp.arange(row_count, dtype=jnp.int32)
        slot_index = row_index // page_rows
        logical = jnp.sum(
            jnp.where(
                slot_table[None, :] == slot_index[:, None],
                jnp.arange(slot_table.shape[0], dtype=jnp.int32)[None, :],
                0,
            ),
            axis=1,
        )
        return logical * page_rows + row_index % page_rows

    def scores_of(key_block):
        raw_scores = (
            jnp.einsum("hqc,kc->hqk", query_rows, key_block, preferred_element_type=jnp.float32)
            * softmax_scale
        )
        visible = positions(key_block.shape[0])[None, None, :] <= query_position[None, :, None]
        return jnp.where(visible, raw_scores, -jnp.inf)

    def probs_grad(key_block):
        return jnp.einsum(
            "hql,kl->hqk",
            grad_latent,
            key_block[:, :latent_width],
            preferred_element_type=jnp.float32,
        )

    key_block = lax.all_gather(own_rows, "ctx", axis=0, tiled=True)
    stats_row_max = jnp.full((head_rows, query_count), neg_big, jnp.float32)
    scores = scores_of(key_block)
    grad_probs = probs_grad(key_block)
    new_max = jnp.maximum(stats_row_max, jnp.max(scores, axis=2))
    weights = jnp.exp(scores - new_max[..., None])
    denominator = jnp.sum(weights, axis=2)
    weighted_sum = jnp.sum(weights * grad_probs, axis=2)
    row_delta = weighted_sum / denominator
    key_block = lax.all_gather(own_rows, "ctx", axis=0, tiled=True)
    scores = scores_of(key_block)
    attn_probs = jnp.exp(scores - new_max[..., None]) / denominator[..., None]
    grad_probs = probs_grad(key_block)
    probs_b = attn_probs.astype(jnp.bfloat16)
    grad_scores = (attn_probs * (grad_probs - row_delta[..., None]) * softmax_scale).astype(
        jnp.bfloat16
    )
    grad_query = jnp.einsum(
        "hqk,kc->hqc", grad_scores, key_block, preferred_element_type=jnp.float32
    )
    out_part = jnp.einsum(
        "hqk,kl->hql", probs_b, key_block[:, :latent_width], preferred_element_type=jnp.float32
    )
    grad_rows = jnp.einsum(
        "hqk,hqc->kc", grad_scores, query_rows, preferred_element_type=jnp.float32
    )
    grad_values = jnp.einsum(
        "hqk,hql->kl", probs_b, grad_latent, preferred_element_type=jnp.float32
    )
    grad_rows = grad_rows + jnp.pad(grad_values, ((0, 0), (0, row_width - latent_width)))
    grad_query, out_part, grad_rows = (grad_query, out_part, grad_rows)
    grad_all = grad_rows
    grad_query, out_sum, grad_all = (grad_query, out_part, grad_all)
    attn_out = out_sum.astype(jnp.bfloat16)
    grad_rope = jnp.swapaxes(grad_query[..., latent_width:], 0, 1)[None]
    grad_qlatent = grad_query[..., :latent_width].astype(jnp.bfloat16)
    grad_nope = jnp.einsum(
        "hql,hnl->qhn", grad_qlatent, key_up, preferred_element_type=jnp.float32
    )[None]
    key_part = jnp.einsum(
        "qhn,hql->hnl", query_nope[0], grad_qlatent, preferred_element_type=jnp.float32
    ).astype(jnp.bfloat16)
    value_part = jnp.einsum(
        "hql,qhv->hlv", attn_out, grad_out[0], preferred_element_type=jnp.float32
    ).astype(jnp.bfloat16)
    grad_key_map, grad_value_map = (
        lax.psum_scatter(key_part, ("ctx", "dp"), scatter_dimension=1, tiled=True).astype(
            jnp.float32
        ),
        lax.psum_scatter(value_part, ("ctx", "dp"), scatter_dimension=1, tiled=True).astype(
            jnp.float32
        ),
    )
    ctx_share = lax.psum_scatter(
        grad_all.astype(jnp.bfloat16), "ctx", scatter_dimension=0, tiled=True
    )
    cache_grad = lax.psum(ctx_share, "head").astype(jnp.float32)
    return (
        grad_nope,
        grad_rope,
        cache_grad.reshape(latent_cache.shape),
        grad_key_map,
        grad_value_map,
    )


def solution(mesh):
    placed = (
        P("dp", "ctx", "head", None),
        P("dp", "ctx", "head", None),
        P("dp", "ctx"),
        P("dp", "ctx", None, None),
        P("dp", None),
        P("head", None, None),
        P("head", None, None),
        P("dp", "ctx", "head", None),
    )
    return jax.shard_map(
        on_device,
        mesh=mesh,
        in_specs=placed,
        out_specs=(
            P("dp", "ctx", "head", None),
            P("dp", "ctx", "head", None),
            P("dp", "ctx", None, None),
            P("head", ("ctx", "dp"), None),
            P("head", ("ctx", "dp"), None),
        ),
        check_vma=False,
    )
```

profile of v0, /device:TPU:0, one launch (start us, length us, event | category | flops | bytes accessed | tf_op | source)
XLA Modules:
  0.0 132.2 jit_solution(11059883925541898286)
XLA Ops:
  8.0 0.0 reduce-scatter.10.cloned.1.call-start
  8.1 0.9 select_reduce_fusion
  9.0 1.1 copy.63
  10.0 7.5 %all_gather.4 = bf16[256,576]{0,1:T(8,128)(2,1)S(1)} all-gather(bf16[128,576]{0,1:T(8,128)(2,1)S(1)} %copy.63), channel_id=1, replica_groups=mesh['head'=8,'ctx'=2,'dp'=2] {'ctx'}, dimensions={0}, use_global_device_ids=true | all-gather | bytes 442368 | tf_op jit(solution)/shard_map/all_gather | solution.py:67
  17.5 1.2 copy.62
  18.8 0.8 broadcast_compare_fusion
  19.6 1.7 %convolution_convert_fusion.1 = bf16[16,128,512]{2,1,0:T(8,128)(2,1)S(1)} fusion(bf16[16,128,512]{2,1,0:T(8,128)(2,1)S(1)} %copy-done, bf16[128,16,128]{2,1,0:T(8,128)(2,1)} %bitcast.50), kind=kOutput, calls=%fused_computation.12 | convolution fusion | flops 269484032 | bytes 4718592 | tf_op jit(solution)/shard_map/qhn,hnl->hql/dot_general | solution.py:16
  21.3 1.1 fusion.7
  22.4 0.5 copy-done.2
  22.9 0.1 copy-done.5
  23.0 0.7 convolution_convert_fusion
  23.7 1.5 %fusion.14 = (f32[16,128]{1,0:T(8,128)S(1)}, f32[16,128]{1,0:T(8,128)S(1)}, f32[16,128,256]{2,1,0:T(8,128)S(1)}) fusion(f32[16,128,256]{2,1,0:T(8,128)S(1)} %get-tuple-element.28, f32[16,128]{1,0:T(8,128)S(1)} %broadcast_maximum_fusion, pred[128,256]{1,0:T(8,128)(4,1)S(1)} %broadcast_compare_fusion, bf16[16,128,512]{2,1,0:T(8,128)(2,1)S(1)} %convolution_convert_fusion, ...), kind=kOutput, calls=%fused_computation.22 | convolution fusion | flops 540012544 | bytes 6610944 | tf_op jit(solution)/shard_map/hql,kl->hqk/dot_general | solution.py:51
  25.2 1.6 %convolution_bitcast_fusion.1 = f32[256,512]{0,1:T(8,128)S(1)} fusion(bf16[16,128,512]{2,1,0:T(8,128)(2,1)S(1)} %convolution_convert_fusion, f32[16,128,256]{2,1,0:T(8,128)S(1)} %get-tuple-element.28, f32[16,128]{1,0:T(8,128)S(1)} %get-tuple-element.25, f32[16,128]{1,0:T(8,128)S(1)} %broadcast_maximum_fusion, pred[128,256]{1,0:T(8,128)(4,1)S(1)} %broadcast_compare_fusion), kind=kOutput, calls=%fused_computation.18 | convolution fusion | flops 539492352 | bytes 4767744 | tf_op jit(solution)/shard_map/hqk,hql->kl/dot_general | solution.py:84
  26.8 1.0 multiply_convert_fusion
  27.8 1.8 %fusion.12 = bf16[256,576]{0,1:T(8,128)(2,1)} fusion(bf16[16,128,256]{2,1,0:T(8,128)(2,1)S(1)} %multiply_convert_fusion, bf16[16,128,64]{2,1,0:T(8,128)(2,1)S(1)} %bitcast.55, bf16[16,128,512]{2,1,0:T(8,128)(2,1)S(1)} %convolution_convert_fusion.1, f32[256,512]{0,1:T(8,128)S(1)} %convolution_bitcast_fusion.1), kind=kOutput, calls=%fused_computation.20 | convolution fusion | flops 608993280 | bytes 4227072 | tf_op jit(solution)/shard_map/hqk,hqc->kc/dot_general | solution.py:81
  29.7 1.9 %copy.90 = bf16[256,576]{1,0:T(8,128)(2,1)} copy(bf16[256,576]{0,1:T(8,128)(2,1)} %fusion.12) | data formatting | bytes 589824
  31.6 0.0 all-reduce.3.cloned.1.call-start
  31.6 14.0 %reduce-scatter.10.cloned.1.call-done = bf16[128,576]{1,0:T(8,128)(2,1)} async-done(((bf16[256,576]{1,0:T(8,128)(2,1)}), bf16[128,576]{1,0:T(8,128)(2,1)}) %reduce-scatter.10.cloned.1.call-update) | async-done | bytes 147472 | tf_op jit(solution)/shard_map/reduce_scatter | solution.py:111
  45.6 0.0 reduce-scatter.8.cloned.1.call-start
  45.7 4.5 %fusion.4 = bf16[16,512,128]{2,1,0:T(8,128)(2,1)} fusion(bf16[128,16,128]{2,1,0:T(8,128)(2,1)} %bitcast.52, bf16[256,576]{0,1:T(8,128)(2,1)S(1)} %all_gather.4, f32[16,128,256]{2,1,0:T(8,128)} %copy-done.3, f32[16,128]{1,0:T(8,128)S(1)} %get-tuple-element.25, f32[16,128]{1,0:T(8,128)S(1)} %broadcast_maximum_fusion, ...), kind=kOutput, calls=%fused_computation.10 | convolution fusion | flops 810024960 | bytes 5029888 | tf_op jit(solution)/shard_map/hql,qhv->hlv/dot_general | solution.py:100
  50.2 0.2 reduce-scatter.6.cloned.1.call-start
  50.4 0.8 fusion.22
  51.2 2.1 %copy-done.1 = f32[16,128,576]{1,2,0:T(8,128)} copy-done((f32[16,128,576]{1,2,0:T(8,128)}, f32[16,128,576]{1,2,0:T(8,128)S(1)}, u32[]{:S(2)}) %copy-start.1) | copy-done | bytes 4718616
  53.4 2.1 %convert_bitcast_fusion = bf16[16,128,512]{1,2,0:T(8,128)(2,1)} fusion(f32[16,128,576]{1,2,0:T(8,128)S(1)} %fusion.22, bf16[128,16,128]{2,1,0:T(8,128)(2,1)S(1)} %bitcast.51), kind=kOutput, calls=%fused_computation.5 | convolution fusion | flops 269484032 | bytes 4718592 | tf_op jit(solution)/shard_map/qhn,hql->hnl/dot_general | solution.py:97
  55.4 4.7 %copy.73 = bf16[16,128,512]{2,0,1:T(8,128)(2,1)} copy(bf16[16,128,512]{1,2,0:T(8,128)(2,1)} %convert_bitcast_fusion) | data formatting | bytes 4194304 | tf_op jit(solution)/shard_map/convert_element_type | solution.py:99
  60.2 3.0 %convolution_bitcast_fusion = f32[1,128,16,128]{3,1,2,0:T(8,128)S(1)} fusion(bf16[16,128,512]{2,1,0:T(8,128)(2,1)S(1)} %copy-done, f32[16,128,576]{1,2,0:T(8,128)} %copy-done.1), kind=kOutput, calls=%fused_computation.16 | convolution fusion | flops 268435456 | bytes 5242880 | tf_op jit(solution)/shard_map/hql,hnl->qhn/dot_general | solution.py:94
  63.1 1.6 %copy.77 = f32[1,128,16,128]{3,2,1,0:T(8,128)} copy(f32[1,128,16,128]{3,1,2,0:T(8,128)S(1)} %convolution_bitcast_fusion) | data formatting | bytes 2097152
  64.7 1.9 %slice_bitcast_fusion = f32[1,128,16,64]{1,3,2,0:T(8,128)} fusion(f32[16,128,576]{1,2,0:T(8,128)} %copy-done.1), kind=kLoop, calls=%fused_computation.23 | loop fusion | bytes 1048576 | tf_op jit(solution)/shard_map/broadcast_in_dim | solution.py:92
  66.6 52.1 %all-reduce.3.cloned.1.call-done = bf16[1,2,64,576]{3,2,1,0:T(8,128)(2,1)} async-done(((bf16[1,2,64,576]{3,2,1,0:T(8,128)(2,1)}), bf16[1,2,64,576]{3,2,1,0:T(8,128)(2,1)}) %all-reduce.3.cloned.1.call-update) | async-done | bytes 147472 | tf_op jit(solution)/shard_map/psum | solution.py:114
  118.7 1.7 %reshape.85 = f32[1,2,64,576]{3,2,1,0:T(8,128)} convert(bf16[1,2,64,576]{3,2,1,0:T(8,128)(2,1)} %all-reduce.3.cloned.1.call-done) | non-fusion elementwise | flops 73728 | bytes 442368 | tf_op jit(solution)/shard_map/reshape | solution.py:118
  120.4 2.1 %convert_element_type.47 = f32[16,128,128]{2,1,0:T(8,128)} convert(bf16[16,128,128]{2,1,0:T(8,128)(2,1)} %reduce-scatter.8.cloned.1.call-done) | non-fusion elementwise | flops 262144 | bytes 1572864 | tf_op jit(solution)/shard_map/convert_element_type | solution.py:107
  122.5 2.3 %copy.78 = f32[16,32,512]{2,1,0:T(8,128)} copy(bf16[16,32,512]{2,0,1:T(8,128)(2,1)} %reduce-scatter.6.cloned.1.call-done) | data formatting | bytes 1572864
  (23 shorter events, 0.1 us)
Async XLA Ops:
  8.0 11.5 %copy-start = (bf16[16,128,512]{2,1,0:T(8,128)(2,1)S(1)}, bf16[16,128,512]{2,1,0:T(8,128)(2,1)}, u32[]{:S(2)}) copy-start(bf16[16,128,512]{2,1,0:T(8,128)(2,1)} %param.13) | copy-start | bytes 6291460
  8.0 37.6 %reduce-scatter.10.cloned.1.call-start = ((), (), s32[]{:S(2)}) async-start(), calls=%async_computation.6 | async-start | bytes 491520 | tf_op jit(solution)/shard_map/reduce_scatter | solution.py:111
  18.8 2.5 %copy-start.6 = (bf16[1,128,16,64]{3,1,2,0:T(8,128)(2,1)}, bf16[1,128,16,64]{3,1,2,0:T(8,128)(2,1)S(1)}, u32[]{:S(2)}) copy-start(bf16[1,128,16,64]{3,1,2,0:T(8,128)(2,1)S(1)} %copy.62) | copy-start | bytes 786436
  21.3 1.6 %copy-start.2 = (bf16[16,512,128]{2,1,0:T(8,128)(2,1)S(1)}, bf16[16,512,128]{2,1,0:T(8,128)(2,1)}, u32[]{:S(2)}) copy-start(bf16[16,512,128]{2,1,0:T(8,128)(2,1)} %param.14) | copy-start | bytes 6291460
  21.3 1.7 %copy-start.5 = (bf16[1,128,16,128]{3,2,1,0:T(8,128)(2,1)S(1)}, bf16[1,128,16,128]{3,2,1,0:T(8,128)(2,1)}, u32[]{:S(2)}) copy-start(bf16[1,128,16,128]{3,2,1,0:T(8,128)(2,1)} %param.15) | copy-start | bytes 1572868
  22.4 4.4 %copy-start.3 = (f32[16,128,256]{2,1,0:T(8,128)}, f32[16,128,256]{2,1,0:T(8,128)S(1)}, u32[]{:S(2)}) copy-start(f32[16,128,256]{2,1,0:T(8,128)S(1)} %get-tuple-element.28) | copy-start | bytes 6291460
  26.8 1.0 copy-start.7
  31.6 87.1 %all-reduce.3.cloned.1.call-start = ((), (), s32[]{:S(2)}) async-start(), calls=%async_computation.3 | async-start | bytes 327680 | tf_op jit(solution)/shard_map/psum | solution.py:114
  45.6 74.7 %reduce-scatter.8.cloned.1.call-start = ((), (), s32[]{:S(2)}) async-start(), calls=%async_computation.5 | async-start | bytes 2621440 | tf_op jit(solution)/shard_map/reduce_scatter | solution.py:107
  50.2 72.3 %reduce-scatter.6.cloned.1.call-start = ((), (), s32[]{:S(2)}) async-start(), calls=%async_computation.4 | async-start | bytes 2621440 | tf_op jit(solution)/shard_map/reduce_scatter | solution.py:104
  50.4 3.0 %copy-start.4 = (bf16[1,128,16,128]{3,2,1,0:T(8,128)(2,1)S(1)}, bf16[1,128,16,128]{3,2,1,0:T(8,128)(2,1)}, u32[]{:S(2)}) copy-start(bf16[1,128,16,128]{3,2,1,0:T(8,128)(2,1)} %param.8) | copy-start | bytes 1572868
  51.2 2.1 %copy-start.1 = (f32[16,128,576]{1,2,0:T(8,128)}, f32[16,128,576]{1,2,0:T(8,128)S(1)}, u32[]{:S(2)}) copy-start(f32[16,128,576]{1,2,0:T(8,128)S(1)} %fusion.22) | copy-start | bytes 14155780
Sparse Core Ops, SparseCore 0:
  31.7 13.8 reduce-scatter.9
  49.3 69.3 all-reduce.2
Sparse Core Ops, SparseCore 1:
  50.3 31.3 reduce-scatter.7
  84.2 31.3 reduce-scatter.5
where the time goes:
time: 133 us; the launch traced here: 132 us
  waiting for transfers between devices  66.1 us (50%)
  matrix products  18.7 us (14%)
  local copies, waits for them, and re-layouts  17.3 us (13%)
  between operations  15.7 us (12%)
  blocking collectives  7.52 us (6%)
  other arithmetic  6.47 us (5%)
    psum x1, waiting for transfers between devices, on_device(): cache_grad = lax.psum(ctx_share, 'head').astype(jnp.float32)  52.1 us
    reduce_scatter x1, waiting for transfers between devices, on_device(): lax.psum_scatter(grad_all.astype(jnp.bfloat16), 'ctx', scatter_dimension=...  14 us
    unnamed x20, local copies, waits for them, and re-layouts  9.7 us
    all_gather x1, blocking collectives, on_device(): key_block = lax.all_gather(own_rows, 'ctx', axis=0, tiled=True)  7.52 us
    convert_element_type x1, local copies, waits for them, and re-layouts, on_device(): key_part = jnp.einsum('qhn,hql->hnl', query_nope[0], grad_qlatent, prefer...  4.71 us
    dot_general x1, matrix products, on_device(): jnp.einsum('hql,qhv->hlv', attn_out, grad_out[0], preferred_element_type=...  4.47 us
    dot_general x1, matrix products, on_device(): jnp.einsum('hql,hnl->qhn', grad_qlatent, key_up, preferred_element_type=j...  2.95 us
  transfers between devices with their start and end apart: 4, of which 2 were waited for; matrix products, arithmetic and copies ran while one was open for 17% of the time, Pallas kernels for 0%

commit v1 on v0

v1 whole, which is shorter than its diff:
```python
import functools

import jax
import jax.numpy as jnp
from jax import lax
from jax.experimental import pallas as pl
from jax.experimental.pallas import tpu as pltpu
from jax.sharding import PartitionSpec as P

softmax_scale = 192.0 ** (-0.5)
F32 = jnp.float32
BF16 = jnp.bfloat16
VMEM_LIMIT = 56 * 1024 * 1024


def dot_nn(a, b):
    return lax.dot_general(a, b, (((1,), (0,)), ((), ())), preferred_element_type=F32)


def dot_nt(a, b):
    return lax.dot_general(a, b, (((1,), (1,)), ((), ())), preferred_element_type=F32)


def dot_tn(a, b):
    return lax.dot_general(a, b, (((0,), (0,)), ((), ())), preferred_element_type=F32)


def main_kernel(
    paired, page_rows, latent_width,
    place_ref, table_ref, pos_ref, keys_ref, qcat_ref, qt_ref, go_ref, ku_ref, vu_ref,
    ds_ref, kn_ref, *rest,
):
    if paired:
        keep0, keep1, send0, send1, mine_ref, other_ref, vt_ref, bp_ref, acc_ref = rest
    else:
        wk_ref, wv_ref, all_ref, vt_ref, bp_ref, acc_ref = rest
    heads, nope_width = ku_ref.shape[0], ku_ref.shape[1]
    value_width = vu_ref.shape[2]
    key_count, row_width = keys_ref.shape
    query_count = go_ref.shape[1]
    blocks = table_ref.shape[0]
    step = pl.program_id(0)
    last = pl.num_programs(0) - 1
    latent = keys_ref[:, :latent_width]
    rotary = keys_ref[:, latent_width:]
    nope_slice, value_slice = bp_ref.shape[1] // heads, vt_ref.shape[1]
    slices = vt_ref.shape[0]

    def place_of(s):
        if not paired:
            return s
        return jnp.bitwise_xor(s % 2, place_ref[1]) * 2 + jnp.bitwise_xor(s // 2, place_ref[0])

    @pl.when(step == 0)
    def _():
        acc_ref[...] = jnp.zeros_like(acc_ref)
        turned = jnp.transpose(latent.astype(F32)).astype(BF16)
        for s in range(slices):
            vt_ref[place_of(s)] = turned[s * value_slice:(s + 1) * value_slice]

    row = lax.broadcasted_iota(jnp.int32, (page_rows, query_count), 0)
    positions = []
    for slot in range(blocks):
        logical = jnp.int32(0)
        for b in range(blocks):
            logical = logical + jnp.where(table_ref[b] == slot, b, 0)
        positions.append(row + logical * page_rows)
    visible = jnp.concatenate(positions, axis=0) <= pos_ref[...]

    kn = dot_nt(latent, ku_ref[...].reshape(heads * nope_width, latent_width)).astype(BF16)
    vu = jnp.concatenate([vu_ref[h] for h in range(heads)], axis=1)
    values = dot_nn(latent, vu).astype(BF16)
    gkn_all, gv_all = [], []
    rotary_sum = None
    for h in range(heads):
        kn_h = kn[:, h * nope_width:(h + 1) * nope_width]
        kn_ref[h] = kn_h
        kcat = jnp.concatenate([kn_h, rotary], axis=1)
        qcat = qcat_ref[h]
        scores = dot_nt(kcat, qcat) * softmax_scale
        scores = jnp.where(visible, scores, -jnp.inf)
        grad_probs = dot_nt(values[:, h * value_width:(h + 1) * value_width], go_ref[h])
        top = jnp.max(scores, axis=0, keepdims=True)
        weights = jnp.exp(scores - top)
        inverse = 1.0 / jnp.sum(weights, axis=0, keepdims=True)
        probs = weights * inverse
        delta = jnp.sum(probs * grad_probs, axis=0, keepdims=True)
        ds = (probs * (grad_probs - delta) * softmax_scale).astype(BF16)
        ds_ref[h] = ds
        gk = dot_nn(ds, qcat)
        gkn_all.append(gk[:, :nope_width].astype(BF16))
        rotary_sum = gk[:, nope_width:] if rotary_sum is None else rotary_sum + gk[:, nope_width:]
        gv_all.append(dot_nn(probs.astype(BF16), go_ref[h]).astype(BF16))
        b = dot_nt(qt_ref[h], ds).astype(BF16)
        for s in range(slices):
            bp_ref[place_of(s), h * nope_slice:(h + 1) * nope_slice] = b[s * nope_slice:(s + 1) * nope_slice]
    gkn = jnp.concatenate(gkn_all, axis=1)
    gv = jnp.concatenate(gv_all, axis=1)
    acc_ref[:, :latent_width] += dot_nn(gkn, ku_ref[...].reshape(heads * nope_width, latent_width)) + dot_nt(gv, vu)
    acc_ref[:, latent_width:] += rotary_sum
    outs = (keep0, keep1, send0, send1) if paired else (None,) * slices
    for s in range(slices):
        key_part = dot_nn(bp_ref[s], latent).astype(BF16)
        value_part = dot_nn(vt_ref[s], gv).astype(BF16)
        for h in range(heads):
            rows = key_part[h * nope_slice:(h + 1) * nope_slice]
            columns = value_part[:, h * value_width:(h + 1) * value_width]
            if paired:
                for j in range(latent_width // value_width):
                    outs[s][h, 0, j * nope_slice:(j + 1) * nope_slice] = rows[:, j * value_width:(j + 1) * value_width]
                outs[s][h, 1] = columns
            else:
                wk_ref[h, s * nope_slice:(s + 1) * nope_slice] = rows
                wv_ref[h, s * value_slice:(s + 1) * value_slice] = columns

    @pl.when(step == last)
    def _():
        if paired:
            half = key_count // 2
            begin = pl.multiple_of(place_ref[0] * half, half)
            away = pl.multiple_of((1 - place_ref[0]) * half, half)
            mine_ref[...] = acc_ref[pl.ds(begin, half)].astype(BF16)
            other_ref[...] = acc_ref[pl.ds(away, half)].astype(BF16)
        else:
            all_ref[...] = acc_ref[...].astype(BF16)


def attention_backward(paired, place, table, pos, keys, qcat, qt, go, key_up, value_up, page_rows, group):
    heads, nope_width, latent_width = key_up.shape
    value_width = value_up.shape[2]
    query_count = go.shape[1]
    key_count, row_width = keys.shape
    slices = 4 if paired else 1
    by_head = lambda *dims: pl.BlockSpec((group,) + dims, lambda i: (i,) + (0,) * len(dims))
    whole = lambda *dims: pl.BlockSpec(dims, lambda i: (0,) * len(dims))
    smem = pl.BlockSpec(memory_space=pltpu.SMEM)
    out = lambda *dims: jax.ShapeDtypeStruct(dims, BF16)
    shapes = [out(heads, key_count, query_count), out(heads, key_count, nope_width)]
    specs = [by_head(key_count, query_count), by_head(key_count, nope_width)]
    if paired:
        depth = latent_width // slices
        shapes += [out(heads, 2, depth, value_width)] * 4 + [out(key_count // 2, row_width)] * 2
        specs += [by_head(2, depth, value_width)] * 4 + [whole(key_count // 2, row_width)] * 2
    else:
        shapes += [out(heads, nope_width, latent_width), out(heads, latent_width, value_width), out(key_count, row_width)]
        specs += [by_head(nope_width, latent_width), by_head(latent_width, value_width), whole(key_count, row_width)]
    return pl.pallas_call(
        functools.partial(main_kernel, paired, page_rows, latent_width),
        grid=(heads // group,),
        in_specs=[
            smem, smem, whole(1, query_count), whole(key_count, row_width),
            by_head(query_count, qcat.shape[2]), by_head(nope_width, query_count), by_head(query_count, value_width),
            by_head(nope_width, latent_width), by_head(latent_width, value_width),
        ],
        out_specs=specs,
        out_shape=shapes,
        scratch_shapes=[
            pltpu.VMEM((slices, latent_width // slices, key_count), BF16),
            pltpu.VMEM((slices, group * nope_width // slices, key_count), BF16),
            pltpu.VMEM((key_count, row_width), F32),
        ],
        compiler_params=pltpu.CompilerParams(vmem_limit_bytes=VMEM_LIMIT),
        cost_estimate=pl.CostEstimate(flops=6_000_000_000, bytes_accessed=12_000_000, transcendentals=0),
        name="attention_backward",
    )(place, table, pos, keys, qcat, qt, go, key_up, value_up)


def query_kernel(ds_ref, kn_ref, rotary_ref, nope_ref, rope_ref):
    nope_width = kn_ref.shape[2]
    heads = ds_ref.shape[0]
    query_count = ds_ref.shape[2]
    rotary = rotary_ref[...]
    for h in range(heads):
        kcat = jnp.concatenate([kn_ref[h], rotary], axis=1)
        gq = dot_tn(ds_ref[h], kcat)
        nope_ref[pl.ds(h, query_count, stride=heads), :] = gq[:, :nope_width]
        rope_ref[pl.ds(h, query_count, stride=heads), :] = gq[:, nope_width:]


def query_gradient(ds, kn, rotary):
    heads, key_count, query_count = ds.shape
    nope_width, rope_width = kn.shape[2], rotary.shape[1]
    nope, rope = pl.pallas_call(
        query_kernel,
        out_shape=[
            jax.ShapeDtypeStruct((query_count * heads, nope_width), F32),
            jax.ShapeDtypeStruct((query_count * heads, rope_width), F32),
        ],
        compiler_params=pltpu.CompilerParams(vmem_limit_bytes=VMEM_LIMIT),
        cost_estimate=pl.CostEstimate(flops=1_000_000_000, bytes_accessed=5_000_000, transcendentals=0),
        name="query_gradient",
    )(ds, kn, rotary)
    return nope.reshape(1, query_count, heads, nope_width), rope.reshape(1, query_count, heads, rope_width)


def finish_kernel(own_ref, near_ref, far_ref, key_ref, value_ref):
    rows = key_ref.shape[1]
    width = own_ref.shape[3]
    for h in range(key_ref.shape[0]):
        total = own_ref[h].astype(F32) + near_ref[h].astype(F32) + far_ref[h].astype(F32)
        for j in range(key_ref.shape[2] // width):
            key_ref[h, :, j * width:(j + 1) * width] = total[0, j * rows:(j + 1) * rows]
        value_ref[h] = total[1]


def finish(own, near, far, group):
    heads, _, depth, width = own.shape
    rows = depth // 4
    return pl.pallas_call(
        finish_kernel,
        grid=(heads // group,),
        in_specs=[pl.BlockSpec((group, 2, depth, width), lambda i: (i, 0, 0, 0))] * 3,
        out_specs=[
            pl.BlockSpec((group, rows, 4 * width), lambda i: (i, 0, 0)),
            pl.BlockSpec((group, depth, width), lambda i: (i, 0, 0)),
        ],
        out_shape=[
            jax.ShapeDtypeStruct((heads, rows, 4 * width), F32),
            jax.ShapeDtypeStruct((heads, depth, width), F32),
        ],
        compiler_params=pltpu.CompilerParams(vmem_limit_bytes=VMEM_LIMIT),
        name="finish",
    )(own, near, far)


def swap(x, axis, size, bits):
    return lax.ppermute(x, axis, [(i, i ^ bits) for i in range(size)])


def on_device(
    sizes, query_nope, query_rope, query_pos, latent_cache, block_table, key_up, value_up, grad_out
):
    head_size, ctx_size, dp_size = sizes
    heads, nope_width, latent_width = key_up.shape
    value_width = value_up.shape[2]
    page_rows, row_width = latent_cache.shape[2:]
    paired = (
        ctx_size == 2 and dp_size == 2 and latent_width == 4 * value_width and nope_width == value_width
        and nope_width % 64 == 0 and value_width % 128 == 0 and heads % 8 == 0
    )
    own_rows = latent_cache[0].reshape(-1, row_width)
    if ctx_size == 2:
        other_rows = swap(own_rows, "ctx", 2, 1)
        first = lax.axis_index("ctx") == 0
        keys = jnp.concatenate(
            [jnp.where(first, own_rows, other_rows), jnp.where(first, other_rows, own_rows)], axis=0
        )
    else:
        keys = lax.all_gather(own_rows, "ctx", axis=0, tiled=True)
    qcat = jnp.swapaxes(jnp.concatenate([query_nope[0], query_rope[0]], axis=2), 0, 1)
    qt = jnp.transpose(query_nope[0], (1, 2, 0))
    go = jnp.swapaxes(grad_out[0], 0, 1)
    place = jnp.stack([lax.axis_index("ctx"), lax.axis_index("dp")]).astype(jnp.int32)
    group = 4 if heads % 4 == 0 else 1
    results = attention_backward(
        paired, place, block_table[0], query_pos, keys, qcat, qt, go, key_up, value_up, page_rows, group
    )
    ds, kn = results[:2]
    rotary = keys[:, latent_width:]
    if heads % 8 == 0:
        grad_nope, grad_rope = query_gradient(ds, kn, rotary)
    else:
        grad_nope = jnp.einsum("hkq,hkn->qhn", ds, kn, preferred_element_type=F32)[None]
        grad_rope = jnp.einsum("hkq,kr->qhr", ds, rotary, preferred_element_type=F32)[None]

    if paired:
        keep0, keep1, send0, send1, mine, other = results[2:]
        near1 = swap(send1, "dp", 2, 1)
        share = mine.astype(F32) + swap(other, "ctx", 2, 1).astype(F32)
        near0 = swap(send0, "dp", 2, 1)
        far = swap((keep1.astype(F32) + near1.astype(F32)).astype(BF16), "ctx", 2, 1)
    else:
        wk, wv, rows = results[2:]
        grad_key_map = lax.psum_scatter(wk, ("ctx", "dp"), scatter_dimension=1, tiled=True).astype(F32)
        grad_value_map = lax.psum_scatter(wv, ("ctx", "dp"), scatter_dimension=1, tiled=True).astype(F32)
        share = lax.psum_scatter(rows, "ctx", scatter_dimension=0, tiled=True).astype(F32)
    if head_size & (head_size - 1) == 0:
        bits = 1
        while bits < head_size:
            rounded = share.astype(BF16)
            got = swap(rounded, "head", head_size, bits | (bits >> 1) if bits >= 4 else bits)
            share = rounded.astype(F32) + got.astype(F32)
            bits *= 2
    else:
        share = lax.psum(share.astype(BF16), "head").astype(F32)
    if paired:
        grad_key_map, grad_value_map = finish(keep0, near0, far, 4)
    return (
        grad_nope,
        grad_rope,
        share.reshape(latent_cache.shape),
        grad_key_map,
        grad_value_map,
    )


def solution(mesh):
    sizes = tuple(mesh.shape[axis] for axis in ("head", "ctx", "dp"))
    placed = (
        P("dp", "ctx", "head", None),
        P("dp", "ctx", "head", None),
        P("dp", "ctx"),
        P("dp", "ctx", None, None),
        P("dp", None),
        P("head", None, None),
        P("head", None, None),
        P("dp", "ctx", "head", None),
    )
    return jax.shard_map(
        functools.partial(on_device, sizes),
        mesh=mesh,
        in_specs=placed,
        out_specs=(
            P("dp", "ctx", "head", None),
            P("dp", "ctx", "head", None),
            P("dp", "ctx", None, None),
            P("head", ("ctx", "dp"), None),
            P("head", ("ctx", "dp"), None),
        ),
        check_vma=False,
    )
```

time: 133 us -> 64.6 us (0.49)
  waiting for transfers between devices: 66.1 us -> 16.8 us
  Pallas kernels: 0 us -> 21.4 us
  matrix products: 18.7 us -> 0 us
  between operations: 15.7 us -> 0.73 us
  starting transfers between devices: 0.35 us -> 11.4 us
  local copies, waits for them, and re-layouts: 17.3 us -> 7.08 us
  blocking collectives: 7.52 us -> 0 us
    psum x1 -> x0, waiting for transfers between devices: 52.1 us -> none  [on_device(): cache_grad = lax.psum(ctx_share, 'head').astype(jnp.float32)]
    pallas_call x0 -> x3, Pallas kernels: none -> 21.4 us  [the longest x1 13.6 us: attention_backward(): pl.pallas_call(functools.partial(main_kernel, paired, page_rows, latent_w...]
    dot_general x10 -> x0, matrix products: 18.7 us -> none  [the longest x1 4.47 us: on_device(): jnp.einsum('hql,qhv->hlv', attn_out, grad_out[0], preferred_element_type=...]
    ppermute x0 -> x8, waiting for transfers between devices: none -> 16.8 us  [swap(): return lax.ppermute(x, axis, [(i, i ^ bits) for i in range(size)])]
    reduce_scatter x3 -> x0, waiting for transfers between devices: 14 us -> none  [the longest x1 14 us: on_device(): lax.psum_scatter(grad_all.astype(jnp.bfloat16), 'ctx', scatter_dimension=...]
    ppermute x0 -> x8, starting transfers between devices: none -> 11.4 us  [swap(): return lax.ppermute(x, axis, [(i, i ^ bits) for i in range(size)])]
    all_gather x1 -> x0, blocking collectives: 7.52 us -> none  [on_device(): key_block = lax.all_gather(own_rows, 'ctx', axis=0, tiled=True)]
    convert_element_type x1 -> x0, local copies, waits for them, and re-layouts: 4.71 us -> none  [on_device(): key_part = jnp.einsum('qhn,hql->hnl', query_nope[0], grad_qlatent, prefer...]
  transfers between devices with their start and end apart: 4 -> 8, of which waited for: 2 -> 4; matrix products, arithmetic and copies ran while one was open for 17% -> 19% of each run, Pallas kernels for 0% -> 6%
where the time goes in v1:
time: 64.6 us; the launch traced here: 64.1 us
  Pallas kernels  21.4 us (33%)
  waiting for transfers between devices  16.8 us (26%)
  starting transfers between devices  11.4 us (18%)
  local copies, waits for them, and re-layouts  7.08 us (11%)
  other arithmetic  6.66 us (10%)
  between operations  0.73 us (1%)
    ppermute x8, waiting for transfers between devices, swap(): return lax.ppermute(x, axis, [(i, i ^ bits) for i in range(size)])  16.8 us
    pallas_call x1, Pallas kernels, attention_backward(): pl.pallas_call(functools.partial(main_kernel, paired, page_rows, latent_w...  13.6 us
    ppermute x8, starting transfers between devices, swap(): return lax.ppermute(x, axis, [(i, i ^ bits) for i in range(size)])  11.4 us
    unnamed x13, local copies, waits for them, and re-layouts  5.79 us
    pallas_call x1, Pallas kernels, finish(): pl.pallas_call(finish_kernel, grid=(heads // group,), in_specs=[pl.BlockS...  4 us
    pallas_call x1, Pallas kernels, query_gradient(): pl.pallas_call(query_kernel, out_shape=[jax.ShapeDtypeStruct((query_count...  3.87 us
    convert_element_type x1, other arithmetic, on_device(): (keep1.astype(F32) + near1.astype(F32)).astype(BF16)  1.59 us
    concatenate x2, other arithmetic, on_device(): jnp.concatenate([jnp.where(first, own_rows, other_rows), jnp.where(first,...  1.4 us
  transfers between devices with their start and end apart: 8, of which 4 were waited for; matrix products, arithmetic and copies ran while one was open for 19% of the time, Pallas kernels for 6%

profile of v1, /device:TPU:0, one launch (start us, length us, event | category | flops | bytes accessed | tf_op | source)
XLA Modules:
  0.0 64.1 jit_solution(4219323777195379837)
XLA Ops:
  0.6 3.0 %collective-permute-start = (bf16[128,576]{1,0:T(8,128)(2,1)}, bf16[128,576]{1,0:T(8,128)(2,1)S(1)}, u32[]{:S(2)}, u32[]{:S(2)}) collective-permute-start(bf16[128,576]{1,0:T(8,128)(2,1)} %bitcast.26), channel_id=1, source_target_pairs={{0,2},{2,0},{1,3},{3,1},{4,6},{6,4},{5,7},{7,5},{8,10},{10,8},{9,1... | collective-permute-start | bytes 442376 | tf_op jit(solution)/shard_map/ppermute | solution.py:227
  3.7 1.5 %copy.13 = bf16[1,128,16,128]{1,3,2,0:T(8,128)(2,1)S(1)} copy(bf16[1,128,16,128]{3,2,1,0:T(8,128)(2,1)} %param.8) | data formatting | bytes 1048576 | tf_op args[0]
  5.1 0.0 copy-start
  5.1 0.0 copy-start.4
  5.2 1.2 %maximum_bitcast_fusion = bf16[16,128,192]{1,2,0:T(8,128)(2,1)S(1)} fusion(bf16[128,16,64]{0,2,1:T(8,128)(2,1)} %bitcast.25, bf16[128,16,128]{0,2,1:T(8,128)(2,1)S(1)} %bitcast.20), kind=kLoop, calls=%fused_computation.1 | loop fusion | flops 1572864 | bytes 1572864 | tf_op jit(solution)/shard_map/transpose | solution.py:250
  6.4 0.9 %copy.18 = bf16[1,128,16,128]{3,1,2,0:T(8,128)(2,1)} copy(bf16[1,128,16,128]{3,2,1,0:T(8,128)(2,1)S(1)} %copy-done.3) | data formatting | bytes 1048576 | tf_op args[7]
  7.4 1.3 %copy.15.qcat_ref = bf16[16,128,192]{2,1,0:T(8,128)(2,1)} copy(bf16[16,128,192]{1,2,0:T(8,128)(2,1)S(1)} %maximum_bitcast_fusion) | data formatting | bytes 1572864 | tf_op jit(solution)/shard_map/transpose | solution.py:250
  8.6 0.6 pad_add_fusion.place_ref
  9.2 0.0 collective-permute-done
  9.3 0.8 %pad_maximum_fusion.keys_ref = bf16[256,576]{1,0:T(8,128)(2,1)} fusion(bf16[128,576]{1,0:T(8,128)(2,1)S(1)} %get-tuple-element.35, bf16[128,576]{1,0:T(8,128)(2,1)S(1)} %get-tuple-element.34), kind=kLoop, calls=%fused_computation.4 | loop fusion | flops 589824 | bytes 589824 | tf_op jit(solution)/shard_map/concatenate | solution.py:245
  10.1 13.6 %attention_backward.1 = (bf16[16,256,128]{2,1,0:T(8,128)(2,1)}, bf16[16,256,128]{2,1,0:T(8,128)(2,1)}, bf16[16,2,128,128]{3,2,1,0:T(8,128)(2,1)}, bf16[16,2,128,...) custom-call(s32[2]{0:T(128)} %pad_add_fusion.place_ref, ...), custom_call_target="tpu_custom_call" | custom-call | flops 6000000000 | bytes 12000000 | tf_op jit(solution)/shard_map/attention_backward/pallas_call | solution.py:147
  23.6 0.1 collective-permute-start.6
  23.7 0.6 %collective-permute-start.1 = (bf16[128,576]{1,0:T(8,128)(2,1)}, bf16[128,576]{1,0:T(8,128)(2,1)S(1)}, u32[]{:S(2)}, u32[]{:S(2)}) collective-permute-start(bf16[128,576]{1,0:T(8,128)(2,1)} %get-tuple-element.22), channel_id=1, source_target_pairs={{0,2},{2,0},{1,3},{3,1},{4,6},{6,4},{5,7},{7,5},{8,10},{10,8},{9,1... | collective-permute-start | bytes 442376 | tf_op jit(solution)/shard_map/ppermute | solution.py:227
  24.4 0.2 collective-permute-start.5
  24.5 6.0 %collective-permute-done.1 = bf16[128,576]{1,0:T(8,128)(2,1)S(1)} collective-permute-done((bf16[128,576]{1,0:T(8,128)(2,1)}, bf16[128,576]{1,0:T(8,128)(2,1)S(1)}, u32[]{:S(2)}, u32[]{:S(2)}) %collective-permute-start.1) | collective-permute-done | bytes 147488 | tf_op jit(solution)/shard_map/ppermute | solution.py:227
  30.5 1.0 %add_convert_fusion.3 = bf16[128,576]{1,0:T(8,128)(2,1)S(1)} fusion(bf16[128,576]{1,0:T(8,128)(2,1)S(1)} %collective-permute-done.1, bf16[128,576]{1,0:T(8,128)(2,1)} %get-tuple-element.21), kind=kLoop, calls=%fused_computation.9 | loop fusion | flops 294912 | bytes 442368 | tf_op jit(solution)/shard_map/convert_element_type | solution.py:280
  31.5 1.6 %collective-permute-start.2 = (bf16[128,576]{1,0:T(8,128)(2,1)S(1)}, bf16[128,576]{1,0:T(8,128)(2,1)S(1)}, u32[]{:S(2)}, u32[]{:S(2)}) collective-permute-start(bf16[128,576]{1,0:T(8,128)(2,1)S(1)} %add_convert_fusion.3), channel_id=1, source_target_pairs={{0,4},{4,0},{8,12},{12,8},{16,20},{20,16},{24,28},{28,24},{1,5},{5... | collective-permute-start | bytes 442376 | tf_op jit(solution)/shard_map/ppermute | solution.py:227
  33.1 0.0 collective-permute-done.6
  33.1 1.6 %add_convert_fusion = bf16[16,2,128,128]{3,2,1,0:T(8,128)(2,1)S(1)} fusion(bf16[16,2,128,128]{3,2,1,0:T(8,128)(2,1)S(1)} %collective-permute-done.6, bf16[16,2,128,128]{3,2,1,0:T(8,128)(2,1)} %get-tuple-element.25), kind=kLoop, calls=%fused_computation | loop fusion | flops 2097152 | bytes 3145728 | tf_op jit(solution)/shard_map/convert_element_type | solution.py:271
  34.7 0.6 %collective-permute-start.7 = (bf16[16,2,128,128]{3,2,1,0:T(8,128)(2,1)S(1)}, bf16[16,2,128,128]{3,2,1,0:T(8,128)(2,1)S(1)}, u32[]{:S(2)}, u32[]{:S(2)}) collective-permute-start(bf16[16,2,128,128]{3,2,1,0:T(8,128)(2,1)S(1)} %add_convert_fusion), channel_id=1, source_target_pairs={{0,2},{2,0},{1,3},{3,1},{4,6},{6,4},{5,7},{7,5},{8,10},{10,8},{9,1... | collective-permute-start | bytes 3145736 | tf_op jit(solution)/shard_map/ppermute | solution.py:227
  35.3 2.0 %collective-permute-done.2 = bf16[128,576]{1,0:T(8,128)(2,1)S(1)} collective-permute-done((bf16[128,576]{1,0:T(8,128)(2,1)S(1)}, bf16[128,576]{1,0:T(8,128)(2,1)S(1)}, u32[]{:S(2)}, u32[]{:S(2)}) %collective-permute-start.2) | collective-permute-done | bytes 147488 | tf_op jit(solution)/shard_map/ppermute | solution.py:227
  37.4 1.6 %collective-permute-start.3 = (bf16[128,576]{1,0:T(8,128)(2,1)S(1)}, bf16[128,576]{1,0:T(8,128)(2,1)S(1)}, u32[]{:S(2)}, u32[]{:S(2)}) collective-permute-start(bf16[128,576]{1,0:T(8,128)(2,1)S(1)} %add_convert_fusion.2), channel_id=1, source_target_pairs={{0,8},{4,12},{8,0},{12,4},{16,24},{20,28},{24,16},{28,20},{1,9},{5... | collective-permute-start | bytes 442376 | tf_op jit(solution)/shard_map/ppermute | solution.py:227
  39.0 3.7 %collective-permute-done.3 = bf16[128,576]{1,0:T(8,128)(2,1)S(1)} collective-permute-done((bf16[128,576]{1,0:T(8,128)(2,1)S(1)}, bf16[128,576]{1,0:T(8,128)(2,1)S(1)}, u32[]{:S(2)}, u32[]{:S(2)}) %collective-permute-start.3) | collective-permute-done | bytes 147488 | tf_op jit(solution)/shard_map/ppermute | solution.py:227
  42.8 3.7 %collective-permute-start.4 = (bf16[128,576]{1,0:T(8,128)(2,1)S(1)}, bf16[128,576]{1,0:T(8,128)(2,1)S(1)}, u32[]{:S(2)}, u32[]{:S(2)}) collective-permute-start(bf16[128,576]{1,0:T(8,128)(2,1)S(1)} %add_convert_fusion.1), channel_id=1, source_target_pairs={{0,24},{4,28},{8,16},{12,20},{16,8},{20,12},{24,0},{28,4},{1,25},{... | collective-permute-start | bytes 442376 | tf_op jit(solution)/shard_map/ppermute | solution.py:227
  46.5 0.6 %fusion.rotary_ref = bf16[256,64]{1,0:T(8,128)(2,1)} fusion(bf16[128,576]{1,0:T(8,128)(2,1)S(1)} %get-tuple-element.34, bf16[128,576]{1,0:T(8,128)(2,1)S(1)} %get-tuple-element.35), kind=kLoop, calls=%fused_computation.12 | loop fusion | flops 65536 | bytes 327680 | tf_op jit(solution)/shard_map/concatenate | solution.py:245
  47.1 3.9 %query_gradient.1 = (f32[2048,128]{1,0:T(8,128)}, f32[2048,64]{1,0:T(8,128)}) custom-call(bf16[16,256,128]{2,1,0:T(8,128)(2,1)} %get-tuple-element.17.ds_ref, bf16[16,256,128]{2,1,0:T(8,128)(2,1)} %get-tuple-element.18.kn_ref, bf16[256,64]{1,0:T(8,128)(2,1)} %fusion.rotary_ref), custom_call_target="tpu_custom_call" | custom-call | flops 1000000000 | bytes 5000000 | tf_op jit(solution)/shard_map/query_gradient/pallas_call | solution.py:183
  51.0 2.4 %copy.16 = f32[1,128,16,64]{1,3,2,0:T(8,128)} copy(f32[1,128,16,64]{3,2,1,0:T(8,128)} %bitcast.22) | data formatting | bytes 1048576
  53.4 0.8 %convert_add_fusion = f32[128,576]{1,0:T(8,128)} fusion(bf16[128,576]{1,0:T(8,128)(2,1)S(1)} %collective-permute-done.4, bf16[128,576]{1,0:T(8,128)(2,1)S(1)} %add_convert_fusion.1), kind=kLoop, calls=%fused_computation.6 | loop fusion | flops 221184 | bytes 589824 | tf_op jit(solution)/shard_map/add | solution.py:282
  54.2 0.0 collective-permute-done.5.near_ref
  54.2 5.0 %collective-permute-done.7.far_ref = bf16[16,2,128,128]{3,2,1,0:T(8,128)(2,1)S(1)} collective-permute-done((bf16[16,2,128,128]{3,2,1,0:T(8,128)(2,1)S(1)}, bf16[16,2,128,128]{3,2,1,0:T(8,128)(2,1)S(1)}, u32[]{:S(2)}, u32[]{:S(2)}) %collective-permute-start.7) | collective-permute-done | bytes 1048608 | tf_op jit(solution)/shard_map/ppermute | solution.py:227
  59.2 1.0 %copy-done.2 = bf16[16,2,128,128]{3,2,1,0:T(8,128)(2,1)} copy-done((bf16[16,2,128,128]{3,2,1,0:T(8,128)(2,1)}, bf16[16,2,128,128]{3,2,1,0:T(8,128)(2,1)S(1)}, u32[]{:S(2)}) %copy-start.2) | copy-done | bytes 1048600
  60.1 4.0 %finish.1 = (f32[16,32,512]{2,1,0:T(8,128)}, f32[16,128,128]{2,1,0:T(8,128)}) custom-call(bf16[16,2,128,128]{3,2,1,0:T(8,128)(2,1)} %get-tuple-element.23.own_ref, bf16[16,2,128,128]{3,2,1,0:T(8,128)(2,1)} %copy-done.1, bf16[16,2,128,128]{3,2,1,0:T(8,128)(2,1)} %copy-done.2), custom_call_target="tpu_custom_call" | custom-call | tf_op jit(solution)/shard_map/finish/pallas_call | solution.py:209
  (11 shorter events, 0.1 us)
Async XLA Ops:
  0.6 5.8 %copy-start.3 = (bf16[1,128,16,128]{3,2,1,0:T(8,128)(2,1)S(1)}, bf16[1,128,16,128]{3,2,1,0:T(8,128)(2,1)}, u32[]{:S(2)}) copy-start(bf16[1,128,16,128]{3,2,1,0:T(8,128)(2,1)} %param.15) | copy-start | bytes 1572868
  0.6 8.6 %collective-permute-start = (bf16[128,576]{1,0:T(8,128)(2,1)}, bf16[128,576]{1,0:T(8,128)(2,1)S(1)}, u32[]{:S(2)}, u32[]{:S(2)}) collective-permute-start(bf16[128,576]{1,0:T(8,128)(2,1)} %bitcast.26), channel_id=1, source_target_pairs={{0,2},{2,0},{1,3},{3,1},{4,6},{6,4},{5,7},{7,5},{8,10},{10,8},{9,1... | collective-permute-start | bytes 442376 | tf_op jit(solution)/shard_map/ppermute | solution.py:227
  5.1 3.5 %copy-start = (bf16[1,128,16,128]{1,3,2,0:T(8,128)(2,1)}, bf16[1,128,16,128]{1,3,2,0:T(8,128)(2,1)S(1)}, u32[]{:S(2)}) copy-start(bf16[1,128,16,128]{1,3,2,0:T(8,128)(2,1)S(1)} %copy.13) | copy-start | bytes 1572868
  5.1 4.1 %copy-start.4 = (bf16[1,2,64,576]{3,2,1,0:T(8,128)(2,1)S(1)}, bf16[1,2,64,576]{3,2,1,0:T(8,128)(2,1)}, u32[]{:S(2)}) copy-start(bf16[1,2,64,576]{3,2,1,0:T(8,128)(2,1)} %param.11) | copy-start | bytes 442372
  23.6 9.4 %collective-permute-start.6 = (bf16[16,2,128,128]{3,2,1,0:T(8,128)(2,1)}, bf16[16,2,128,128]{3,2,1,0:T(8,128)(2,1)S(1)}, u32[]{:S(2)}, u32[]{:S(2)}) collective-permute-start(bf16[16,2,128,128]{3,2,1,0:T(8,128)(2,1)} %get-tuple-element.26), channel_id=1, source_target_pairs={{0,1},{1,0},{2,3},{3,2},{4,5},{5,4},{6,7},{7,6},{8,9},{9,8},{10,11... | collective-permute-start | bytes 3145736 | tf_op jit(solution)/shard_map/ppermute | solution.py:227
  23.7 6.8 %collective-permute-start.1 = (bf16[128,576]{1,0:T(8,128)(2,1)}, bf16[128,576]{1,0:T(8,128)(2,1)S(1)}, u32[]{:S(2)}, u32[]{:S(2)}) collective-permute-start(bf16[128,576]{1,0:T(8,128)(2,1)} %get-tuple-element.22), channel_id=1, source_target_pairs={{0,2},{2,0},{1,3},{3,1},{4,6},{6,4},{5,7},{7,5},{8,10},{10,8},{9,1... | collective-permute-start | bytes 442376 | tf_op jit(solution)/shard_map/ppermute | solution.py:227
  24.4 29.8 %collective-permute-start.5 = (bf16[16,2,128,128]{3,2,1,0:T(8,128)(2,1)}, bf16[16,2,128,128]{3,2,1,0:T(8,128)(2,1)S(1)}, u32[]{:S(2)}, u32[]{:S(2)}) collective-permute-start(bf16[16,2,128,128]{3,2,1,0:T(8,128)(2,1)} %get-tuple-element.24), channel_id=1, source_target_pairs={{0,1},{1,0},{2,3},{3,2},{4,5},{5,4},{6,7},{7,6},{8,9},{9,8},{10,11... | collective-permute-start | bytes 3145736 | tf_op jit(solution)/shard_map/ppermute | solution.py:227
  31.5 5.8 %collective-permute-start.2 = (bf16[128,576]{1,0:T(8,128)(2,1)S(1)}, bf16[128,576]{1,0:T(8,128)(2,1)S(1)}, u32[]{:S(2)}, u32[]{:S(2)}) collective-permute-start(bf16[128,576]{1,0:T(8,128)(2,1)S(1)} %add_convert_fusion.3), channel_id=1, source_target_pairs={{0,4},{4,0},{8,12},{12,8},{16,20},{20,16},{24,28},{28,24},{1,5},{5... | collective-permute-start | bytes 442376 | tf_op jit(solution)/shard_map/ppermute | solution.py:227
  34.7 24.5 %collective-permute-start.7 = (bf16[16,2,128,128]{3,2,1,0:T(8,128)(2,1)S(1)}, bf16[16,2,128,128]{3,2,1,0:T(8,128)(2,1)S(1)}, u32[]{:S(2)}, u32[]{:S(2)}) collective-permute-start(bf16[16,2,128,128]{3,2,1,0:T(8,128)(2,1)S(1)} %add_convert_fusion), channel_id=1, source_target_pairs={{0,2},{2,0},{1,3},{3,1},{4,6},{6,4},{5,7},{7,5},{8,10},{10,8},{9,1... | collective-permute-start | bytes 3145736 | tf_op jit(solution)/shard_map/ppermute | solution.py:227
  37.4 5.4 %collective-permute-start.3 = (bf16[128,576]{1,0:T(8,128)(2,1)S(1)}, bf16[128,576]{1,0:T(8,128)(2,1)S(1)}, u32[]{:S(2)}, u32[]{:S(2)}) collective-permute-start(bf16[128,576]{1,0:T(8,128)(2,1)S(1)} %add_convert_fusion.2), channel_id=1, source_target_pairs={{0,8},{4,12},{8,0},{12,4},{16,24},{20,28},{24,16},{28,20},{1,9},{5... | collective-permute-start | bytes 442376 | tf_op jit(solution)/shard_map/ppermute | solution.py:227
  42.8 10.6 %collective-permute-start.4 = (bf16[128,576]{1,0:T(8,128)(2,1)S(1)}, bf16[128,576]{1,0:T(8,128)(2,1)S(1)}, u32[]{:S(2)}, u32[]{:S(2)}) collective-permute-start(bf16[128,576]{1,0:T(8,128)(2,1)S(1)} %add_convert_fusion.1), channel_id=1, source_target_pairs={{0,24},{4,28},{8,16},{12,20},{16,8},{20,12},{24,0},{28,4},{1,25},{... | collective-permute-start | bytes 442376 | tf_op jit(solution)/shard_map/ppermute | solution.py:227
  54.2 5.0 %copy-start.1 = (bf16[16,2,128,128]{3,2,1,0:T(8,128)(2,1)}, bf16[16,2,128,128]{3,2,1,0:T(8,128)(2,1)S(1)}, u32[]{:S(2)}) copy-start(bf16[16,2,128,128]{3,2,1,0:T(8,128)(2,1)S(1)} %collective-permute-done.5.near_ref) | copy-start | bytes 3145732
  59.2 1.0 %copy-start.2 = (bf16[16,2,128,128]{3,2,1,0:T(8,128)(2,1)}, bf16[16,2,128,128]{3,2,1,0:T(8,128)(2,1)S(1)}, u32[]{:S(2)}) copy-start(bf16[16,2,128,128]{3,2,1,0:T(8,128)(2,1)S(1)} %collective-permute-done.7.far_ref) | copy-start | bytes 3145732

commit v2 on v1

v2 whole, which is shorter than its diff:
```python
import functools

import jax
import jax.numpy as jnp
from jax import lax
from jax.experimental import pallas as pl
from jax.experimental.pallas import tpu as pltpu
from jax.sharding import PartitionSpec as P

softmax_scale = 192.0 ** (-0.5)
F32 = jnp.float32
BF16 = jnp.bfloat16
MIB = 1024 * 1024
PLAN = ((4, True), (4, True), (8, False))


def dot_nn(a, b):
    return lax.dot_general(a, b, (((1,), (0,)), ((), ())), preferred_element_type=F32)


def dot_nt(a, b):
    return lax.dot_general(a, b, (((1,), (1,)), ((), ())), preferred_element_type=F32)


def dot_tn(a, b):
    return lax.dot_general(a, b, (((0,), (0,)), ((), ())), preferred_element_type=F32)


def params(mib):
    return pltpu.CompilerParams(vmem_limit_bytes=mib * MIB)


def cost(flops, moved):
    return pl.CostEstimate(flops=flops, bytes_accessed=moved, transcendentals=0)


def prepare_kernel(
    parts, page_rows, nope_hbm, rope_hbm, go_hbm, ku_hbm, vu_hbm, own_hbm, pos_hbm, table_hbm,
    qt_ref, go_ref, ku_ref, vu_ref, own_ref, bias_ref, kn_ref, va_ref,
    nope_in, go_in, rows_ref, pos_ref, table_ref, sems,
):
    heads, nope_width, latent_width = ku_ref.shape
    value_width = vu_ref.shape[2]
    query_count = go_ref.shape[1]
    moves = (
        (nope_hbm, nope_in), (go_hbm, go_in), (own_hbm, own_ref), (ku_hbm, ku_ref), (vu_hbm, vu_ref),
        (rope_hbm, qt_ref.at[:, nope_width:, :]), (table_hbm, table_ref), (pos_hbm, pos_ref),
    )
    copies = [pltpu.make_async_copy(a, b, sems.at[i]) for i, (a, b) in enumerate(moves)]
    for copy in copies:
        copy.start()
    copies[0].wait()
    rows_ref[...] = nope_in[...].astype(F32).reshape(query_count * heads, nope_width)
    for h in range(heads):
        qt_ref[h, :nope_width] = jnp.transpose(rows_ref[pl.ds(h, query_count, stride=heads), :]).astype(BF16)
    copies[1].wait()
    rows_ref[...] = go_in[...].astype(F32).reshape(query_count * heads, nope_width)
    for h in range(heads):
        go_ref[h] = rows_ref[pl.ds(h, query_count, stride=heads), :].astype(BF16)
    copies[6].wait()
    copies[7].wait()
    blocks = table_ref.shape[1]
    row = lax.broadcasted_iota(jnp.int32, (page_rows, query_count), 0)
    part_blocks = blocks // parts
    for i in range(blocks):
        slot = jnp.bitwise_xor(lax.axis_index("ctx"), i // part_blocks) * part_blocks + i % part_blocks if parts == 2 else i
        logical = jnp.int32(0)
        for b in range(blocks):
            logical = logical + jnp.where(table_ref[0, b] == slot, b, 0)
        visible = row + logical * page_rows <= pos_ref[...]
        bias_ref[i * page_rows:(i + 1) * page_rows] = jnp.where(visible, 0.0, -jnp.inf)
    copies[2].wait()
    latent = own_ref[:, :latent_width]
    copies[3].wait()
    step = 2
    for h in range(0, heads, step):
        ku = ku_ref[h:h + step].reshape(step * nope_width, latent_width)
        kn_ref[:, h * nope_width:(h + step) * nope_width] = dot_nt(latent, ku).astype(BF16)
    copies[4].wait()
    for h in range(0, heads, step):
        vu = jnp.concatenate([vu_ref[h + i] for i in range(step)], axis=1)
        va_ref[:, h * value_width:(h + step) * value_width] = dot_nn(latent, vu).astype(BF16)
    copies[5].wait()


def prepare(parts, nope, rope, go, key_up, value_up, own, pos, table, page_rows):
    query_count, heads, nope_width = nope.shape
    value_width = go.shape[2]
    key_count = table.shape[1] * page_rows
    out = lambda *dims: jax.ShapeDtypeStruct(dims, BF16)
    hbm = pl.BlockSpec(memory_space=pltpu.HBM)
    return pl.pallas_call(
        functools.partial(prepare_kernel, parts, page_rows),
        in_specs=[hbm] * 8,
        out_specs=[pl.BlockSpec(memory_space=pltpu.VMEM)] * 8,
        out_shape=[
            out(heads, nope_width + rope.shape[1], query_count), out(heads, query_count, value_width),
            out(*key_up.shape), out(*value_up.shape), out(*own.shape),
            jax.ShapeDtypeStruct((key_count, query_count), F32),
            out(own.shape[0], heads * nope_width), out(own.shape[0], heads * value_width),
        ],
        scratch_shapes=[
            pltpu.VMEM((query_count, heads, nope_width), BF16),
            pltpu.VMEM((query_count, heads, value_width), BF16),
            pltpu.VMEM((query_count * heads, nope_width), F32),
            pltpu.VMEM((1, query_count), jnp.int32),
            pltpu.SMEM((1, table.shape[1]), jnp.int32),
            pltpu.SemaphoreType.DMA((8,)),
        ],
        compiler_params=params(16),
        cost_estimate=cost(600_000_000, 12_000_000),
        name="prepare",
    )(*(pltpu.with_memory_space_constraint(x, pltpu.HBM) for x in (nope, rope, go, key_up, value_up, own, pos, table)))


def turned_values(paired, latent, vt_ref):
    slices, depth = vt_ref.shape[:2]
    turned = jnp.transpose(latent.astype(F32)).astype(BF16)
    for s in range(slices):
        vt_ref[place_of(paired, s)] = turned[s * depth:(s + 1) * depth]


def place_of(paired, s):
    if not paired:
        return s
    return jnp.bitwise_xor(s % 2, lax.axis_index("dp")) * 2 + jnp.bitwise_xor(s // 2, lax.axis_index("ctx"))


def weight_group(paired, at, qt, ds, gv, latent, vt_ref, bp_ref, outs):
    slices = vt_ref.shape[0]
    nope_slice = bp_ref.shape[1] // len(ds)
    value_width = gv.shape[1] // len(ds)
    for h in range(len(ds)):
        b = dot_nt(qt[h], ds[h]).astype(BF16)
        for s in range(slices):
            bp_ref[place_of(paired, s), h * nope_slice:(h + 1) * nope_slice] = b[s * nope_slice:(s + 1) * nope_slice]
    for s in range(slices):
        value_part = dot_nn(vt_ref[s], gv).astype(BF16)
        key_part = dot_nn(bp_ref[s], latent).astype(BF16)
        for h in range(len(ds)):
            rows = key_part[h * nope_slice:(h + 1) * nope_slice]
            columns = value_part[:, h * value_width:(h + 1) * value_width]
            if paired:
                for j in range(latent.shape[1] // value_width):
                    outs[s][at + h, 0, j * nope_slice:(j + 1) * nope_slice] = rows[:, j * value_width:(j + 1) * value_width]
                outs[s][at + h, 1] = columns
            else:
                outs[0][at + h] = rows
                outs[1][at + h] = columns


def attend_kernel(paired, first, final, weights, parts, begin, count, latent_width, qt_ref, go_ref, ku_ref, vu_ref, bias_ref, kn_own, va_own, *rest):
    rest = list(rest)
    part_refs = [rest.pop(0) for _ in range(parts)]
    before_ref = None if first else rest.pop(0)
    ds_ref, kn_ref = rest.pop(0), rest.pop(0)
    gv_ref = None if weights else rest.pop(0)
    outs = [rest.pop(0) for _ in range(4 if paired else 2)] if weights else None
    total_refs = [rest.pop(0) for _ in range(parts if final else 1)]
    nope_width = ku_ref.shape[1]
    value_width = vu_ref.shape[2]
    latent = jnp.concatenate([r[:, :latent_width] for r in part_refs], axis=0)
    rotary = jnp.concatenate([r[:, latent_width:] for r in part_refs], axis=0)
    if weights:
        vt_ref, bp_ref = rest
        turned_values(paired, latent, vt_ref)
        group = bp_ref.shape[1] * bp_ref.shape[0] // nope_width
    else:
        group = min(4, count)
    if not first:
        total = before_ref[...]
        total_latent, total_rotary = total[:, :latent_width], total[:, latent_width:]
    for g in range(0, count, group):
        at = begin + g
        heads = range(at, at + group)
        ku = ku_ref[at:at + group].reshape(group * nope_width, latent_width)
        vu = jnp.concatenate([vu_ref[h] for h in heads], axis=1)
        kn, values = kn_own[:, at * nope_width:(at + group) * nope_width], va_own[:, at * value_width:(at + group) * value_width]
        if parts == 2:
            far = latent[latent.shape[0] // 2:]
            kn = jnp.concatenate([kn, dot_nt(far, ku).astype(BF16)], axis=0)
            values = jnp.concatenate([values, dot_nn(far, vu).astype(BF16)], axis=0)
        raw = []
        for i, h in enumerate(heads):
            kn_h = kn[:, i * nope_width:(i + 1) * nope_width]
            kn_ref[g + i] = kn_h
            raw.append((
                dot_nn(jnp.concatenate([kn_h, rotary], axis=1), qt_ref[h]),
                dot_nt(values[:, i * value_width:(i + 1) * value_width], go_ref[h]),
            ))
        soft = []
        for scores, grad_probs in raw:
            scores = scores * softmax_scale + bias_ref[...]
            top = jnp.max(scores, axis=0, keepdims=True)
            weight = jnp.exp(scores - top)
            inverse = 1.0 / jnp.sum(weight, axis=0, keepdims=True)
            delta = jnp.sum(weight * grad_probs, axis=0, keepdims=True) * inverse
            probs = weight * inverse
            soft.append((probs.astype(BF16), (probs * ((grad_probs - delta) * softmax_scale)).astype(BF16)))
        gkn, gv = [], []
        rotary_sum = None
        for i, h in enumerate(heads):
            probs, ds = soft[i]
            ds_ref[g + i] = ds
            gk = dot_nt(ds, qt_ref[h])
            gkn.append(gk[:, :nope_width].astype(BF16))
            rotary_sum = gk[:, nope_width:] if rotary_sum is None else rotary_sum + gk[:, nope_width:]
            gv.append(dot_nn(probs, go_ref[h]).astype(BF16))
        gv = jnp.concatenate(gv, axis=1)
        latent_sum = dot_nn(jnp.concatenate(gkn, axis=1), ku) + dot_nt(gv, vu)
        if first and g == 0:
            total_latent, total_rotary = latent_sum, rotary_sum
        else:
            total_latent, total_rotary = total_latent + latent_sum, total_rotary + rotary_sum
        if weights:
            weight_group(paired, g, [qt_ref[h, :nope_width] for h in heads], [d for _, d in soft], gv, latent, vt_ref, bp_ref, outs)
        else:
            gv_ref[:, g * value_width:(g + group) * value_width] = gv
    start = 0
    for ref in total_refs:
        stop = start + ref.shape[0]
        ref[:, :latent_width] = total_latent[start:stop].astype(ref.dtype)
        ref[:, latent_width:] = total_rotary[start:stop].astype(ref.dtype)
        start = stop


def partial_shapes(paired, count, nope_width, latent_width, value_width):
    if paired:
        return [jax.ShapeDtypeStruct((count, 2, latent_width // 4, value_width), BF16)] * 4
    return [
        jax.ShapeDtypeStruct((count, nope_width, latent_width), BF16),
        jax.ShapeDtypeStruct((count, latent_width, value_width), BF16),
    ]


def partial_scratch(paired, group, key_count, nope_width, latent_width):
    slices = 4 if paired else 1
    return [
        pltpu.VMEM((slices, latent_width // slices, key_count), BF16),
        pltpu.VMEM((slices, group * nope_width // slices, key_count), BF16),
    ]


def attend(paired, begin, count, weights, final, qt, go, key_up, value_up, bias, kn_own, va_own, parts, before):
    _, nope_width, latent_width = key_up.shape
    value_width = value_up.shape[2]
    key_count, query_count = bias.shape
    row_width = parts[0].shape[1]
    out = lambda *dims: jax.ShapeDtypeStruct(dims, BF16)
    shapes = [out(count, key_count, query_count), out(count, key_count, nope_width)]
    if weights:
        shapes += partial_shapes(paired, count, nope_width, latent_width, value_width)
    else:
        shapes += [out(key_count, count * value_width)]
    shapes += [out(*p.shape) for p in parts] if final else [jax.ShapeDtypeStruct((key_count, row_width), F32)]
    group = min(4, count) if paired else 1
    return pl.pallas_call(
        functools.partial(attend_kernel, paired, before is None, final, weights, len(parts), begin, count, latent_width),
        out_shape=shapes,
        scratch_shapes=partial_scratch(paired, group, key_count, nope_width, latent_width) if weights else [],
        compiler_params=params(14 if paired else 56),
        cost_estimate=cost(count * (400_000_000 if weights else 300_000_000), count * 500_000),
        name="attend",
    )(qt, go, key_up, value_up, bias, kn_own, va_own, *parts, *([] if before is None else [before]))


def weights_kernel(paired, parts, begin, latent_width, qt_ref, ds_ref, gv_ref, *rest):
    part_refs, outs, vt_ref, bp_ref = rest[:parts], rest[parts:-2], rest[-2], rest[-1]
    latent = jnp.concatenate([r[:, :latent_width] for r in part_refs], axis=0)
    turned_values(paired, latent, vt_ref)
    count = ds_ref.shape[0]
    value_width = gv_ref.shape[1] // count
    nope_width = bp_ref.shape[1] if not paired else gv_ref.shape[1] // count
    group = min(4, count)
    for g in range(0, count, group):
        weight_group(
            paired, g, [qt_ref[begin + g + i, :nope_width] for i in range(group)], [ds_ref[g + i] for i in range(group)],
            gv_ref[:, g * value_width:(g + group) * value_width], latent, vt_ref, bp_ref, outs,
        )


def weight_partials(paired, begin, qt, ds, gv, parts, nope_width, latent_width):
    count, key_count, _ = ds.shape
    return pl.pallas_call(
        functools.partial(weights_kernel, paired, len(parts), begin, latent_width),
        out_shape=partial_shapes(paired, count, nope_width, latent_width, gv.shape[1] // count),
        scratch_shapes=partial_scratch(paired, min(4, count), key_count, nope_width, latent_width),
        compiler_params=params(14),
        cost_estimate=cost(count * 100_000_000, count * 400_000),
        name="weight_partials",
    )(qt, ds, gv, *parts)


def query_kernel(counts, parts, *refs):
    rotary_refs, refs = refs[:parts], refs[parts:]
    nope_ref, rope_ref = refs[-2:]
    rotary = jnp.concatenate([r[...] for r in rotary_refs], axis=0)
    nope_width = nope_ref.shape[1]
    rotary = rotary[:, rotary.shape[1] - rope_ref.shape[1]:]
    heads = sum(counts)
    query_count = rope_ref.shape[2]
    head = 0
    for c, count in enumerate(counts):
        ds_ref, kn_ref = refs[2 * c], refs[2 * c + 1]
        for h in range(count):
            ds = ds_ref[h]
            nope_ref[pl.ds(head, query_count, stride=heads), :] = dot_tn(ds, kn_ref[h])
            rope_ref[head] = dot_tn(rotary, ds)
            head += 1


def query_gradient(pairs, parts, rope_width):
    counts = [ds.shape[0] for ds, _ in pairs]
    heads = sum(counts)
    query_count, nope_width = pairs[0][0].shape[2], pairs[0][1].shape[2]
    nope, rope = pl.pallas_call(
        functools.partial(query_kernel, counts, len(parts)),
        out_shape=[
            jax.ShapeDtypeStruct((query_count * heads, nope_width), F32),
            jax.ShapeDtypeStruct((heads, rope_width, query_count), F32),
        ],
        compiler_params=params(8),
        cost_estimate=pl.CostEstimate(flops=1_000_000_000, bytes_accessed=5_000_000, transcendentals=0),
        name="query_gradient",
    )(*parts, *[x for pair in pairs for x in pair])
    return nope.reshape(1, query_count, heads, nope_width), jnp.transpose(rope, (2, 0, 1))[None]


def finish_kernel(own_ref, near_ref, far_ref, *rest):
    key_ref, value_ref = rest[-2:]
    rows = key_ref.shape[1]
    width = own_ref.shape[3]
    for h in range(key_ref.shape[0]):
        total = own_ref[h].astype(F32) + near_ref[h].astype(F32) + far_ref[h].astype(F32)
        for j in range(key_ref.shape[2] // width):
            key_ref[h, :, j * width:(j + 1) * width] = total[0, j * rows:(j + 1) * rows]
        value_ref[h] = total[1]


def finish(own, near, far, heads, begin, before, group):
    count, _, depth, width = own.shape
    rows = depth // 4
    offset = begin // group
    return pl.pallas_call(
        finish_kernel,
        grid=(count // group,),
        in_specs=[pl.BlockSpec((group, 2, depth, width), lambda i: (i, 0, 0, 0))] * 3
        + [pl.BlockSpec(memory_space=pl.ANY)] * len(before),
        out_specs=[
            pl.BlockSpec((group, rows, 4 * width), lambda i: (i + offset, 0, 0)),
            pl.BlockSpec((group, depth, width), lambda i: (i + offset, 0, 0)),
        ],
        out_shape=[
            jax.ShapeDtypeStruct((heads, rows, 4 * width), F32),
            jax.ShapeDtypeStruct((heads, depth, width), F32),
        ],
        input_output_aliases={3: 0, 4: 1} if before else {},
        compiler_params=params(8),
        cost_estimate=pl.CostEstimate(flops=1_000_000, bytes_accessed=300_000 * count, transcendentals=0),
        name="finish",
    )(own, near, far, *before)


def swap(x, axis, size, bits):
    return lax.ppermute(x, axis, [(i, i ^ bits) for i in range(size)])


def on_device(
    sizes, query_nope, query_rope, query_pos, latent_cache, block_table, key_up, value_up, grad_out
):
    head_size, ctx_size, dp_size = sizes
    heads, nope_width, latent_width = key_up.shape
    value_width = value_up.shape[2]
    page_rows, row_width = latent_cache.shape[2:]
    paired = (
        ctx_size == 2 and dp_size == 2 and latent_width == 4 * value_width and nope_width == value_width
        and nope_width % 64 == 0 and value_width % 128 == 0 and heads % 16 == 0
    )
    own_rows = latent_cache[0].reshape(-1, row_width)
    if ctx_size == 2:
        parts = [own_rows, swap(own_rows, "ctx", 2, 1)]
    else:
        parts = [lax.all_gather(own_rows, "ctx", axis=0, tiled=True)]
    rope = jnp.transpose(query_rope[0], (1, 2, 0))
    if paired:
        qt, go, ku, vu, own, bias, kn_own, va_own = prepare(
            2, query_nope[0], rope, grad_out[0], key_up, value_up, own_rows, query_pos, block_table, page_rows
        )
        parts[0] = own
        plan = [(heads * n // 16, weights) for n, weights in PLAN]
    else:
        qt = jnp.concatenate([jnp.transpose(query_nope[0], (1, 2, 0)), rope], axis=1)
        go, ku, vu = jnp.swapaxes(grad_out[0], 0, 1), key_up, value_up
        if ctx_size == 2:
            first = lax.axis_index("ctx") == 0
            parts = [jnp.concatenate([jnp.where(first, parts[0], parts[1]), jnp.where(first, parts[1], parts[0])], axis=0)]
        slots = jnp.arange(block_table.shape[1], dtype=jnp.int32)
        logical = jnp.sum(jnp.where(block_table[0][None, :] == slots[:, None], slots[None, :], 0), axis=1)
        positions = (logical[:, None] * page_rows + jnp.arange(page_rows, dtype=jnp.int32)[None, :]).reshape(-1, 1)
        bias = jnp.where(positions <= query_pos, 0.0, -jnp.inf).astype(F32)
        latent = parts[0][:, :latent_width]
        kn_own = jnp.einsum("kl,hnl->khn", latent, key_up, preferred_element_type=F32).astype(BF16).reshape(latent.shape[0], -1)
        va_own = jnp.einsum("kl,hlv->khv", latent, value_up, preferred_element_type=F32).astype(BF16).reshape(latent.shape[0], -1)
        plan = [(1, True)] * heads
    pairs, pieces, partials, total = [], [], [], None
    begin = 0
    for n, (count, weights) in enumerate(plan):
        final = n == len(plan) - 1
        results = list(attend(
            paired, begin, count, weights, final, qt, go, ku, vu, bias, kn_own, va_own, parts, total,
        ))
        pairs.append((results[0], results[1]))
        ends = results[-len(parts):] if final else results[-1:]
        if weights:
            made = results[2:len(results) - len(ends)]
        else:
            made = weight_partials(paired, begin, qt, results[0], results[2], parts, nope_width, latent_width)
        partials.append((begin, made))
        total = ends[0]
        begin += count
    if paired:
        for begin, (keep0, keep1, send0, send1) in partials:
            near1 = swap(send1, "dp", 2, 1)
            near0 = swap(send0, "dp", 2, 1)
            far = swap((keep1.astype(F32) + near1.astype(F32)).astype(BF16), "ctx", 2, 1)
            pieces.append((begin, (keep0, near0, far)))
        grad_nope, grad_rope = query_gradient(pairs, parts, query_rope.shape[3])
        mine, other = ends
        share = mine.astype(F32) + swap(other, "ctx", 2, 1).astype(F32)
    else:
        ds, kn = (jnp.concatenate(x, axis=0) for x in zip(*pairs))
        wk, wv = (jnp.concatenate(x, axis=0) for x in zip(*(made for _, made in partials)))
        grad_nope = jnp.einsum("hkq,hkn->qhn", ds, kn, preferred_element_type=F32)[None]
        rotary = parts[0][:, latent_width:]
        grad_rope = jnp.einsum("hkq,kr->qhr", ds, rotary, preferred_element_type=F32)[None]
        grad_key_map = lax.psum_scatter(wk, ("ctx", "dp"), scatter_dimension=1, tiled=True).astype(F32)
        grad_value_map = lax.psum_scatter(wv, ("ctx", "dp"), scatter_dimension=1, tiled=True).astype(F32)
        share = lax.psum_scatter(ends[0], "ctx", scatter_dimension=0, tiled=True).astype(F32)
    if head_size & (head_size - 1) == 0:
        bits = 1
        while bits < head_size:
            rounded = share.astype(BF16)
            got = swap(rounded, "head", head_size, bits | (bits >> 1) if bits >= 4 else bits)
            share = rounded.astype(F32) + got.astype(F32)
            bits *= 2
    else:
        share = lax.psum(share.astype(BF16), "head").astype(F32)
    if paired:
        maps = ()
        for begin, piece in pieces:
            maps = finish(*piece, heads, begin, maps, min(4, piece[0].shape[0]))
        grad_key_map, grad_value_map = maps
    return (
        grad_nope,
        grad_rope,
        share.reshape(latent_cache.shape),
        grad_key_map,
        grad_value_map,
    )


def solution(mesh):
    sizes = tuple(mesh.shape[axis] for axis in ("head", "ctx", "dp"))
    placed = (
        P("dp", "ctx", "head", None),
        P("dp", "ctx", "head", None),
        P("dp", "ctx"),
        P("dp", "ctx", None, None),
        P("dp", None),
        P("head", None, None),
        P("head", None, None),
        P("dp", "ctx", "head", None),
    )
    return jax.shard_map(
        functools.partial(on_device, sizes),
        mesh=mesh,
        in_specs=placed,
        out_specs=(
            P("dp", "ctx", "head", None),
            P("dp", "ctx", "head", None),
            P("dp", "ctx", None, None),
            P("head", ("ctx", "dp"), None),
            P("head", ("ctx", "dp"), None),
        ),
        check_vma=False,
    )
```

time: 64.6 us -> 52.8 us (0.82)
  local copies, waits for them, and re-layouts: 7.08 us -> 0 us
  Pallas kernels: 21.4 us -> 15.4 us
  other arithmetic: 6.66 us -> 1.17 us
  starting transfers between devices: 11.4 us -> 16.1 us
  waiting for transfers between devices: 16.8 us -> 19.2 us
    pallas_call x3 -> x9, Pallas kernels: 21.4 us -> 15.4 us  [the longest x3 5.86 us: attend(): pl.pallas_call(functools.partial(attend_kernel, paired, before is None, f...]
    unnamed x13 -> x0, local copies, waits for them, and re-layouts: 5.79 us -> none
    ppermute x8 -> x14, starting transfers between devices: 11.4 us -> 16.1 us  [swap(): return lax.ppermute(x, axis, [(i, i ^ bits) for i in range(size)])]
    ppermute x8 -> x14, waiting for transfers between devices: 16.8 us -> 19.2 us  [swap(): return lax.ppermute(x, axis, [(i, i ^ bits) for i in range(size)])]
    concatenate x2 -> x0, other arithmetic: 1.4 us -> none  [on_device(): jnp.concatenate([jnp.where(first, own_rows, other_rows), jnp.where(first,...]
    convert_element_type x1 -> x3, other arithmetic: 1.59 us -> 0.29 us  [on_device(): (keep1.astype(F32) + near1.astype(F32)).astype(BF16)]
    transpose x1 -> x0, local copies, waits for them, and re-layouts: 1.29 us -> none  [on_device(): jnp.swapaxes(jnp.concatenate([query_nope[0], query_rope[0]], axis=2), 0, 1)]
    transpose x1 -> x0, other arithmetic: 1.23 us -> none  [on_device(): jnp.swapaxes(jnp.concatenate([query_nope[0], query_rope[0]], axis=2), 0, 1)]
  transfers between devices with their start and end apart: 8 -> 14, of which waited for: 4 -> 7; matrix products, arithmetic and copies ran while one was open for 19% -> 2% of each run, Pallas kernels for 6% -> 16%
where the time goes in v2:
time: 52.8 us; the launch traced here: 52.6 us
  waiting for transfers between devices  19.2 us (36%)
  starting transfers between devices  16.1 us (30%)
  Pallas kernels  15.4 us (29%)
  other arithmetic  1.17 us (2%)
  between operations  0.73 us (1%)
    ppermute x14, waiting for transfers between devices, swap(): return lax.ppermute(x, axis, [(i, i ^ bits) for i in range(size)])  19.2 us
    ppermute x14, starting transfers between devices, swap(): return lax.ppermute(x, axis, [(i, i ^ bits) for i in range(size)])  16.1 us
    pallas_call x3, Pallas kernels, attend(): pl.pallas_call(functools.partial(attend_kernel, paired, before is None, f...  5.86 us
    pallas_call x1, Pallas kernels, prepare(): pl.pallas_call(functools.partial(prepare_kernel, parts, page_rows), in_sp...  3.71 us
    pallas_call x3, Pallas kernels, finish(): pl.pallas_call(finish_kernel, grid=(count // group,), in_specs=[pl.BlockS...  2.77 us
    pallas_call x1, Pallas kernels, query_gradient(): pl.pallas_call(functools.partial(query_kernel, counts, len(parts)), out_s...  1.92 us
    pallas_call x1, Pallas kernels, weight_partials(): pl.pallas_call(functools.partial(weights_kernel, paired, len(parts), begi...  1.11 us
  transfers between devices with their start and end apart: 14, of which 7 were waited for; matrix products, arithmetic and copies ran while one was open for 2% of the time, Pallas kernels for 16%

profile of v2, /device:TPU:0, one launch (start us, length us, event | category | flops | bytes accessed | tf_op | source)
XLA Modules:
  0.0 52.6 jit_solution(567023999397720415)
XLA Ops:
  0.6 3.0 %collective-permute-start = (bf16[128,576]{1,0:T(8,128)(2,1)}, bf16[128,576]{1,0:T(8,128)(2,1)S(1)}, u32[]{:S(2)}, u32[]{:S(2)}) collective-permute-start(bf16[128,576]{1,0:T(8,128)(2,1)} %bitcast.15), channel_id=1, source_target_pairs={{0,2},{2,0},{1,3},{3,1},{4,6},{6,4},{5,7},{7,5},{8,10},{10,8},{9,1... | collective-permute-start | bytes 442376 | tf_op jit(solution)/shard_map/ppermute | solution.py:365
  3.7 3.7 %prepare.1 = (bf16[16,192,128]{2,1,0:T(8,128)(2,1)S(1)}, bf16[16,128,128]{2,1,0:T(8,128)(2,1)S(1)}, bf16[16,128,512]{2,1,0:T(8,128)(2,1)S(1)}, bf16[16,512,128]{...) custom-call(bf16[128,16,128]{2,1,0:T(8,128)(2,1)} %bitcast.11, ...), custom_call_target="tpu_custom_call" | custom-call | flops 600000000 | bytes 12000000 | tf_op jit(solution)/shard_map/prepare/pallas_call | solution.py:92
  7.4 0.7 %collective-permute-done.rest_1_.refs_1_ = bf16[128,576]{1,0:T(8,128)(2,1)S(1)} collective-permute-done((bf16[128,576]{1,0:T(8,128)(2,1)}, bf16[128,576]{1,0:T(8,128)(2,1)S(1)}, u32[]{:S(2)}, u32[]{:S(2)}) %collective-permute-start) | collective-permute-done | bytes 147488 | tf_op jit(solution)/shard_map/ppermute | solution.py:365
  8.1 1.7 %attend.3 = (bf16[4,256,128]{2,1,0:T(8,128)(2,1)S(1)}, bf16[4,256,128]{2,1,0:T(8,128)(2,1)S(1)}, bf16[4,2,128,128]{3,2,1,0:T(8,128)(2,1)S(1)}, bf16[4,2,128,128]...) custom-call(bf16[16,192,128]{2,1,0:T(8,128)(2,1)S(1)} %get-tuple-ele, ...), custom_call_target="tpu_custom_call" | custom-call | flops 1600000000 | bytes 2000000 | tf_op jit(solution)/shard_map/attend/pallas_call | solution.py:257
  9.8 1.7 %attend.4 = (bf16[4,256,128]{2,1,0:T(8,128)(2,1)S(1)}, bf16[4,256,128]{2,1,0:T(8,128)(2,1)S(1)}, bf16[4,2,128,128]{3,2,1,0:T(8,128)(2,1)S(1)}, bf16[4,2,128,128]...) custom-call(bf16[16,192,128]{2,1,0:T(8,128)(2,1)S(1)} %get-tuple-ele, ...), custom_call_target="tpu_custom_call" | custom-call | flops 1600000000 | bytes 2000000 | tf_op jit(solution)/shard_map/attend/pallas_call | solution.py:257
  11.6 2.4 %attend.5 = (bf16[8,256,128]{2,1,0:T(8,128)(2,1)S(1)}, bf16[8,256,128]{2,1,0:T(8,128)(2,1)S(1)}, bf16[256,1024]{1,0:T(8,128)(2,1)S(1)}, bf16[128,576]{1,0:T(8,128)(2,1)S(1)}, bf16[128,576]{1,0:T(8,128)(2,1)S(1)}) custom-call(bf16[16,192,128]{2,1,0:T(8,128)(2,1)S(1)} %get-tuple-element.45.qt_ref, bf16[16,128,128]{2,1,0:T(8,128)(2,1)S(1)} %get-tuple-element.46.go_ref, ...), custom_call_target="tpu_custom_call" | custom-call | flops 2400000000 | bytes 4000000 | tf_op jit(solution)/shard_map/attend/pallas_call | solution.py:257
  14.0 1.8 %collective-permute-start.1 = (bf16[128,576]{1,0:T(8,128)(2,1)S(1)}, bf16[128,576]{1,0:T(8,128)(2,1)S(1)}, u32[]{:S(2)}, u32[]{:S(2)}) collective-permute-start(bf16[128,576]{1,0:T(8,128)(2,1)S(1)} %get-tuple-element.63), channel_id=1, source_target_pairs={{0,2},{2,0},{1,3},{3,1},{4,6},{6,4},{5,7},{7,5},{8,10},{10,8},{9,1... | collective-permute-start | bytes 442376 | tf_op jit(solution)/shard_map/ppermute | solution.py:365
  15.8 1.1 %weight_partials.1 = (bf16[8,2,128,128]{3,2,1,0:T(8,128)(2,1)S(1)}, bf16[8,2,128,128]{3,2,1,0:T(8,128)(2,1)S(1)}, bf16[8,2,128,128]{3,2,1,0:T(8,128)(2,1)S(1)}, bf16[8,2,128,128]{3,2,1,0:T(8,128)(2,1)S(1)}) custom-call(bf16[16,192,128]{2,1,0:T(8,128)(2,1)S(1)} %get-tuple-element.45.qt_ref, bf16[8,256,128]{2,1,0:T(8,128)(2,1)S(1)} %get-tuple-element.58.refs_6_.ds_ref, ...), custom_call_target="tpu_custom_call" | custom-call | flops 800000000 | bytes 3200000 | tf_op jit(solution)/shard_map/weight_partials/pallas_call | solution.py:284
  16.9 0.6 %collective-permute-start.5 = (bf16[8,2,128,128]{3,2,1,0:T(8,128)(2,1)S(1)}, bf16[8,2,128,128]{3,2,1,0:T(8,128)(2,1)S(1)}, u32[]{:S(2)}, u32[]{:S(2)}) collective-permute-start(bf16[8,2,128,128]{3,2,1,0:T(8,128)(2,1)S(1)} %get-tuple-element.66), channel_id=1, source_target_pairs={{0,1},{1,0},{2,3},{3,2},{4,5},{5,4},{6,7},{7,6},{8,9},{9,8},{10,11... | collective-permute-start | bytes 1572872 | tf_op jit(solution)/shard_map/ppermute | solution.py:365
  17.4 0.1 collective-permute-start.6
  17.5 0.4 collective-permute-start.8
  17.9 1.5 %collective-permute-done.1 = bf16[128,576]{1,0:T(8,128)(2,1)S(1)} collective-permute-done((bf16[128,576]{1,0:T(8,128)(2,1)S(1)}, bf16[128,576]{1,0:T(8,128)(2,1)S(1)}, u32[]{:S(2)}, u32[]{:S(2)}) %collective-permute-start.1) | collective-permute-done | bytes 147488 | tf_op jit(solution)/shard_map/ppermute | solution.py:365
  19.5 0.6 %collective-permute-start.11 = (bf16[4,2,128,128]{3,2,1,0:T(8,128)(2,1)S(1)}, bf16[4,2,128,128]{3,2,1,0:T(8,128)(2,1)S(1)}, u32[]{:S(2)}, u32[]{:S(2)}) collective-permute-start(bf16[4,2,128,128]{3,2,1,0:T(8,128)(2,1)S(1)} %get-tuple-element.74), channel_id=1, source_target_pairs={{0,1},{1,0},{2,3},{3,2},{4,5},{5,4},{6,7},{7,6},{8,9},{9,8},{10,11... | collective-permute-start | bytes 786440 | tf_op jit(solution)/shard_map/ppermute | solution.py:365
  20.0 0.1 add_convert_fusion.2
  20.1 0.8 %collective-permute-done.12 = bf16[4,2,128,128]{3,2,1,0:T(8,128)(2,1)S(1)} collective-permute-done((bf16[4,2,128,128]{3,2,1,0:T(8,128)(2,1)S(1)}, bf16[4,2,128,128]{3,2,1,0:T(8,128)(2,1)S(1)}, u32[]{:S(2)}, u32[]{:S(2)}) %collective-permute-start.12) | collective-permute-done | bytes 262176 | tf_op jit(solution)/shard_map/ppermute | solution.py:365
  20.9 1.6 %collective-permute-start.2 = (bf16[128,576]{1,0:T(8,128)(2,1)S(1)}, bf16[128,576]{1,0:T(8,128)(2,1)S(1)}, u32[]{:S(2)}, u32[]{:S(2)}) collective-permute-start(bf16[128,576]{1,0:T(8,128)(2,1)S(1)} %add_convert_fusion.5), channel_id=1, source_target_pairs={{0,4},{4,0},{8,12},{12,8},{16,20},{20,16},{24,28},{28,24},{1,5},{5... | collective-permute-start | bytes 442376 | tf_op jit(solution)/shard_map/ppermute | solution.py:365
  22.6 0.1 add_convert_fusion.1
  22.7 4.5 %collective-permute-done.2 = bf16[128,576]{1,0:T(8,128)(2,1)S(1)} collective-permute-done((bf16[128,576]{1,0:T(8,128)(2,1)S(1)}, bf16[128,576]{1,0:T(8,128)(2,1)S(1)}, u32[]{:S(2)}, u32[]{:S(2)}) %collective-permute-start.2) | collective-permute-done | bytes 147488 | tf_op jit(solution)/shard_map/ppermute | solution.py:365
  27.2 1.7 %collective-permute-start.13 = (bf16[4,2,128,128]{3,2,1,0:T(8,128)(2,1)S(1)}, bf16[4,2,128,128]{3,2,1,0:T(8,128)(2,1)S(1)}, u32[]{:S(2)}, u32[]{:S(2)}) collective-permute-start(bf16[4,2,128,128]{3,2,1,0:T(8,128)(2,1)S(1)} %add_convert_fusion.1), channel_id=1, source_target_pairs={{0,2},{2,0},{1,3},{3,1},{4,6},{6,4},{5,7},{7,5},{8,10},{10,8},{9,1... | collective-permute-start | bytes 786440 | tf_op jit(solution)/shard_map/ppermute | solution.py:365
  28.9 1.6 %collective-permute-start.3 = (bf16[128,576]{1,0:T(8,128)(2,1)S(1)}, bf16[128,576]{1,0:T(8,128)(2,1)S(1)}, u32[]{:S(2)}, u32[]{:S(2)}) collective-permute-start(bf16[128,576]{1,0:T(8,128)(2,1)S(1)} %add_convert_fusion.4), channel_id=1, source_target_pairs={{0,8},{4,12},{8,0},{12,4},{16,24},{20,28},{24,16},{28,20},{1,9},{5... | collective-permute-start | bytes 442376 | tf_op jit(solution)/shard_map/ppermute | solution.py:365
  30.5 0.1 add_convert_fusion
  30.7 0.6 %collective-permute-start.10 = (bf16[4,2,128,128]{3,2,1,0:T(8,128)(2,1)S(1)}, bf16[4,2,128,128]{3,2,1,0:T(8,128)(2,1)S(1)}, u32[]{:S(2)}, u32[]{:S(2)}) collective-permute-start(bf16[4,2,128,128]{3,2,1,0:T(8,128)(2,1)S(1)} %add_convert_fusion.2), channel_id=1, source_target_pairs={{0,2},{2,0},{1,3},{3,1},{4,6},{6,4},{5,7},{7,5},{8,10},{10,8},{9,1... | collective-permute-start | bytes 786440 | tf_op jit(solution)/shard_map/ppermute | solution.py:365
  31.3 3.0 %collective-permute-done.3 = bf16[128,576]{1,0:T(8,128)(2,1)S(1)} collective-permute-done((bf16[128,576]{1,0:T(8,128)(2,1)S(1)}, bf16[128,576]{1,0:T(8,128)(2,1)S(1)}, u32[]{:S(2)}, u32[]{:S(2)}) %collective-permute-start.3) | collective-permute-done | bytes 147488 | tf_op jit(solution)/shard_map/ppermute | solution.py:365
  34.3 0.4 collective-permute-start.7
  34.7 1.7 %collective-permute-done.13.far_ref = bf16[4,2,128,128]{3,2,1,0:T(8,128)(2,1)S(1)} collective-permute-done((bf16[4,2,128,128]{3,2,1,0:T(8,128)(2,1)S(1)}, bf16[4,2,128,128]{3,2,1,0:T(8,128)(2,1)S(1)}, u32[]{:S(2)}, u32[]{:S(2)}) %collective-permute-start.13) | collective-permute-done | bytes 262176 | tf_op jit(solution)/shard_map/ppermute | solution.py:365
  36.4 3.7 %collective-permute-start.4 = (bf16[128,576]{1,0:T(8,128)(2,1)S(1)}, bf16[128,576]{1,0:T(8,128)(2,1)S(1)}, u32[]{:S(2)}, u32[]{:S(2)}) collective-permute-start(bf16[128,576]{1,0:T(8,128)(2,1)S(1)} %add_convert_fusion.3), channel_id=1, source_target_pairs={{0,24},{4,28},{8,16},{12,20},{16,8},{20,12},{24,0},{28,4},{1,25},{... | collective-permute-start | bytes 442376 | tf_op jit(solution)/shard_map/ppermute | solution.py:365
  40.2 1.9 %query_gradient.1 = (f32[2048,128]{1,0:T(8,128)}, f32[16,64,128]{2,1,0:T(8,128)}) custom-call(bf16[128,576]{1,0:T(8,128)(2,1)S(1)} %get-tuple-element.44.rest_0_.refs_0_, bf16[128,576]{1,0:T(8,128)(2,1)S(1)} %collective-permute-done.rest_1_.refs_1_, bf16[4,256,128]{2,1,0:T(8,128)(2,1)S(1)} %get-tuple-element.52.refs_2_, ...), custom_call_target="tpu_custom_call" | custom-call | flops 1000000000 | bytes 5000000 | tf_op jit(solution)/shard_map/query_gradient/pallas_call | solution.py:316
  42.1 0.9 %finish.3 = (f32[16,32,512]{2,1,0:T(8,128)}, f32[16,128,128]{2,1,0:T(8,128)}) custom-call(bf16[4,2,128,128]{3,2,1,0:T(8,128)(2,1)S(1)} %get-tuple-element.73.own_ref, bf16[4,2,128,128]{3,2,1,0:T(8,128)(2,1)S(1)} %collective-permute-done.11.near_ref, bf16[4,2,128,128]{3,2,1,0:T(8,128)(2,1)S(1)} %collective-permute-done.13.far_ref), custom_call_target="tpu_custom_call" | custom-call | flops 1000000 | bytes 1200000 | tf_op jit(solution)/shard_map/finish/pallas_call | solution.py:344
  43.0 0.9 %finish.4 = (f32[16,32,512]{2,1,0:T(8,128)}, f32[16,128,128]{2,1,0:T(8,128)}) custom-call(bf16[4,2,128,128]{3,2,1,0:T(8,128)(2,1)S(1)} %get-tuple-element.69.own_ref, bf16[4,2,128,128]{3,2,1,0:T(8,128)(2,1)S(1)} %collective-permute-done.8.near_ref, ...), custom_call_target="tpu_custom_call", output_to_operand_aliasing={{0}: (3, {}), {1}: (4, {})} | custom-call | flops 1000000 | bytes 1200000 | tf_op jit(solution)/shard_map/finish/pallas_call | solution.py:344
  43.8 0.8 %convert_add_fusion = f32[128,576]{1,0:T(8,128)} fusion(bf16[128,576]{1,0:T(8,128)(2,1)S(1)} %collective-permute-done.4, bf16[128,576]{1,0:T(8,128)(2,1)S(1)} %add_convert_fusion.3), kind=kLoop, calls=%fused_computation.3 | loop fusion | flops 221184 | bytes 589824 | tf_op jit(solution)/shard_map/add | solution.py:444
  44.6 7.0 %collective-permute-done.7.far_ref = bf16[8,2,128,128]{3,2,1,0:T(8,128)(2,1)S(1)} collective-permute-done((bf16[8,2,128,128]{3,2,1,0:T(8,128)(2,1)S(1)}, bf16[8,2,128,128]{3,2,1,0:T(8,128)(2,1)S(1)}, u32[]{:S(2)}, u32[]{:S(2)}) %collective-permute-start.7) | collective-permute-done | bytes 524320 | tf_op jit(solution)/shard_map/ppermute | solution.py:365
  51.6 1.0 %finish.5 = (f32[16,32,512]{2,1,0:T(8,128)}, f32[16,128,128]{2,1,0:T(8,128)}) custom-call(bf16[8,2,128,128]{3,2,1,0:T(8,128)(2,1)S(1)} %get-tuple-element.65.own_ref, bf16[8,2,128,128]{3,2,1,0:T(8,128)(2,1)S(1)} %collective-permute-done.5.near_ref, ...), custom_call_target="tpu_custom_call", output_to_operand_aliasing={{0}: (3, {}), {1}: (4, {})} | custom-call | flops 1000000 | bytes 2400000 | tf_op jit(solution)/shard_map/finish/pallas_call | solution.py:344
  (12 shorter events, 0.1 us)
Async XLA Ops:
  0.6 7.4 %collective-permute-start = (bf16[128,576]{1,0:T(8,128)(2,1)}, bf16[128,576]{1,0:T(8,128)(2,1)S(1)}, u32[]{:S(2)}, u32[]{:S(2)}) collective-permute-start(bf16[128,576]{1,0:T(8,128)(2,1)} %bitcast.15), channel_id=1, source_target_pairs={{0,2},{2,0},{1,3},{3,1},{4,6},{6,4},{5,7},{7,5},{8,10},{10,8},{9,1... | collective-permute-start | bytes 442376 | tf_op jit(solution)/shard_map/ppermute | solution.py:365
  14.0 5.5 %collective-permute-start.1 = (bf16[128,576]{1,0:T(8,128)(2,1)S(1)}, bf16[128,576]{1,0:T(8,128)(2,1)S(1)}, u32[]{:S(2)}, u32[]{:S(2)}) collective-permute-start(bf16[128,576]{1,0:T(8,128)(2,1)S(1)} %get-tuple-element.63), channel_id=1, source_target_pairs={{0,2},{2,0},{1,3},{3,1},{4,6},{6,4},{5,7},{7,5},{8,10},{10,8},{9,1... | collective-permute-start | bytes 442376 | tf_op jit(solution)/shard_map/ppermute | solution.py:365
  15.8 3.7 %collective-permute-start.9 = (bf16[4,2,128,128]{3,2,1,0:T(8,128)(2,1)S(1)}, bf16[4,2,128,128]{3,2,1,0:T(8,128)(2,1)S(1)}, u32[]{:S(2)}, u32[]{:S(2)}) collective-permute-start(bf16[4,2,128,128]{3,2,1,0:T(8,128)(2,1)S(1)} %get-tuple-element.72), channel_id=1, source_target_pairs={{0,1},{1,0},{2,3},{3,2},{4,5},{5,4},{6,7},{7,6},{8,9},{9,8},{10,11... | collective-permute-start | bytes 786440 | tf_op jit(solution)/shard_map/ppermute | solution.py:365
  16.9 27.7 %collective-permute-start.5 = (bf16[8,2,128,128]{3,2,1,0:T(8,128)(2,1)S(1)}, bf16[8,2,128,128]{3,2,1,0:T(8,128)(2,1)S(1)}, u32[]{:S(2)}, u32[]{:S(2)}) collective-permute-start(bf16[8,2,128,128]{3,2,1,0:T(8,128)(2,1)S(1)} %get-tuple-element.66), channel_id=1, source_target_pairs={{0,1},{1,0},{2,3},{3,2},{4,5},{5,4},{6,7},{7,6},{8,9},{9,8},{10,11... | collective-permute-start | bytes 1572872 | tf_op jit(solution)/shard_map/ppermute | solution.py:365
  17.4 11.5 %collective-permute-start.6 = (bf16[8,2,128,128]{3,2,1,0:T(8,128)(2,1)S(1)}, bf16[8,2,128,128]{3,2,1,0:T(8,128)(2,1)S(1)}, u32[]{:S(2)}, u32[]{:S(2)}) collective-permute-start(bf16[8,2,128,128]{3,2,1,0:T(8,128)(2,1)S(1)} %get-tuple-element.68), channel_id=1, source_target_pairs={{0,1},{1,0},{2,3},{3,2},{4,5},{5,4},{6,7},{7,6},{8,9},{9,8},{10,11... | collective-permute-start | bytes 1572872 | tf_op jit(solution)/shard_map/ppermute | solution.py:365
  17.5 25.4 %collective-permute-start.8 = (bf16[4,2,128,128]{3,2,1,0:T(8,128)(2,1)S(1)}, bf16[4,2,128,128]{3,2,1,0:T(8,128)(2,1)S(1)}, u32[]{:S(2)}, u32[]{:S(2)}) collective-permute-start(bf16[4,2,128,128]{3,2,1,0:T(8,128)(2,1)S(1)} %get-tuple-element.70), channel_id=1, source_target_pairs={{0,1},{1,0},{2,3},{3,2},{4,5},{5,4},{6,7},{7,6},{8,9},{9,8},{10,11... | collective-permute-start | bytes 786440 | tf_op jit(solution)/shard_map/ppermute | solution.py:365
  19.4 1.5 %collective-permute-start.12 = (bf16[4,2,128,128]{3,2,1,0:T(8,128)(2,1)S(1)}, bf16[4,2,128,128]{3,2,1,0:T(8,128)(2,1)S(1)}, u32[]{:S(2)}, u32[]{:S(2)}) collective-permute-start(bf16[4,2,128,128]{3,2,1,0:T(8,128)(2,1)S(1)} %get-tuple-element.76), channel_id=1, source_target_pairs={{0,1},{1,0},{2,3},{3,2},{4,5},{5,4},{6,7},{7,6},{8,9},{9,8},{10,11... | collective-permute-start | bytes 786440 | tf_op jit(solution)/shard_map/ppermute | solution.py:365
  19.5 11.2 %collective-permute-start.11 = (bf16[4,2,128,128]{3,2,1,0:T(8,128)(2,1)S(1)}, bf16[4,2,128,128]{3,2,1,0:T(8,128)(2,1)S(1)}, u32[]{:S(2)}, u32[]{:S(2)}) collective-permute-start(bf16[4,2,128,128]{3,2,1,0:T(8,128)(2,1)S(1)} %get-tuple-element.74), channel_id=1, source_target_pairs={{0,1},{1,0},{2,3},{3,2},{4,5},{5,4},{6,7},{7,6},{8,9},{9,8},{10,11... | collective-permute-start | bytes 786440 | tf_op jit(solution)/shard_map/ppermute | solution.py:365
  20.9 6.2 %collective-permute-start.2 = (bf16[128,576]{1,0:T(8,128)(2,1)S(1)}, bf16[128,576]{1,0:T(8,128)(2,1)S(1)}, u32[]{:S(2)}, u32[]{:S(2)}) collective-permute-start(bf16[128,576]{1,0:T(8,128)(2,1)S(1)} %add_convert_fusion.5), channel_id=1, source_target_pairs={{0,4},{4,0},{8,12},{12,8},{16,20},{20,16},{24,28},{28,24},{1,5},{5... | collective-permute-start | bytes 442376 | tf_op jit(solution)/shard_map/ppermute | solution.py:365
  27.2 9.2 %collective-permute-start.13 = (bf16[4,2,128,128]{3,2,1,0:T(8,128)(2,1)S(1)}, bf16[4,2,128,128]{3,2,1,0:T(8,128)(2,1)S(1)}, u32[]{:S(2)}, u32[]{:S(2)}) collective-permute-start(bf16[4,2,128,128]{3,2,1,0:T(8,128)(2,1)S(1)} %add_convert_fusion.1), channel_id=1, source_target_pairs={{0,2},{2,0},{1,3},{3,1},{4,6},{6,4},{5,7},{7,5},{8,10},{10,8},{9,1... | collective-permute-start | bytes 786440 | tf_op jit(solution)/shard_map/ppermute | solution.py:365
  28.9 5.4 %collective-permute-start.3 = (bf16[128,576]{1,0:T(8,128)(2,1)S(1)}, bf16[128,576]{1,0:T(8,128)(2,1)S(1)}, u32[]{:S(2)}, u32[]{:S(2)}) collective-permute-start(bf16[128,576]{1,0:T(8,128)(2,1)S(1)} %add_convert_fusion.4), channel_id=1, source_target_pairs={{0,8},{4,12},{8,0},{12,4},{16,24},{20,28},{24,16},{28,20},{1,9},{5... | collective-permute-start | bytes 442376 | tf_op jit(solution)/shard_map/ppermute | solution.py:365
  30.7 12.3 %collective-permute-start.10 = (bf16[4,2,128,128]{3,2,1,0:T(8,128)(2,1)S(1)}, bf16[4,2,128,128]{3,2,1,0:T(8,128)(2,1)S(1)}, u32[]{:S(2)}, u32[]{:S(2)}) collective-permute-start(bf16[4,2,128,128]{3,2,1,0:T(8,128)(2,1)S(1)} %add_convert_fusion.2), channel_id=1, source_target_pairs={{0,2},{2,0},{1,3},{3,1},{4,6},{6,4},{5,7},{7,5},{8,10},{10,8},{9,1... | collective-permute-start | bytes 786440 | tf_op jit(solution)/shard_map/ppermute | solution.py:365
  34.3 17.3 %collective-permute-start.7 = (bf16[8,2,128,128]{3,2,1,0:T(8,128)(2,1)S(1)}, bf16[8,2,128,128]{3,2,1,0:T(8,128)(2,1)S(1)}, u32[]{:S(2)}, u32[]{:S(2)}) collective-permute-start(bf16[8,2,128,128]{3,2,1,0:T(8,128)(2,1)S(1)} %add_convert_fusion), channel_id=1, source_target_pairs={{0,2},{2,0},{1,3},{3,1},{4,6},{6,4},{5,7},{7,5},{8,10},{10,8},{9,1... | collective-permute-start | bytes 1572872 | tf_op jit(solution)/shard_map/ppermute | solution.py:365
  36.4 7.4 %collective-permute-start.4 = (bf16[128,576]{1,0:T(8,128)(2,1)S(1)}, bf16[128,576]{1,0:T(8,128)(2,1)S(1)}, u32[]{:S(2)}, u32[]{:S(2)}) collective-permute-start(bf16[128,576]{1,0:T(8,128)(2,1)S(1)} %add_convert_fusion.3), channel_id=1, source_target_pairs={{0,24},{4,28},{8,16},{12,20},{16,8},{20,12},{24,0},{28,4},{1,25},{... | collective-permute-start | bytes 442376 | tf_op jit(solution)/shard_map/ppermute | solution.py:365

commit v3 on v2

--- a/solution.py
+++ b/solution.py
@@ -1,4 +1,5 @@
 import functools
+import math
 
 import jax
 import jax.numpy as jnp
@@ -11,7 +12,11 @@
 F32 = jnp.float32
 BF16 = jnp.bfloat16
 MIB = 1024 * 1024
-PLAN = ((4, True), (4, True), (8, False))
+PLAN = ((4, True, (4,)), (12, False, (12,)))
+WAITS = (None, None)
+FARS = {2: (0,)}
+NEARS = {}
+FRONT = True
 
 
 def dot_nn(a, b):
@@ -337,14 +342,15 @@
         value_ref[h] = total[1]
 
 
-def finish(own, near, far, heads, begin, before, group):
-    count, _, depth, width = own.shape
+def finish(own, near, far, inner, heads, begin, before, group):
+    count, _, depth, width = far.shape
     rows = depth // 4
-    offset = begin // group
+    inside, offset = inner // group, begin // group
     return pl.pallas_call(
         finish_kernel,
         grid=(count // group,),
-        in_specs=[pl.BlockSpec((group, 2, depth, width), lambda i: (i, 0, 0, 0))] * 3
+        in_specs=[pl.BlockSpec((group, 2, depth, width), lambda i: (i + inside, 0, 0, 0))] * 2
+        + [pl.BlockSpec((group, 2, depth, width), lambda i: (i, 0, 0, 0))]
         + [pl.BlockSpec(memory_space=pl.ANY)] * len(before),
         out_specs=[
             pl.BlockSpec((group, rows, 4 * width), lambda i: (i + offset, 0, 0)),
@@ -363,6 +369,12 @@
 
 def swap(x, axis, size, bits):
     return lax.ppermute(x, axis, [(i, i ^ bits) for i in range(size)])
+
+
+def after(x, arrays, which):
+    for n in which:
+        x, arrays[n] = lax.optimization_barrier((x, arrays[n]))
+    return x
 
 
 def on_device(
@@ -387,7 +399,7 @@
             2, query_nope[0], rope, grad_out[0], key_up, value_up, own_rows, query_pos, block_table, page_rows
         )
         parts[0] = own
-        plan = [(heads * n // 16, weights) for n, weights in PLAN]
+        plan = [(heads * n // 16, weights, [heads * c // 16 for c in cuts]) for n, weights, cuts in PLAN]
     else:
         qt = jnp.concatenate([jnp.transpose(query_nope[0], (1, 2, 0)), rope], axis=1)
         go, ku, vu = jnp.swapaxes(grad_out[0], 0, 1), key_up, value_up
@@ -401,10 +413,10 @@
         latent = parts[0][:, :latent_width]
         kn_own = jnp.einsum("kl,hnl->khn", latent, key_up, preferred_element_type=F32).astype(BF16).reshape(latent.shape[0], -1)
         va_own = jnp.einsum("kl,hlv->khv", latent, value_up, preferred_element_type=F32).astype(BF16).reshape(latent.shape[0], -1)
-        plan = [(1, True)] * heads
-    pairs, pieces, partials, total = [], [], [], None
+        plan = [(1, True, ())] * heads
+    pairs, partials, pieces, fars, nears, total = [], [], [], [], [], None
     begin = 0
-    for n, (count, weights) in enumerate(plan):
+    for n, (count, weights, cuts) in enumerate(plan):
         final = n == len(plan) - 1
         results = list(attend(
             paired, begin, count, weights, final, qt, go, ku, vu, bias, kn_own, va_own, parts, total,
@@ -415,21 +427,32 @@
             made = results[2:len(results) - len(ends)]
         else:
             made = weight_partials(paired, begin, qt, results[0], results[2], parts, nope_width, latent_width)
-        partials.append((begin, made))
+        partials.append(made)
         total = ends[0]
+        if paired:
+            keep0, keep1, send0, send1 = made
+            near1 = swap(send1, "dp", 2, 1)
+            inner = 0
+            for size in cuts:
+                cut = slice(inner, inner + size)
+                sent = (keep1[cut].astype(F32) + near1[cut].astype(F32)).astype(BF16)
+                pieces.append((keep0, n, inner, begin + inner))
+                if FRONT and n == len(plan) - 2:
+                    total, sent = lax.optimization_barrier((total, sent))
+                fars.append(swap(sent, "ctx", 2, 1))
+                inner += size
+            if WAITS[n] is not None:
+                send0, fars[WAITS[n]] = lax.optimization_barrier((send0, fars[WAITS[n]]))
+            nears.append(swap(send0, "dp", 2, 1))
         begin += count
     if paired:
-        for begin, (keep0, keep1, send0, send1) in partials:
-            near1 = swap(send1, "dp", 2, 1)
-            near0 = swap(send0, "dp", 2, 1)
-            far = swap((keep1.astype(F32) + near1.astype(F32)).astype(BF16), "ctx", 2, 1)
-            pieces.append((begin, (keep0, near0, far)))
         grad_nope, grad_rope = query_gradient(pairs, parts, query_rope.shape[3])
         mine, other = ends
+        other = after(other, fars, FARS.get(0, ()))
         share = mine.astype(F32) + swap(other, "ctx", 2, 1).astype(F32)
     else:
         ds, kn = (jnp.concatenate(x, axis=0) for x in zip(*pairs))
-        wk, wv = (jnp.concatenate(x, axis=0) for x in zip(*(made for _, made in partials)))
+        wk, wv = (jnp.concatenate(x, axis=0) for x in zip(*partials))
         grad_nope = jnp.einsum("hkq,hkn->qhn", ds, kn, preferred_element_type=F32)[None]
         rotary = parts[0][:, latent_width:]
         grad_rope = jnp.einsum("hkq,kr->qhr", ds, rotary, preferred_element_type=F32)[None]
@@ -437,18 +460,21 @@
         grad_value_map = lax.psum_scatter(wv, ("ctx", "dp"), scatter_dimension=1, tiled=True).astype(F32)
         share = lax.psum_scatter(ends[0], "ctx", scatter_dimension=0, tiled=True).astype(F32)
     if head_size & (head_size - 1) == 0:
-        bits = 1
+        bits, n = 1, 0
         while bits < head_size:
             rounded = share.astype(BF16)
+            if paired:
+                rounded = after(rounded, fars, FARS.get(n + 1, ()))
+                rounded = after(rounded, nears, NEARS.get(n + 1, ()))
             got = swap(rounded, "head", head_size, bits | (bits >> 1) if bits >= 4 else bits)
             share = rounded.astype(F32) + got.astype(F32)
-            bits *= 2
+            bits, n = bits * 2, n + 1
     else:
         share = lax.psum(share.astype(BF16), "head").astype(F32)
     if paired:
         maps = ()
-        for begin, piece in pieces:
-            maps = finish(*piece, heads, begin, maps, min(4, piece[0].shape[0]))
+        for (own0, n, inner, begin), far in zip(pieces, fars):
+            maps = finish(own0, nears[n], far, inner, heads, begin, maps, math.gcd(begin, inner, far.shape[0]))
         grad_key_map, grad_value_map = maps
     return (
         grad_nope,

time: 52.8 us -> 47.6 us (0.902)
  waiting for transfers between devices: 19.2 us -> 16.1 us
  starting transfers between devices: 16.1 us -> 14.4 us
    ppermute x14 -> x11, waiting for transfers between devices: 19.2 us -> 16.1 us  [swap(): return lax.ppermute(x, axis, [(i, i ^ bits) for i in range(size)])]
    ppermute x14 -> x11, starting transfers between devices: 16.1 us -> 14.4 us  [swap(): return lax.ppermute(x, axis, [(i, i ^ bits) for i in range(size)])]
    pallas_call x3 -> x2, Pallas kernels: 5.86 us -> 5.21 us  [attend(): pl.pallas_call(functools.partial(attend_kernel, paired, before is None, f...]
    pallas_call x3 -> x2, Pallas kernels: 2.77 us -> 2.66 us  [finish(): pl.pallas_call(finish_kernel, grid=(count // group,), in_specs=[pl.BlockS...]
  transfers between devices with their start and end apart: 14 -> 11, of which waited for: 7 -> 8; matrix products, arithmetic and copies ran while one was open for 2% -> 2% of each run, Pallas kernels for 16% -> 14%
where the time goes in v3:
time: 47.6 us; the launch traced here: 47.5 us
  waiting for transfers between devices  16.1 us (34%)
  Pallas kernels  15.1 us (32%)
  starting transfers between devices  14.4 us (30%)
  other arithmetic  1.24 us (3%)
  between operations  0.7 us (1%)
    ppermute x11, waiting for transfers between devices, swap(): return lax.ppermute(x, axis, [(i, i ^ bits) for i in range(size)])  16.1 us
    ppermute x11, starting transfers between devices, swap(): return lax.ppermute(x, axis, [(i, i ^ bits) for i in range(size)])  14.4 us
    pallas_call x2, Pallas kernels, attend(): pl.pallas_call(functools.partial(attend_kernel, paired, before is None, f...  5.21 us
    pallas_call x1, Pallas kernels, prepare(): pl.pallas_call(functools.partial(prepare_kernel, parts, page_rows), in_sp...  3.71 us
    pallas_call x2, Pallas kernels, finish(): pl.pallas_call(finish_kernel, grid=(count // group,), in_specs=[pl.BlockS...  2.66 us
    pallas_call x1, Pallas kernels, query_gradient(): pl.pallas_call(functools.partial(query_kernel, counts, len(parts)), out_s...  1.92 us
    pallas_call x1, Pallas kernels, weight_partials(): pl.pallas_call(functools.partial(weights_kernel, paired, len(parts), begi...  1.57 us
  transfers between devices with their start and end apart: 11, of which 8 were waited for; matrix products, arithmetic and copies ran while one was open for 2% of the time, Pallas kernels for 14%

profile of v3, /device:TPU:0, one launch (start us, length us, event | category | flops | bytes accessed | tf_op | source)
XLA Modules:
  0.0 47.5 jit_solution(17993059026303105821)
XLA Ops:
  0.6 3.0 %collective-permute-start = (bf16[128,576]{1,0:T(8,128)(2,1)}, bf16[128,576]{1,0:T(8,128)(2,1)S(1)}, u32[]{:S(2)}, u32[]{:S(2)}) collective-permute-start(bf16[128,576]{1,0:T(8,128)(2,1)} %bitcast.15), channel_id=1, source_target_pairs={{0,2},{2,0},{1,3},{3,1},{4,6},{6,4},{5,7},{7,5},{8,10},{10,8},{9,1... | collective-permute-start | bytes 442376 | tf_op jit(solution)/shard_map/ppermute | solution.py:371
  3.7 3.7 %prepare.1 = (bf16[16,192,128]{2,1,0:T(8,128)(2,1)S(1)}, bf16[16,128,128]{2,1,0:T(8,128)(2,1)S(1)}, bf16[16,128,512]{2,1,0:T(8,128)(2,1)S(1)}, bf16[16,512,128]{...) custom-call(bf16[128,16,128]{2,1,0:T(8,128)(2,1)} %bitcast.11, ...), custom_call_target="tpu_custom_call" | custom-call | flops 600000000 | bytes 12000000 | tf_op jit(solution)/shard_map/prepare/pallas_call | solution.py:97
  7.4 0.7 %collective-permute-done.rest_1_.refs_1_ = bf16[128,576]{1,0:T(8,128)(2,1)S(1)} collective-permute-done((bf16[128,576]{1,0:T(8,128)(2,1)}, bf16[128,576]{1,0:T(8,128)(2,1)S(1)}, u32[]{:S(2)}, u32[]{:S(2)}) %collective-permute-start) | collective-permute-done | bytes 147488 | tf_op jit(solution)/shard_map/ppermute | solution.py:371
  8.1 1.7 %attend.2 = (bf16[4,256,128]{2,1,0:T(8,128)(2,1)S(1)}, bf16[4,256,128]{2,1,0:T(8,128)(2,1)S(1)}, bf16[4,2,128,128]{3,2,1,0:T(8,128)(2,1)S(1)}, bf16[4,2,128,128]...) custom-call(bf16[16,192,128]{2,1,0:T(8,128)(2,1)S(1)} %get-tuple-ele, ...), custom_call_target="tpu_custom_call" | custom-call | flops 1600000000 | bytes 2000000 | tf_op jit(solution)/shard_map/attend/pallas_call | solution.py:262
  9.8 0.1 collective-permute-start.1
  9.9 1.5 %collective-permute-done.1 = bf16[4,2,128,128]{3,2,1,0:T(8,128)(2,1)S(1)} collective-permute-done((bf16[4,2,128,128]{3,2,1,0:T(8,128)(2,1)S(1)}, bf16[4,2,128,128]{3,2,1,0:T(8,128)(2,1)S(1)}, u32[]{:S(2)}, u32[]{:S(2)}) %collective-permute-start.1) | collective-permute-done | bytes 262176 | tf_op jit(solution)/shard_map/ppermute | solution.py:371
  11.4 0.1 add_convert_fusion.1
  11.5 3.5 %attend.3 = (bf16[12,256,128]{2,1,0:T(8,128)(2,1)S(1)}, bf16[12,256,128]{2,1,0:T(8,128)(2,1)S(1)}, bf16[256,1536]{1,0:T(8,128)(2,1)S(1)}, bf16[128,576]{1,0:T(8,128)(2,1)S(1)}, bf16[128,576]{1,0:T(8,128)(2,1)S(1)}) custom-call(bf16[16,192,128]{2,1,0:T(8,128)(2,1)S(1)} %get-tuple-element.40.qt_ref, bf16[16,128,128]{2,1,0:T(8,128)(2,1)S(1)} %get-tuple-element.41.go_ref, ...), custom_call_target="tpu_custom_call" | custom-call | flops 3600000000 | bytes 6000000 | tf_op jit(solution)/shard_map/attend/pallas_call | solution.py:262
  15.0 1.6 %weight_partials.1 = (bf16[12,2,128,128]{3,2,1,0:T(8,128)(2,1)S(1)}, bf16[12,2,128,128]{3,2,1,0:T(8,128)(2,1)S(1)}, bf16[12,2,128,128]{3,2,1,0:T(8,128)(2,1)S(1)}, bf16[12,2,128,128]{3,2,1,0:T(8,128)(2,1)S(1)}) custom-call(bf16[16,192,128]{2,1,0:T(8,128)(2,1)S(1)} %get-tuple-element.40.qt_ref, bf16[12,256,128]{2,1,0:T(8,128)(2,1)S(1)} %get-tuple-element.53.refs_4_.ds_ref, ...), custom_call_target="tpu_custom_call" | custom-call | flops 1200000000 | bytes 4800000 | tf_op jit(solution)/shard_map/weight_partials/pallas_call | solution.py:289
  16.5 0.2 collective-permute-start.8
  16.7 1.7 %collective-permute-start.2 = (bf16[128,576]{1,0:T(8,128)(2,1)S(1)}, bf16[128,576]{1,0:T(8,128)(2,1)S(1)}, u32[]{:S(2)}, u32[]{:S(2)}) collective-permute-start(bf16[128,576]{1,0:T(8,128)(2,1)S(1)} %get-tuple-element.58), channel_id=1, source_target_pairs={{0,2},{2,0},{1,3},{3,1},{4,6},{6,4},{5,7},{7,5},{8,10},{10,8},{9,1... | collective-permute-start | bytes 442376 | tf_op jit(solution)/shard_map/ppermute | solution.py:371
  18.5 0.3 collective-permute-start.4
  18.8 0.0 collective-permute-start.7
  18.8 5.0 %collective-permute-done.2 = bf16[128,576]{1,0:T(8,128)(2,1)S(1)} collective-permute-done((bf16[128,576]{1,0:T(8,128)(2,1)S(1)}, bf16[128,576]{1,0:T(8,128)(2,1)S(1)}, u32[]{:S(2)}, u32[]{:S(2)}) %collective-permute-start.2) | collective-permute-done | bytes 147488 | tf_op jit(solution)/shard_map/ppermute | solution.py:371
  23.8 1.8 %collective-permute-start.3 = (bf16[128,576]{1,0:T(8,128)(2,1)S(1)}, bf16[128,576]{1,0:T(8,128)(2,1)S(1)}, u32[]{:S(2)}, u32[]{:S(2)}) collective-permute-start(bf16[128,576]{1,0:T(8,128)(2,1)S(1)} %add_convert_fusion.4), channel_id=1, source_target_pairs={{0,4},{4,0},{8,12},{12,8},{16,20},{20,16},{24,28},{28,24},{1,5},{5... | collective-permute-start | bytes 442376 | tf_op jit(solution)/shard_map/ppermute | solution.py:371
  25.6 0.0 collective-permute-done.8
  25.6 0.3 add_convert_fusion
  25.9 1.6 %collective-permute-start.9 = (bf16[12,2,128,128]{3,2,1,0:T(8,128)(2,1)S(1)}, bf16[12,2,128,128]{3,2,1,0:T(8,128)(2,1)S(1)}, u32[]{:S(2)}, u32[]{:S(2)}) collective-permute-start(bf16[12,2,128,128]{3,2,1,0:T(8,128)(2,1)S(1)} %add_convert_fusion), channel_id=1, source_target_pairs={{0,2},{2,0},{1,3},{3,1},{4,6},{6,4},{5,7},{7,5},{8,10},{10,8},{9,1... | collective-permute-start | bytes 2359304 | tf_op jit(solution)/shard_map/ppermute | solution.py:371
  27.5 1.7 %collective-permute-done.3 = bf16[128,576]{1,0:T(8,128)(2,1)S(1)} collective-permute-done((bf16[128,576]{1,0:T(8,128)(2,1)S(1)}, bf16[128,576]{1,0:T(8,128)(2,1)S(1)}, u32[]{:S(2)}, u32[]{:S(2)}) %collective-permute-start.3) | collective-permute-done | bytes 147488 | tf_op jit(solution)/shard_map/ppermute | solution.py:371
  29.2 0.1 collective-permute-done.4.far_ref
  29.4 1.8 %collective-permute-start.5 = (bf16[128,576]{1,0:T(8,128)(2,1)S(1)}, bf16[128,576]{1,0:T(8,128)(2,1)S(1)}, u32[]{:S(2)}, u32[]{:S(2)}) collective-permute-start(bf16[128,576]{1,0:T(8,128)(2,1)S(1)} %add_convert_fusion.3), channel_id=1, source_target_pairs={{0,8},{4,12},{8,0},{12,4},{16,24},{20,28},{24,16},{28,20},{1,9},{5... | collective-permute-start | bytes 442376 | tf_op jit(solution)/shard_map/ppermute | solution.py:371
  31.2 0.0 collective-permute-start.10
  31.2 3.5 %collective-permute-done.5 = bf16[128,576]{1,0:T(8,128)(2,1)S(1)} collective-permute-done((bf16[128,576]{1,0:T(8,128)(2,1)S(1)}, bf16[128,576]{1,0:T(8,128)(2,1)S(1)}, u32[]{:S(2)}, u32[]{:S(2)}) %collective-permute-start.5) | collective-permute-done | bytes 147488 | tf_op jit(solution)/shard_map/ppermute | solution.py:371
  34.8 3.9 %collective-permute-start.6 = (bf16[128,576]{1,0:T(8,128)(2,1)S(1)}, bf16[128,576]{1,0:T(8,128)(2,1)S(1)}, u32[]{:S(2)}, u32[]{:S(2)}) collective-permute-start(bf16[128,576]{1,0:T(8,128)(2,1)S(1)} %add_convert_fusion.2), channel_id=1, source_target_pairs={{0,24},{4,28},{8,16},{12,20},{16,8},{20,12},{24,0},{28,4},{1,25},{... | collective-permute-start | bytes 442376 | tf_op jit(solution)/shard_map/ppermute | solution.py:371
  38.6 1.9 %query_gradient.1 = (f32[2048,128]{1,0:T(8,128)}, f32[16,64,128]{2,1,0:T(8,128)}) custom-call(bf16[128,576]{1,0:T(8,128)(2,1)S(1)} %get-tuple-element.39.rest_0_.refs_0_, bf16[128,576]{1,0:T(8,128)(2,1)S(1)} %collective-permute-done.rest_1_.refs_1_, bf16[4,256,128]{2,1,0:T(8,128)(2,1)S(1)} %get-tuple-element.47.refs_2_, ...), custom_call_target="tpu_custom_call" | custom-call | flops 1000000000 | bytes 5000000 | tf_op jit(solution)/shard_map/query_gradient/pallas_call | solution.py:321
  40.6 0.0 collective-permute-done.10.near_ref
  40.6 0.9 %finish.2 = (f32[16,32,512]{2,1,0:T(8,128)}, f32[16,128,128]{2,1,0:T(8,128)}) custom-call(bf16[4,2,128,128]{3,2,1,0:T(8,128)(2,1)S(1)} %get-tuple-element.66.own_ref, bf16[4,2,128,128]{3,2,1,0:T(8,128)(2,1)S(1)} %collective-permute-done.10.near_ref, bf16[4,2,128,128]{3,2,1,0:T(8,128)(2,1)S(1)} %collective-permute-done.4.far_ref), custom_call_target="tpu_custom_call" | custom-call | flops 1000000 | bytes 1200000 | tf_op jit(solution)/shard_map/finish/pallas_call | solution.py:349
  41.4 0.6 %collective-permute-done.6 = bf16[128,576]{1,0:T(8,128)(2,1)S(1)} collective-permute-done((bf16[128,576]{1,0:T(8,128)(2,1)S(1)}, bf16[128,576]{1,0:T(8,128)(2,1)S(1)}, u32[]{:S(2)}, u32[]{:S(2)}) %collective-permute-start.6) | collective-permute-done | bytes 147488 | tf_op jit(solution)/shard_map/ppermute | solution.py:371
  42.0 0.8 %convert_add_fusion = f32[128,576]{1,0:T(8,128)} fusion(bf16[128,576]{1,0:T(8,128)(2,1)S(1)} %collective-permute-done.6, bf16[128,576]{1,0:T(8,128)(2,1)S(1)} %add_convert_fusion.2), kind=kLoop, calls=%fused_computation.2 | loop fusion | flops 221184 | bytes 589824 | tf_op jit(solution)/shard_map/add | solution.py:470
  42.8 0.0 collective-permute-done.7.near_ref
  42.8 2.9 %collective-permute-done.9.far_ref = bf16[12,2,128,128]{3,2,1,0:T(8,128)(2,1)S(1)} collective-permute-done((bf16[12,2,128,128]{3,2,1,0:T(8,128)(2,1)S(1)}, bf16[12,2,128,128]{3,2,1,0:T(8,128)(2,1)S(1)}, u32[]{:S(2)}, u32[]{:S(2)}) %collective-permute-start.9) | collective-permute-done | bytes 786464 | tf_op jit(solution)/shard_map/ppermute | solution.py:371
  45.7 1.8 %finish.3 = (f32[16,32,512]{2,1,0:T(8,128)}, f32[16,128,128]{2,1,0:T(8,128)}) custom-call(bf16[12,2,128,128]{3,2,1,0:T(8,128)(2,1)S(1)} %get-tuple-element.62.own_ref, bf16[12,2,128,128]{3,2,1,0:T(8,128)(2,1)S(1)} %collective-permute-done.7.near_ref, ...), custom_call_target="tpu_custom_call", output_to_operand_aliasing={{0}: (3, {}), {1}: (4, {})} | custom-call | flops 1000000 | bytes 3600000 | tf_op jit(solution)/shard_map/finish/pallas_call | solution.py:349
  (3 shorter events, 0.1 us)
Async XLA Ops:
  0.6 7.4 %collective-permute-start = (bf16[128,576]{1,0:T(8,128)(2,1)}, bf16[128,576]{1,0:T(8,128)(2,1)S(1)}, u32[]{:S(2)}, u32[]{:S(2)}) collective-permute-start(bf16[128,576]{1,0:T(8,128)(2,1)} %bitcast.15), channel_id=1, source_target_pairs={{0,2},{2,0},{1,3},{3,1},{4,6},{6,4},{5,7},{7,5},{8,10},{10,8},{9,1... | collective-permute-start | bytes 442376 | tf_op jit(solution)/shard_map/ppermute | solution.py:371
  9.8 1.6 %collective-permute-start.1 = (bf16[4,2,128,128]{3,2,1,0:T(8,128)(2,1)S(1)}, bf16[4,2,128,128]{3,2,1,0:T(8,128)(2,1)S(1)}, u32[]{:S(2)}, u32[]{:S(2)}) collective-permute-start(bf16[4,2,128,128]{3,2,1,0:T(8,128)(2,1)S(1)} %get-tuple-element.51), channel_id=1, source_target_pairs={{0,1},{1,0},{2,3},{3,2},{4,5},{5,4},{6,7},{7,6},{8,9},{9,8},{10,11... | collective-permute-start | bytes 786440 | tf_op jit(solution)/shard_map/ppermute | solution.py:371
  16.5 9.1 %collective-permute-start.8 = (bf16[12,2,128,128]{3,2,1,0:T(8,128)(2,1)S(1)}, bf16[12,2,128,128]{3,2,1,0:T(8,128)(2,1)S(1)}, u32[]{:S(2)}, u32[]{:S(2)}) collective-permute-start(bf16[12,2,128,128]{3,2,1,0:T(8,128)(2,1)S(1)} %get-tuple-element.65), channel_id=1, source_target_pairs={{0,1},{1,0},{2,3},{3,2},{4,5},{5,4},{6,7},{7,6},{8,9},{9,8},{10,11... | collective-permute-start | bytes 2359304 | tf_op jit(solution)/shard_map/ppermute | solution.py:371
  16.7 7.0 %collective-permute-start.2 = (bf16[128,576]{1,0:T(8,128)(2,1)S(1)}, bf16[128,576]{1,0:T(8,128)(2,1)S(1)}, u32[]{:S(2)}, u32[]{:S(2)}) collective-permute-start(bf16[128,576]{1,0:T(8,128)(2,1)S(1)} %get-tuple-element.58), channel_id=1, source_target_pairs={{0,2},{2,0},{1,3},{3,1},{4,6},{6,4},{5,7},{7,5},{8,10},{10,8},{9,1... | collective-permute-start | bytes 442376 | tf_op jit(solution)/shard_map/ppermute | solution.py:371
  18.5 10.9 %collective-permute-start.4 = (bf16[4,2,128,128]{3,2,1,0:T(8,128)(2,1)S(1)}, bf16[4,2,128,128]{3,2,1,0:T(8,128)(2,1)S(1)}, u32[]{:S(2)}, u32[]{:S(2)}) collective-permute-start(bf16[4,2,128,128]{3,2,1,0:T(8,128)(2,1)S(1)} %add_convert_fusion.1), channel_id=1, source_target_pairs={{0,2},{2,0},{1,3},{3,1},{4,6},{6,4},{5,7},{7,5},{8,10},{10,8},{9,1... | collective-permute-start | bytes 786440 | tf_op jit(solution)/shard_map/ppermute | solution.py:371
  18.8 24.0 %collective-permute-start.7 = (bf16[12,2,128,128]{3,2,1,0:T(8,128)(2,1)S(1)}, bf16[12,2,128,128]{3,2,1,0:T(8,128)(2,1)S(1)}, u32[]{:S(2)}, u32[]{:S(2)}) collective-permute-start(bf16[12,2,128,128]{3,2,1,0:T(8,128)(2,1)S(1)} %get-tuple-element.63), channel_id=1, source_target_pairs={{0,1},{1,0},{2,3},{3,2},{4,5},{5,4},{6,7},{7,6},{8,9},{9,8},{10,11... | collective-permute-start | bytes 2359304 | tf_op jit(solution)/shard_map/ppermute | solution.py:371
  23.8 5.4 %collective-permute-start.3 = (bf16[128,576]{1,0:T(8,128)(2,1)S(1)}, bf16[128,576]{1,0:T(8,128)(2,1)S(1)}, u32[]{:S(2)}, u32[]{:S(2)}) collective-permute-start(bf16[128,576]{1,0:T(8,128)(2,1)S(1)} %add_convert_fusion.4), channel_id=1, source_target_pairs={{0,4},{4,0},{8,12},{12,8},{16,20},{20,16},{24,28},{28,24},{1,5},{5... | collective-permute-start | bytes 442376 | tf_op jit(solution)/shard_map/ppermute | solution.py:371
  25.9 19.8 %collective-permute-start.9 = (bf16[12,2,128,128]{3,2,1,0:T(8,128)(2,1)S(1)}, bf16[12,2,128,128]{3,2,1,0:T(8,128)(2,1)S(1)}, u32[]{:S(2)}, u32[]{:S(2)}) collective-permute-start(bf16[12,2,128,128]{3,2,1,0:T(8,128)(2,1)S(1)} %add_convert_fusion), channel_id=1, source_target_pairs={{0,2},{2,0},{1,3},{3,1},{4,6},{6,4},{5,7},{7,5},{8,10},{10,8},{9,1... | collective-permute-start | bytes 2359304 | tf_op jit(solution)/shard_map/ppermute | solution.py:371
  29.4 5.3 %collective-permute-start.5 = (bf16[128,576]{1,0:T(8,128)(2,1)S(1)}, bf16[128,576]{1,0:T(8,128)(2,1)S(1)}, u32[]{:S(2)}, u32[]{:S(2)}) collective-permute-start(bf16[128,576]{1,0:T(8,128)(2,1)S(1)} %add_convert_fusion.3), channel_id=1, source_target_pairs={{0,8},{4,12},{8,0},{12,4},{16,24},{20,28},{24,16},{28,20},{1,9},{5... | collective-permute-start | bytes 442376 | tf_op jit(solution)/shard_map/ppermute | solution.py:371
  31.2 9.4 %collective-permute-start.10 = (bf16[4,2,128,128]{3,2,1,0:T(8,128)(2,1)S(1)}, bf16[4,2,128,128]{3,2,1,0:T(8,128)(2,1)S(1)}, u32[]{:S(2)}, u32[]{:S(2)}) collective-permute-start(bf16[4,2,128,128]{3,2,1,0:T(8,128)(2,1)S(1)} %get-tuple-element.67), channel_id=1, source_target_pairs={{0,1},{1,0},{2,3},{3,2},{4,5},{5,4},{6,7},{7,6},{8,9},{9,8},{10,11... | collective-permute-start | bytes 786440 | tf_op jit(solution)/shard_map/ppermute | solution.py:371
  34.8 7.3 %collective-permute-start.6 = (bf16[128,576]{1,0:T(8,128)(2,1)S(1)}, bf16[128,576]{1,0:T(8,128)(2,1)S(1)}, u32[]{:S(2)}, u32[]{:S(2)}) collective-permute-start(bf16[128,576]{1,0:T(8,128)(2,1)S(1)} %add_convert_fusion.2), channel_id=1, source_target_pairs={{0,24},{4,28},{8,16},{12,20},{16,8},{20,12},{24,0},{28,4},{1,25},{... | collective-permute-start | bytes 442376 | tf_op jit(solution)/shard_map/ppermute | solution.py:371

commit v4 on v2

--- a/solution.py
+++ b/solution.py
@@ -1,4 +1,5 @@
 import functools
+import math
 
 import jax
 import jax.numpy as jnp
@@ -11,7 +12,16 @@
 F32 = jnp.float32
 BF16 = jnp.bfloat16
 MIB = 1024 * 1024
-PLAN = ((4, True), (4, True), (8, False))
+PLAN = ((4, True), (4, False), (4, False), (4, False))
+CUTS = ((4,), (4,), (4,), (4,))
+GROUPS = ((0,), (1,), (2,))
+WAITS = (None, None, None, None)
+FARS = {2: (0,)}
+NEARS = {}
+FRONT = 1
+WEIGHT_COST = 100_000_000
+JOIN = (2, 3)
+LATE = True
 
 
 def dot_nn(a, b):
@@ -264,31 +274,35 @@
     )(qt, go, key_up, value_up, bias, kn_own, va_own, *parts, *([] if before is None else [before]))
 
 
-def weights_kernel(paired, parts, begin, latent_width, qt_ref, ds_ref, gv_ref, *rest):
+def weights_kernel(paired, parts, counts, begin, latent_width, qt_ref, *rest):
+    chunk_refs, rest = rest[:2 * len(counts)], rest[2 * len(counts):]
     part_refs, outs, vt_ref, bp_ref = rest[:parts], rest[parts:-2], rest[-2], rest[-1]
     latent = jnp.concatenate([r[:, :latent_width] for r in part_refs], axis=0)
     turned_values(paired, latent, vt_ref)
-    count = ds_ref.shape[0]
-    value_width = gv_ref.shape[1] // count
-    nope_width = bp_ref.shape[1] if not paired else gv_ref.shape[1] // count
-    group = min(4, count)
-    for g in range(0, count, group):
-        weight_group(
-            paired, g, [qt_ref[begin + g + i, :nope_width] for i in range(group)], [ds_ref[g + i] for i in range(group)],
-            gv_ref[:, g * value_width:(g + group) * value_width], latent, vt_ref, bp_ref, outs,
-        )
-
-
-def weight_partials(paired, begin, qt, ds, gv, parts, nope_width, latent_width):
-    count, key_count, _ = ds.shape
+    at = 0
+    for n, count in enumerate(counts):
+        ds_ref, gv_ref = chunk_refs[2 * n], chunk_refs[2 * n + 1]
+        value_width = gv_ref.shape[1] // count
+        group = min(4, count)
+        for g in range(0, count, group):
+            weight_group(
+                paired, at, [qt_ref[begin + at + i, :value_width] for i in range(group)], [ds_ref[g + i] for i in range(group)],
+                gv_ref[:, g * value_width:(g + group) * value_width], latent, vt_ref, bp_ref, outs,
+            )
+            at += group
+
+
+def weight_partials(begin, qt, chunks, parts, nope_width, latent_width):
+    counts = [ds.shape[0] for ds, _ in chunks]
+    count, key_count = sum(counts), chunks[0][0].shape[1]
     return pl.pallas_call(
-        functools.partial(weights_kernel, paired, len(parts), begin, latent_width),
-        out_shape=partial_shapes(paired, count, nope_width, latent_width, gv.shape[1] // count),
-        scratch_shapes=partial_scratch(paired, min(4, count), key_count, nope_width, latent_width),
+        functools.partial(weights_kernel, True, len(parts), counts, begin, latent_width),
+        out_shape=partial_shapes(True, count, nope_width, latent_width, nope_width),
+        scratch_shapes=partial_scratch(True, 4, key_count, nope_width, latent_width),
         compiler_params=params(14),
-        cost_estimate=cost(count * 100_000_000, count * 400_000),
+        cost_estimate=cost(count * WEIGHT_COST, count * 400_000),
         name="weight_partials",
-    )(qt, ds, gv, *parts)
+    )(qt, *[x for chunk in chunks for x in chunk], *parts)
 
 
 def query_kernel(counts, parts, *refs):
@@ -326,43 +340,64 @@
     return nope.reshape(1, query_count, heads, nope_width), jnp.transpose(rope, (2, 0, 1))[None]
 
 
-def finish_kernel(own_ref, near_ref, far_ref, *rest):
-    key_ref, value_ref = rest[-2:]
-    rows = key_ref.shape[1]
-    width = own_ref.shape[3]
-    for h in range(key_ref.shape[0]):
-        total = own_ref[h].astype(F32) + near_ref[h].astype(F32) + far_ref[h].astype(F32)
-        for j in range(key_ref.shape[2] // width):
-            key_ref[h, :, j * width:(j + 1) * width] = total[0, j * rows:(j + 1) * rows]
-        value_ref[h] = total[1]
-
-
-def finish(own, near, far, heads, begin, before, group):
-    count, _, depth, width = own.shape
+def finish_kernel(places, first, far_ref, *rest):
+    sources, rest = rest[:2 * len(places)], rest[2 * len(places) + (0 if first else 2):]
+    key_hbm, value_hbm, key_ref, value_ref, sems = rest
+    rows, width = key_ref.shape[1], value_ref.shape[2]
+    copies = []
+    for n, (inner, count, at, begin) in enumerate(places):
+        own_ref, near_ref = sources[2 * n], sources[2 * n + 1]
+        step = math.gcd(count, 2)
+        for g in range(0, count, step):
+            for h in range(g, g + step):
+                total = own_ref[inner + h].astype(F32) + near_ref[inner + h].astype(F32) + far_ref[at + h].astype(F32)
+                for j in range(key_ref.shape[2] // width):
+                    key_ref[at + h, :, j * width:(j + 1) * width] = total[0, j * rows:(j + 1) * rows]
+                value_ref[at + h] = total[1]
+            for source, target in ((key_ref, key_hbm), (value_ref, value_hbm)):
+                copies.append(pltpu.make_async_copy(
+                    source.at[at + g:at + g + step], target.at[begin + g:begin + g + step], sems.at[len(copies)]
+                ))
+                copies[-1].start()
+    for copy in copies:
+        copy.wait()
+
+
+def finish(pieces, far, heads, before):
+    total, _, depth, width = far.shape
     rows = depth // 4
-    offset = begin // group
+    places = [(inner, count, at, begin) for _, _, inner, count, at, begin in pieces]
+    moves = sum(2 * count // math.gcd(count, 2) for _, count, _, _ in places)
+    vmem, hbm = pl.BlockSpec(memory_space=pltpu.VMEM), pl.BlockSpec(memory_space=pltpu.HBM)
+    operands = [far] + [x for piece in pieces for x in piece[:2]]
     return pl.pallas_call(
-        finish_kernel,
-        grid=(count // group,),
-        in_specs=[pl.BlockSpec((group, 2, depth, width), lambda i: (i, 0, 0, 0))] * 3
-        + [pl.BlockSpec(memory_space=pl.ANY)] * len(before),
-        out_specs=[
-            pl.BlockSpec((group, rows, 4 * width), lambda i: (i + offset, 0, 0)),
-            pl.BlockSpec((group, depth, width), lambda i: (i + offset, 0, 0)),
-        ],
+        functools.partial(finish_kernel, places, not before),
+        in_specs=[vmem] * len(operands) + [hbm] * len(before),
+        out_specs=[hbm] * 2,
         out_shape=[
             jax.ShapeDtypeStruct((heads, rows, 4 * width), F32),
             jax.ShapeDtypeStruct((heads, depth, width), F32),
         ],
-        input_output_aliases={3: 0, 4: 1} if before else {},
+        scratch_shapes=[
+            pltpu.VMEM((total, rows, 4 * width), F32),
+            pltpu.VMEM((total, depth, width), F32),
+            pltpu.SemaphoreType.DMA((moves,)),
+        ],
+        input_output_aliases={len(operands): 0, len(operands) + 1: 1} if before else {},
         compiler_params=params(8),
-        cost_estimate=pl.CostEstimate(flops=1_000_000, bytes_accessed=300_000 * count, transcendentals=0),
+        cost_estimate=cost(1_000_000, 300_000 * total),
         name="finish",
-    )(own, near, far, *before)
+    )(*operands, *before)
 
 
 def swap(x, axis, size, bits):
     return lax.ppermute(x, axis, [(i, i ^ bits) for i in range(size)])
+
+
+def after(x, arrays, which):
+    for n in which:
+        x, arrays[n] = lax.optimization_barrier((x, arrays[n]))
+    return x
 
 
 def on_device(
@@ -402,34 +437,61 @@
         kn_own = jnp.einsum("kl,hnl->khn", latent, key_up, preferred_element_type=F32).astype(BF16).reshape(latent.shape[0], -1)
         va_own = jnp.einsum("kl,hlv->khv", latent, value_up, preferred_element_type=F32).astype(BF16).reshape(latent.shape[0], -1)
         plan = [(1, True)] * heads
-    pairs, pieces, partials, total = [], [], [], None
+    pairs, partials, pieces, fars, nears, later, total = [], [], [], [], [], [], None
+
+    def send(begin, made):
+        n = len(nears)
+        keep0, keep1, send0, send1 = made
+        near1 = swap(send1, "dp", 2, 1)
+        inner = 0
+        for size in CUTS[n]:
+            cut = slice(inner, inner + heads * size // 16)
+            sums = (keep1[cut].astype(F32) + near1[cut].astype(F32)).astype(BF16)
+            at = 0
+            if n in JOIN:
+                at = fars[-1].shape[0]
+                sums = jnp.concatenate([fars.pop(), sums], axis=0)
+            pieces.append((keep0, n, (inner, cut.stop - inner, at, begin + inner), len(fars)))
+            fars.append(sums)
+            inner = cut.stop
+        nears.append(send0)
+
     begin = 0
     for n, (count, weights) in enumerate(plan):
         final = n == len(plan) - 1
+        if paired and final and FRONT:
+            total, *fars[:FRONT] = lax.optimization_barrier((total, *fars[:FRONT]))
         results = list(attend(
             paired, begin, count, weights, final, qt, go, ku, vu, bias, kn_own, va_own, parts, total,
         ))
         pairs.append((results[0], results[1]))
         ends = results[-len(parts):] if final else results[-1:]
-        if weights:
-            made = results[2:len(results) - len(ends)]
+        if not weights:
+            later.append((begin, (results[0], results[2])))
+        elif paired:
+            send(begin, results[2:6])
         else:
-            made = weight_partials(paired, begin, qt, results[0], results[2], parts, nope_width, latent_width)
-        partials.append((begin, made))
+            partials.append(results[2:4])
         total = ends[0]
         begin += count
+    for group in GROUPS if paired else ():
+        chunks = [later[n][1] for n in group]
+        if LATE and group[-1] != len(later) - 1:
+            ends[-1], chunks[-1] = lax.optimization_barrier((ends[-1], chunks[-1]))
+        send(later[group[0]][0], weight_partials(later[group[0]][0], qt, chunks, parts, nope_width, latent_width))
+    fars = [swap(x, "ctx", 2, 1) for x in fars]
+    for n, send0 in enumerate(nears):
+        if WAITS[n] is not None:
+            send0, fars[WAITS[n]] = lax.optimization_barrier((send0, fars[WAITS[n]]))
+        nears[n] = swap(send0, "dp", 2, 1)
     if paired:
-        for begin, (keep0, keep1, send0, send1) in partials:
-            near1 = swap(send1, "dp", 2, 1)
-            near0 = swap(send0, "dp", 2, 1)
-            far = swap((keep1.astype(F32) + near1.astype(F32)).astype(BF16), "ctx", 2, 1)
-            pieces.append((begin, (keep0, near0, far)))
         grad_nope, grad_rope = query_gradient(pairs, parts, query_rope.shape[3])
         mine, other = ends
+        other = after(other, fars, FARS.get(0, ()))
         share = mine.astype(F32) + swap(other, "ctx", 2, 1).astype(F32)
     else:
         ds, kn = (jnp.concatenate(x, axis=0) for x in zip(*pairs))
-        wk, wv = (jnp.concatenate(x, axis=0) for x in zip(*(made for _, made in partials)))
+        wk, wv = (jnp.concatenate(x, axis=0) for x in zip(*partials))
         grad_nope = jnp.einsum("hkq,hkn->qhn", ds, kn, preferred_element_type=F32)[None]
         rotary = parts[0][:, latent_width:]
         grad_rope = jnp.einsum("hkq,kr->qhr", ds, rotary, preferred_element_type=F32)[None]
@@ -437,18 +499,22 @@
         grad_value_map = lax.psum_scatter(wv, ("ctx", "dp"), scatter_dimension=1, tiled=True).astype(F32)
         share = lax.psum_scatter(ends[0], "ctx", scatter_dimension=0, tiled=True).astype(F32)
     if head_size & (head_size - 1) == 0:
-        bits = 1
+        bits, n = 1, 0
         while bits < head_size:
             rounded = share.astype(BF16)
+            if paired:
+                rounded = after(rounded, fars, FARS.get(n + 1, ()))
+                rounded = after(rounded, nears, NEARS.get(n + 1, ()))
             got = swap(rounded, "head", head_size, bits | (bits >> 1) if bits >= 4 else bits)
             share = rounded.astype(F32) + got.astype(F32)
-            bits *= 2
+            bits, n = bits * 2, n + 1
     else:
         share = lax.psum(share.astype(BF16), "head").astype(F32)
     if paired:
         maps = ()
-        for begin, piece in pieces:
-            maps = finish(*piece, heads, begin, maps, min(4, piece[0].shape[0]))
+        for m, far in enumerate(fars):
+            part = [(own0, nears[n], *place) for own0, n, place, to in pieces if to == m]
+            maps = finish(part, far, heads, maps)
         grad_key_map, grad_value_map = maps
     return (
         grad_nope,

time: 52.8 us -> 44.4 us (0.84)
  waiting for transfers between devices: 19.2 us -> 11.5 us
  starting transfers between devices: 16.1 us -> 15.5 us
    ppermute x14 -> x15, waiting for transfers between devices: 19.2 us -> 11.5 us  [swap(): return lax.ppermute(x, axis, [(i, i ^ bits) for i in range(size)])]
    ppermute x14 -> x15, starting transfers between devices: 16.1 us -> 15.5 us  [swap(): return lax.ppermute(x, axis, [(i, i ^ bits) for i in range(size)])]
    pallas_call x3 -> x4, Pallas kernels: 5.86 us -> 5.59 us  [attend(): pl.pallas_call(functools.partial(attend_kernel, paired, before is None, f...]
    pallas_call x4 -> x5, Pallas kernels: 3.88 us -> 4.01 us  [the longest x2 2.1 us: finish(): pl.pallas_call(functools.partial(finish_kernel, places, not before), in_s...]
  transfers between devices with their start and end apart: 14 -> 15, of which waited for: 7 -> 6; matrix products, arithmetic and copies ran while one was open for 2% -> 3% of each run, Pallas kernels for 16% -> 25%
where the time goes in v4:
time: 44.4 us; the launch traced here: 44.3 us
  starting transfers between devices  15.5 us (35%)
  Pallas kernels  15.2 us (34%)
  waiting for transfers between devices  11.5 us (26%)
  other arithmetic  1.26 us (3%)
  between operations  0.8 us (2%)
    ppermute x15, starting transfers between devices, swap(): return lax.ppermute(x, axis, [(i, i ^ bits) for i in range(size)])  15.5 us
    ppermute x15, waiting for transfers between devices, swap(): return lax.ppermute(x, axis, [(i, i ^ bits) for i in range(size)])  11.5 us
    pallas_call x4, Pallas kernels, attend(): pl.pallas_call(functools.partial(attend_kernel, paired, before is None, f...  5.59 us
    pallas_call x1, Pallas kernels, prepare(): pl.pallas_call(functools.partial(prepare_kernel, parts, page_rows), in_sp...  3.71 us
    pallas_call x2, Pallas kernels, finish(): pl.pallas_call(functools.partial(finish_kernel, places, not before), in_s...  2.1 us
    pallas_call x1, Pallas kernels, query_gradient(): pl.pallas_call(functools.partial(query_kernel, counts, len(parts)), out_s...  1.92 us
    pallas_call x3, Pallas kernels, weight_partials(): pl.pallas_call(functools.partial(weights_kernel, True, len(parts), counts...  1.91 us
  transfers between devices with their start and end apart: 15, of which 6 were waited for; matrix products, arithmetic and copies ran while one was open for 3% of the time, Pallas kernels for 25%

profile of v4, /device:TPU:0, one launch (start us, length us, event | category | flops | bytes accessed | tf_op | source)
XLA Modules:
  0.0 44.3 jit_solution(3348031985731177812)
XLA Ops:
  0.6 3.0 %collective-permute-start = (bf16[128,576]{1,0:T(8,128)(2,1)}, bf16[128,576]{1,0:T(8,128)(2,1)S(1)}, u32[]{:S(2)}, u32[]{:S(2)}) collective-permute-start(bf16[128,576]{1,0:T(8,128)(2,1)} %bitcast.15), channel_id=1, source_target_pairs={{0,2},{2,0},{1,3},{3,1},{4,6},{6,4},{5,7},{7,5},{8,10},{10,8},{9,1... | collective-permute-start | bytes 442376 | tf_op jit(solution)/shard_map/ppermute | solution.py:394
  3.7 3.7 %prepare.1 = (bf16[16,192,128]{2,1,0:T(8,128)(2,1)S(1)}, bf16[16,128,128]{2,1,0:T(8,128)(2,1)S(1)}, bf16[16,128,512]{2,1,0:T(8,128)(2,1)S(1)}, bf16[16,512,128]{...) custom-call(bf16[128,16,128]{2,1,0:T(8,128)(2,1)} %bitcast.11, ...), custom_call_target="tpu_custom_call" | custom-call | flops 600000000 | bytes 12000000 | tf_op jit(solution)/shard_map/prepare/pallas_call | solution.py:102
  7.4 0.7 %collective-permute-done.rest_1_.refs_1_.rest_3_ = bf16[128,576]{1,0:T(8,128)(2,1)S(1)} collective-permute-done((bf16[128,576]{1,0:T(8,128)(2,1)}, bf16[128,576]{1,0:T(8,128)(2,1)S(1)}, u32[]{:S(2)}, u32[]{:S(2)}) %collective-permute-start) | collective-permute-done | bytes 147488 | tf_op jit(solution)/shard_map/ppermute | solution.py:394
  8.1 1.7 %attend.4 = (bf16[4,256,128]{2,1,0:T(8,128)(2,1)S(1)}, bf16[4,256,128]{2,1,0:T(8,128)(2,1)S(1)}, bf16[4,2,128,128]{3,2,1,0:T(8,128)(2,1)S(1)}, bf16[4,2,128,128]...) custom-call(bf16[16,192,128]{2,1,0:T(8,128)(2,1)S(1)} %get-tuple-ele, ...), custom_call_target="tpu_custom_call" | custom-call | flops 1600000000 | bytes 2000000 | tf_op jit(solution)/shard_map/attend/pallas_call | solution.py:267
  9.9 1.3 %attend.5 = (bf16[4,256,128]{2,1,0:T(8,128)(2,1)S(1)}, bf16[4,256,128]{2,1,0:T(8,128)(2,1)S(1)}, bf16[256,512]{1,0:T(8,128)(2,1)S(1)}, f32[256,576]{1,0:T(8,128)S(1)}) custom-call(bf16[16,192,128]{2,1,0:T(8,128)(2,1)S(1)} %get-tuple-element.62.qt_ref, bf16[16,128,128]{2,1,0:T(8,128)(2,1)S(1)} %get-tuple-element.63.go_ref, ...), custom_call_target="tpu_custom_call" | custom-call | flops 1200000000 | bytes 2000000 | tf_op jit(solution)/shard_map/attend/pallas_call | solution.py:267
  11.2 1.3 %attend.6 = (bf16[4,256,128]{2,1,0:T(8,128)(2,1)S(1)}, bf16[4,256,128]{2,1,0:T(8,128)(2,1)S(1)}, bf16[256,512]{1,0:T(8,128)(2,1)S(1)}, f32[256,576]{1,0:T(8,128)S(1)}) custom-call(bf16[16,192,128]{2,1,0:T(8,128)(2,1)S(1)} %get-tuple-element.62.qt_ref, bf16[16,128,128]{2,1,0:T(8,128)(2,1)S(1)} %get-tuple-element.63.go_ref, ...), custom_call_target="tpu_custom_call" | custom-call | flops 1200000000 | bytes 2000000 | tf_op jit(solution)/shard_map/attend/pallas_call | solution.py:267
  12.5 0.1 add_convert_fusion.3
  12.6 1.3 %attend.7 = (bf16[4,256,128]{2,1,0:T(8,128)(2,1)S(1)}, bf16[4,256,128]{2,1,0:T(8,128)(2,1)S(1)}, bf16[256,512]{1,0:T(8,128)(2,1)S(1)}, bf16[128,576]{1,0:T(8,128)(2,1)S(1)}, bf16[128,576]{1,0:T(8,128)(2,1)S(1)}) custom-call(bf16[16,192,128]{2,1,0:T(8,128)(2,1)S(1)} %get-tuple-element.62.qt_ref, bf16[16,128,128]{2,1,0:T(8,128)(2,1)S(1)} %get-tuple-element.63.go_ref, ...), custom_call_target="tpu_custom_call" | custom-call | flops 1200000000 | bytes 2000000 | tf_op jit(solution)/shard_map/attend/pallas_call | solution.py:267
  13.9 1.8 %collective-permute-start.2 = (bf16[128,576]{1,0:T(8,128)(2,1)S(1)}, bf16[128,576]{1,0:T(8,128)(2,1)S(1)}, u32[]{:S(2)}, u32[]{:S(2)}) collective-permute-start(bf16[128,576]{1,0:T(8,128)(2,1)S(1)} %get-tuple-element.90), channel_id=1, source_target_pairs={{0,2},{2,0},{1,3},{3,1},{4,6},{6,4},{5,7},{7,5},{8,10},{10,8},{9,1... | collective-permute-start | bytes 442376 | tf_op jit(solution)/shard_map/ppermute | solution.py:394
  15.7 0.3 collective-permute-start.4
  15.9 0.6 %weight_partials.5 = (bf16[4,2,128,128]{3,2,1,0:T(8,128)(2,1)S(1)}, bf16[4,2,128,128]{3,2,1,0:T(8,128)(2,1)S(1)}, bf16[4,2,128,128]{3,2,1,0:T(8,128)(2,1)S(1)}, bf16[4,2,128,128]{3,2,1,0:T(8,128)(2,1)S(1)}) custom-call(bf16[16,192,128]{2,1,0:T(8,128)(2,1)S(1)} %get-tuple-element.62.qt_ref, bf16[4,256,128]{2,1,0:T(8,128)(2,1)S(1)} %get-tuple-element.81.refs_8_.rest_0_, ...), custom_call_target="tpu_custom_call" | custom-call | flops 400000000 | bytes 1600000 | tf_op jit(solution)/shard_map/weight_partials/pallas_call | solution.py:298
  16.7 0.6 %weight_partials.4 = (bf16[4,2,128,128]{3,2,1,0:T(8,128)(2,1)S(1)}, bf16[4,2,128,128]{3,2,1,0:T(8,128)(2,1)S(1)}, bf16[4,2,128,128]{3,2,1,0:T(8,128)(2,1)S(1)}, bf16[4,2,128,128]{3,2,1,0:T(8,128)(2,1)S(1)}) custom-call(bf16[16,192,128]{2,1,0:T(8,128)(2,1)S(1)} %get-tuple-element.62.qt_ref, bf16[4,256,128]{2,1,0:T(8,128)(2,1)S(1)} %get-tuple-element.97.refs_6_.rest_0_, ...), custom_call_target="tpu_custom_call" | custom-call | flops 400000000 | bytes 1600000 | tf_op jit(solution)/shard_map/weight_partials/pallas_call | solution.py:298
  17.3 0.6 %collective-permute-start.8 = (bf16[4,2,128,128]{3,2,1,0:T(8,128)(2,1)S(1)}, bf16[4,2,128,128]{3,2,1,0:T(8,128)(2,1)S(1)}, u32[]{:S(2)}, u32[]{:S(2)}) collective-permute-start(bf16[4,2,128,128]{3,2,1,0:T(8,128)(2,1)S(1)} %get-tuple-element.100), channel_id=1, source_target_pairs={{0,1},{1,0},{2,3},{3,2},{4,5},{5,4},{6,7},{7,6},{8,9},{9,8},{10,11... | collective-permute-start | bytes 786440 | tf_op jit(solution)/shard_map/ppermute | solution.py:394
  17.9 0.6 %weight_partials.3 = (bf16[4,2,128,128]{3,2,1,0:T(8,128)(2,1)S(1)}, bf16[4,2,128,128]{3,2,1,0:T(8,128)(2,1)S(1)}, bf16[4,2,128,128]{3,2,1,0:T(8,128)(2,1)S(1)}, bf16[4,2,128,128]{3,2,1,0:T(8,128)(2,1)S(1)}) custom-call(bf16[16,192,128]{2,1,0:T(8,128)(2,1)S(1)} %get-tuple-element.62.qt_ref, bf16[4,256,128]{2,1,0:T(8,128)(2,1)S(1)} %get-tuple-element.93.refs_4_.rest_0_, ...), custom_call_target="tpu_custom_call" | custom-call | flops 400000000 | bytes 1600000 | tf_op jit(solution)/shard_map/weight_partials/pallas_call | solution.py:298
  18.5 0.1 collective-permute-start.7
  18.6 2.3 %collective-permute-done.2 = bf16[128,576]{1,0:T(8,128)(2,1)S(1)} collective-permute-done((bf16[128,576]{1,0:T(8,128)(2,1)S(1)}, bf16[128,576]{1,0:T(8,128)(2,1)S(1)}, u32[]{:S(2)}, u32[]{:S(2)}) %collective-permute-start.2) | collective-permute-done | bytes 147488 | tf_op jit(solution)/shard_map/ppermute | solution.py:394
  21.0 1.8 %collective-permute-start.3 = (bf16[128,576]{1,0:T(8,128)(2,1)S(1)}, bf16[128,576]{1,0:T(8,128)(2,1)S(1)}, u32[]{:S(2)}, u32[]{:S(2)}) collective-permute-start(bf16[128,576]{1,0:T(8,128)(2,1)S(1)} %add_convert_fusion.6), channel_id=1, source_target_pairs={{0,4},{4,0},{8,12},{12,8},{16,20},{20,16},{24,28},{28,24},{1,5},{5... | collective-permute-start | bytes 442376 | tf_op jit(solution)/shard_map/ppermute | solution.py:394
  22.8 0.1 add_convert_fusion.1
  22.9 0.1 add_convert_fusion.2
  23.0 0.1 pad_maximum_fusion
  23.1 1.6 %collective-permute-start.10 = (bf16[12,2,128,128]{3,2,1,0:T(8,128)(2,1)S(1)}, bf16[12,2,128,128]{3,2,1,0:T(8,128)(2,1)S(1)}, u32[]{:S(2)}, u32[]{:S(2)}) collective-permute-start(bf16[12,2,128,128]{3,2,1,0:T(8,128)(2,1)S(1)} %pad_maximum_fusion), channel_id=1, source_target_pairs={{0,2},{2,0},{1,3},{3,1},{4,6},{6,4},{5,7},{7,5},{8,10},{10,8},{9,1... | collective-permute-start | bytes 2359304 | tf_op jit(solution)/shard_map/ppermute | solution.py:394
  24.7 1.8 %collective-permute-done.3 = bf16[128,576]{1,0:T(8,128)(2,1)S(1)} collective-permute-done((bf16[128,576]{1,0:T(8,128)(2,1)S(1)}, bf16[128,576]{1,0:T(8,128)(2,1)S(1)}, u32[]{:S(2)}, u32[]{:S(2)}) %collective-permute-start.3) | collective-permute-done | bytes 147488 | tf_op jit(solution)/shard_map/ppermute | solution.py:394
  26.5 1.8 %collective-permute-start.5 = (bf16[128,576]{1,0:T(8,128)(2,1)S(1)}, bf16[128,576]{1,0:T(8,128)(2,1)S(1)}, u32[]{:S(2)}, u32[]{:S(2)}) collective-permute-start(bf16[128,576]{1,0:T(8,128)(2,1)S(1)} %add_convert_fusion.5), channel_id=1, source_target_pairs={{0,8},{4,12},{8,0},{12,4},{16,24},{20,28},{24,16},{28,20},{1,9},{5... | collective-permute-start | bytes 442376 | tf_op jit(solution)/shard_map/ppermute | solution.py:394
  28.4 3.6 %collective-permute-done.5 = bf16[128,576]{1,0:T(8,128)(2,1)S(1)} collective-permute-done((bf16[128,576]{1,0:T(8,128)(2,1)S(1)}, bf16[128,576]{1,0:T(8,128)(2,1)S(1)}, u32[]{:S(2)}, u32[]{:S(2)}) %collective-permute-start.5) | collective-permute-done | bytes 147488 | tf_op jit(solution)/shard_map/ppermute | solution.py:394
  32.1 3.8 %collective-permute-start.6 = (bf16[128,576]{1,0:T(8,128)(2,1)S(1)}, bf16[128,576]{1,0:T(8,128)(2,1)S(1)}, u32[]{:S(2)}, u32[]{:S(2)}) collective-permute-start(bf16[128,576]{1,0:T(8,128)(2,1)S(1)} %add_convert_fusion.4), channel_id=1, source_target_pairs={{0,24},{4,28},{8,16},{12,20},{16,8},{20,12},{24,0},{28,4},{1,25},{... | collective-permute-start | bytes 442376 | tf_op jit(solution)/shard_map/ppermute | solution.py:394
  35.9 0.5 %collective-permute-start.12 = (bf16[4,2,128,128]{3,2,1,0:T(8,128)(2,1)S(1)}, bf16[4,2,128,128]{3,2,1,0:T(8,128)(2,1)S(1)}, u32[]{:S(2)}, u32[]{:S(2)}) collective-permute-start(bf16[4,2,128,128]{3,2,1,0:T(8,128)(2,1)S(1)} %get-tuple-element.107), channel_id=1, source_target_pairs={{0,1},{1,0},{2,3},{3,2},{4,5},{5,4},{6,7},{7,6},{8,9},{9,8},{10,11... | collective-permute-start | bytes 786440 | tf_op jit(solution)/shard_map/ppermute | solution.py:394
  36.4 1.9 %query_gradient.1 = (f32[2048,128]{1,0:T(8,128)}, f32[16,64,128]{2,1,0:T(8,128)}) custom-call(bf16[128,576]{1,0:T(8,128)(2,1)S(1)} %get-tuple-element.61.rest_0_.refs_0_.rest_2_, bf16[128,576]{1,0:T(8,128)(2,1)S(1)} %collective-permute-done.rest_1_.refs_1_.rest_3_, bf16[4,256,128]{2,1,0:T(8,128)(2,1)S(1)} %get-tuple-element.69.refs_2_, ...), custom_call_target="tpu_custom_call" | custom-call | flops 1000000000 | bytes 5000000 | tf_op jit(solution)/shard_map/query_gradient/pallas_call | solution.py:330
  38.3 0.8 %finish.2 = (f32[16,32,512]{2,1,0:T(8,128)}, f32[16,128,128]{2,1,0:T(8,128)}) custom-call(bf16[4,2,128,128]{3,2,1,0:T(8,128)(2,1)S(1)} %collective-permute-done.4.far_ref, bf16[4,2,128,128]{3,2,1,0:T(8,128)(2,1)S(1)} %get-tuple-element.111.rest_0_, bf16[4,2,128,128]{3,2,1,0:T(8,128)(2,1)S(1)} %collective-permute-done.14.rest_1_), custom_call_target="tpu_custom_call" | custom-call | flops 1000000 | bytes 1200000 | tf_op jit(solution)/shard_map/finish/pallas_call | solution.py:373
  39.2 0.2 collective-permute-done.6
  39.3 0.8 %convert_add_fusion = f32[128,576]{1,0:T(8,128)} fusion(bf16[128,576]{1,0:T(8,128)(2,1)S(1)} %collective-permute-done.6, bf16[128,576]{1,0:T(8,128)(2,1)S(1)} %add_convert_fusion.4), kind=kLoop, calls=%fused_computation.5 | loop fusion | flops 221184 | bytes 589824 | tf_op jit(solution)/shard_map/add | solution.py:509
  40.1 2.9 %collective-permute-done.10.far_ref = bf16[12,2,128,128]{3,2,1,0:T(8,128)(2,1)S(1)} collective-permute-done((bf16[12,2,128,128]{3,2,1,0:T(8,128)(2,1)S(1)}, bf16[12,2,128,128]{3,2,1,0:T(8,128)(2,1)S(1)}, u32[]{:S(2)}, u32[]{:S(2)}) %collective-permute-start.10) | collective-permute-done | bytes 786464 | tf_op jit(solution)/shard_map/ppermute | solution.py:394
  43.0 1.3 %finish.3 = (f32[16,32,512]{2,1,0:T(8,128)}, f32[16,128,128]{2,1,0:T(8,128)}) custom-call(bf16[12,2,128,128]{3,2,1,0:T(8,128)(2,1)S(1)} %collective-permute-done.10.far_ref, bf16[4,2,128,128]{3,2,1,0:T(8,128)(2,1)S(1)} %get-tuple-element.104.rest_0_, ...), custom_call_target="tpu_custom_call", output_to_operand_aliasing={{0}: (7, {}), {1}: (8, {})} | custom-call | flops 1000000 | bytes 3600000 | tf_op jit(solution)/shard_map/finish/pallas_call | solution.py:373
  (18 shorter events, 0.4 us)
Async XLA Ops:
  0.6 7.4 %collective-permute-start = (bf16[128,576]{1,0:T(8,128)(2,1)}, bf16[128,576]{1,0:T(8,128)(2,1)S(1)}, u32[]{:S(2)}, u32[]{:S(2)}) collective-permute-start(bf16[128,576]{1,0:T(8,128)(2,1)} %bitcast.15), channel_id=1, source_target_pairs={{0,2},{2,0},{1,3},{3,1},{4,6},{6,4},{5,7},{7,5},{8,10},{10,8},{9,1... | collective-permute-start | bytes 442376 | tf_op jit(solution)/shard_map/ppermute | solution.py:394
  9.8 2.7 %collective-permute-start.1 = (bf16[4,2,128,128]{3,2,1,0:T(8,128)(2,1)S(1)}, bf16[4,2,128,128]{3,2,1,0:T(8,128)(2,1)S(1)}, u32[]{:S(2)}, u32[]{:S(2)}) collective-permute-start(bf16[4,2,128,128]{3,2,1,0:T(8,128)(2,1)S(1)} %get-tuple-element.79), channel_id=1, source_target_pairs={{0,1},{1,0},{2,3},{3,2},{4,5},{5,4},{6,7},{7,6},{8,9},{9,8},{10,11... | collective-permute-start | bytes 786440 | tf_op jit(solution)/shard_map/ppermute | solution.py:394
  13.9 7.1 %collective-permute-start.2 = (bf16[128,576]{1,0:T(8,128)(2,1)S(1)}, bf16[128,576]{1,0:T(8,128)(2,1)S(1)}, u32[]{:S(2)}, u32[]{:S(2)}) collective-permute-start(bf16[128,576]{1,0:T(8,128)(2,1)S(1)} %get-tuple-element.90), channel_id=1, source_target_pairs={{0,2},{2,0},{1,3},{3,1},{4,6},{6,4},{5,7},{7,5},{8,10},{10,8},{9,1... | collective-permute-start | bytes 442376 | tf_op jit(solution)/shard_map/ppermute | solution.py:394
  15.7 10.9 %collective-permute-start.4 = (bf16[4,2,128,128]{3,2,1,0:T(8,128)(2,1)S(1)}, bf16[4,2,128,128]{3,2,1,0:T(8,128)(2,1)S(1)}, u32[]{:S(2)}, u32[]{:S(2)}) collective-permute-start(bf16[4,2,128,128]{3,2,1,0:T(8,128)(2,1)S(1)} %add_convert_fusion.3), channel_id=1, source_target_pairs={{0,2},{2,0},{1,3},{3,1},{4,6},{6,4},{5,7},{7,5},{8,10},{10,8},{9,1... | collective-permute-start | bytes 786440 | tf_op jit(solution)/shard_map/ppermute | solution.py:394
  16.6 6.1 %collective-permute-start.9 = (bf16[4,2,128,128]{3,2,1,0:T(8,128)(2,1)S(1)}, bf16[4,2,128,128]{3,2,1,0:T(8,128)(2,1)S(1)}, u32[]{:S(2)}, u32[]{:S(2)}) collective-permute-start(bf16[4,2,128,128]{3,2,1,0:T(8,128)(2,1)S(1)} %get-tuple-element.103), channel_id=1, source_target_pairs={{0,1},{1,0},{2,3},{3,2},{4,5},{5,4},{6,7},{7,6},{8,9},{9,8},{10,11... | collective-permute-start | bytes 786440 | tf_op jit(solution)/shard_map/ppermute | solution.py:394
  17.3 5.5 %collective-permute-start.8 = (bf16[4,2,128,128]{3,2,1,0:T(8,128)(2,1)S(1)}, bf16[4,2,128,128]{3,2,1,0:T(8,128)(2,1)S(1)}, u32[]{:S(2)}, u32[]{:S(2)}) collective-permute-start(bf16[4,2,128,128]{3,2,1,0:T(8,128)(2,1)S(1)} %get-tuple-element.100), channel_id=1, source_target_pairs={{0,1},{1,0},{2,3},{3,2},{4,5},{5,4},{6,7},{7,6},{8,9},{9,8},{10,11... | collective-permute-start | bytes 786440 | tf_op jit(solution)/shard_map/ppermute | solution.py:394
  18.5 4.4 %collective-permute-start.7 = (bf16[4,2,128,128]{3,2,1,0:T(8,128)(2,1)S(1)}, bf16[4,2,128,128]{3,2,1,0:T(8,128)(2,1)S(1)}, u32[]{:S(2)}, u32[]{:S(2)}) collective-permute-start(bf16[4,2,128,128]{3,2,1,0:T(8,128)(2,1)S(1)} %get-tuple-element.96), channel_id=1, source_target_pairs={{0,1},{1,0},{2,3},{3,2},{4,5},{5,4},{6,7},{7,6},{8,9},{9,8},{10,11... | collective-permute-start | bytes 786440 | tf_op jit(solution)/shard_map/ppermute | solution.py:394
  21.0 5.5 %collective-permute-start.3 = (bf16[128,576]{1,0:T(8,128)(2,1)S(1)}, bf16[128,576]{1,0:T(8,128)(2,1)S(1)}, u32[]{:S(2)}, u32[]{:S(2)}) collective-permute-start(bf16[128,576]{1,0:T(8,128)(2,1)S(1)} %add_convert_fusion.6), channel_id=1, source_target_pairs={{0,4},{4,0},{8,12},{12,8},{16,20},{20,16},{24,28},{28,24},{1,5},{5... | collective-permute-start | bytes 442376 | tf_op jit(solution)/shard_map/ppermute | solution.py:394
  23.1 19.9 %collective-permute-start.10 = (bf16[12,2,128,128]{3,2,1,0:T(8,128)(2,1)S(1)}, bf16[12,2,128,128]{3,2,1,0:T(8,128)(2,1)S(1)}, u32[]{:S(2)}, u32[]{:S(2)}) collective-permute-start(bf16[12,2,128,128]{3,2,1,0:T(8,128)(2,1)S(1)} %pad_maximum_fusion), channel_id=1, source_target_pairs={{0,2},{2,0},{1,3},{3,1},{4,6},{6,4},{5,7},{7,5},{8,10},{10,8},{9,1... | collective-permute-start | bytes 2359304 | tf_op jit(solution)/shard_map/ppermute | solution.py:394
  26.5 5.5 %collective-permute-start.5 = (bf16[128,576]{1,0:T(8,128)(2,1)S(1)}, bf16[128,576]{1,0:T(8,128)(2,1)S(1)}, u32[]{:S(2)}, u32[]{:S(2)}) collective-permute-start(bf16[128,576]{1,0:T(8,128)(2,1)S(1)} %add_convert_fusion.5), channel_id=1, source_target_pairs={{0,8},{4,12},{8,0},{12,4},{16,24},{20,28},{24,16},{28,20},{1,9},{5... | collective-permute-start | bytes 442376 | tf_op jit(solution)/shard_map/ppermute | solution.py:394
  28.4 8.0 %collective-permute-start.14 = (bf16[4,2,128,128]{3,2,1,0:T(8,128)(2,1)S(1)}, bf16[4,2,128,128]{3,2,1,0:T(8,128)(2,1)S(1)}, u32[]{:S(2)}, u32[]{:S(2)}) collective-permute-start(bf16[4,2,128,128]{3,2,1,0:T(8,128)(2,1)S(1)} %get-tuple-element.112), channel_id=1, source_target_pairs={{0,1},{1,0},{2,3},{3,2},{4,5},{5,4},{6,7},{7,6},{8,9},{9,8},{10,11... | collective-permute-start | bytes 786440 | tf_op jit(solution)/shard_map/ppermute | solution.py:394
  32.1 7.3 %collective-permute-start.6 = (bf16[128,576]{1,0:T(8,128)(2,1)S(1)}, bf16[128,576]{1,0:T(8,128)(2,1)S(1)}, u32[]{:S(2)}, u32[]{:S(2)}) collective-permute-start(bf16[128,576]{1,0:T(8,128)(2,1)S(1)} %add_convert_fusion.4), channel_id=1, source_target_pairs={{0,24},{4,28},{8,16},{12,20},{16,8},{20,12},{24,0},{28,4},{1,25},{... | collective-permute-start | bytes 442376 | tf_op jit(solution)/shard_map/ppermute | solution.py:394
  35.9 4.2 %collective-permute-start.13 = (bf16[4,2,128,128]{3,2,1,0:T(8,128)(2,1)S(1)}, bf16[4,2,128,128]{3,2,1,0:T(8,128)(2,1)S(1)}, u32[]{:S(2)}, u32[]{:S(2)}) collective-permute-start(bf16[4,2,128,128]{3,2,1,0:T(8,128)(2,1)S(1)} %get-tuple-element.109), channel_id=1, source_target_pairs={{0,1},{1,0},{2,3},{3,2},{4,5},{5,4},{6,7},{7,6},{8,9},{9,8},{10,11... | collective-permute-start | bytes 786440 | tf_op jit(solution)/shard_map/ppermute | solution.py:394
  35.9 4.2 %collective-permute-start.12 = (bf16[4,2,128,128]{3,2,1,0:T(8,128)(2,1)S(1)}, bf16[4,2,128,128]{3,2,1,0:T(8,128)(2,1)S(1)}, u32[]{:S(2)}, u32[]{:S(2)}) collective-permute-start(bf16[4,2,128,128]{3,2,1,0:T(8,128)(2,1)S(1)} %get-tuple-element.107), channel_id=1, source_target_pairs={{0,1},{1,0},{2,3},{3,2},{4,5},{5,4},{6,7},{7,6},{8,9},{9,8},{10,11... | collective-permute-start | bytes 786440 | tf_op jit(solution)/shard_map/ppermute | solution.py:394
  36.4 3.7 %collective-permute-start.11 = (bf16[4,2,128,128]{3,2,1,0:T(8,128)(2,1)S(1)}, bf16[4,2,128,128]{3,2,1,0:T(8,128)(2,1)S(1)}, u32[]{:S(2)}, u32[]{:S(2)}) collective-permute-start(bf16[4,2,128,128]{3,2,1,0:T(8,128)(2,1)S(1)} %get-tuple-element.105), channel_id=1, source_target_pairs={{0,1},{1,0},{2,3},{3,2},{4,5},{5,4},{6,7},{7,6},{8,9},{9,8},{10,11... | collective-permute-start | bytes 786440 | tf_op jit(solution)/shard_map/ppermute | solution.py:394

commit v5 on v4

--- a/solution.py
+++ b/solution.py
@@ -12,7 +12,7 @@
 F32 = jnp.float32
 BF16 = jnp.bfloat16
 MIB = 1024 * 1024
-PLAN = ((4, True), (4, False), (4, False), (4, False))
+PLAN = ((4, True), (4, False), (8, False))
 CUTS = ((4,), (4,), (4,), (4,))
 GROUPS = ((0,), (1,), (2,))
 WAITS = (None, None, None, None)
@@ -20,6 +20,7 @@
 NEARS = {}
 FRONT = 1
 WEIGHT_COST = 100_000_000
+ATTEND_COST = 300_000_000
 JOIN = (2, 3)
 LATE = True
 
@@ -180,7 +181,7 @@
     if not first:
         total = before_ref[...]
         total_latent, total_rotary = total[:, :latent_width], total[:, latent_width:]
-    for g in range(0, count, group):
+    def front(g):
         at = begin + g
         heads = range(at, at + group)
         ku = ku_ref[at:at + group].reshape(group * nope_width, latent_width)
@@ -198,6 +199,13 @@
                 dot_nn(jnp.concatenate([kn_h, rotary], axis=1), qt_ref[h]),
                 dot_nt(values[:, i * value_width:(i + 1) * value_width], go_ref[h]),
             ))
+        return at, heads, ku, vu, raw
+
+    ahead = front(0)
+    for g in range(0, count, group):
+        at, heads, ku, vu, raw = ahead
+        if g + group < count:
+            ahead = front(g + group)
         soft = []
         for scores, grad_probs in raw:
             scores = scores * softmax_scale + bias_ref[...]
@@ -269,22 +277,22 @@
         out_shape=shapes,
         scratch_shapes=partial_scratch(paired, group, key_count, nope_width, latent_width) if weights else [],
         compiler_params=params(14 if paired else 56),
-        cost_estimate=cost(count * (400_000_000 if weights else 300_000_000), count * 500_000),
+        cost_estimate=cost(count * (400_000_000 if weights else ATTEND_COST), count * 500_000),
         name="attend",
     )(qt, go, key_up, value_up, bias, kn_own, va_own, *parts, *([] if before is None else [before]))
 
 
-def weights_kernel(paired, parts, counts, begin, latent_width, qt_ref, *rest):
-    chunk_refs, rest = rest[:2 * len(counts)], rest[2 * len(counts):]
+def weights_kernel(paired, parts, spans, begin, latent_width, qt_ref, *rest):
+    chunk_refs, rest = rest[:2 * len(spans)], rest[2 * len(spans):]
     part_refs, outs, vt_ref, bp_ref = rest[:parts], rest[parts:-2], rest[-2], rest[-1]
     latent = jnp.concatenate([r[:, :latent_width] for r in part_refs], axis=0)
     turned_values(paired, latent, vt_ref)
     at = 0
-    for n, count in enumerate(counts):
+    for n, (first, count) in enumerate(spans):
         ds_ref, gv_ref = chunk_refs[2 * n], chunk_refs[2 * n + 1]
-        value_width = gv_ref.shape[1] // count
+        value_width = gv_ref.shape[1] // ds_ref.shape[0]
         group = min(4, count)
-        for g in range(0, count, group):
+        for g in range(first, first + count, group):
             weight_group(
                 paired, at, [qt_ref[begin + at + i, :value_width] for i in range(group)], [ds_ref[g + i] for i in range(group)],
                 gv_ref[:, g * value_width:(g + group) * value_width], latent, vt_ref, bp_ref, outs,
@@ -292,11 +300,10 @@
             at += group
 
 
-def weight_partials(begin, qt, chunks, parts, nope_width, latent_width):
-    counts = [ds.shape[0] for ds, _ in chunks]
-    count, key_count = sum(counts), chunks[0][0].shape[1]
+def weight_partials(begin, qt, chunks, spans, parts, nope_width, latent_width):
+    count, key_count = sum(n for _, n in spans), chunks[0][0].shape[1]
     return pl.pallas_call(
-        functools.partial(weights_kernel, True, len(parts), counts, begin, latent_width),
+        functools.partial(weights_kernel, True, len(parts), spans, begin, latent_width),
         out_shape=partial_shapes(True, count, nope_width, latent_width, nope_width),
         scratch_shapes=partial_scratch(True, 4, key_count, nope_width, latent_width),
         compiler_params=params(14),
@@ -467,7 +474,8 @@
         pairs.append((results[0], results[1]))
         ends = results[-len(parts):] if final else results[-1:]
         if not weights:
-            later.append((begin, (results[0], results[2])))
+            step = math.gcd(count, heads // 4)
+            later += [(begin + at, final, (results[0], results[2]), (at, step)) for at in range(0, count, step)]
         elif paired:
             send(begin, results[2:6])
         else:
@@ -475,10 +483,11 @@
         total = ends[0]
         begin += count
     for group in GROUPS if paired else ():
-        chunks = [later[n][1] for n in group]
-        if LATE and group[-1] != len(later) - 1:
+        chunks = [later[n][2] for n in group]
+        if LATE and not later[group[-1]][1]:
             ends[-1], chunks[-1] = lax.optimization_barrier((ends[-1], chunks[-1]))
-        send(later[group[0]][0], weight_partials(later[group[0]][0], qt, chunks, parts, nope_width, latent_width))
+        spans = [later[n][3] for n in group]
+        send(later[group[0]][0], weight_partials(later[group[0]][0], qt, chunks, spans, parts, nope_width, latent_width))
     fars = [swap(x, "ctx", 2, 1) for x in fars]
     for n, send0 in enumerate(nears):
         if WAITS[n] is not None:

time: 44.4 us -> 44.1 us (level)
    pallas_call x4 -> x3, Pallas kernels: 5.59 us -> 5.33 us  [attend(): pl.pallas_call(functools.partial(attend_kernel, paired, before is None, f...]
  transfers between devices with their start and end apart: 15 -> 15, of which waited for: 6 -> 8; matrix products, arithmetic and copies ran while one was open for 3% -> 3% of each run, Pallas kernels for 25% -> 22%
where the time goes in v5:
time: 44.1 us; the launch traced here: 44 us
  starting transfers between devices  15.5 us (35%)
  Pallas kernels  15 us (34%)
  waiting for transfers between devices  11.5 us (26%)
  other arithmetic  1.26 us (3%)
  between operations  0.78 us (2%)
    ppermute x15, starting transfers between devices, swap(): return lax.ppermute(x, axis, [(i, i ^ bits) for i in range(size)])  15.5 us
    ppermute x15, waiting for transfers between devices, swap(): return lax.ppermute(x, axis, [(i, i ^ bits) for i in range(size)])  11.5 us
    pallas_call x3, Pallas kernels, attend(): pl.pallas_call(functools.partial(attend_kernel, paired, before is None, f...  5.33 us
    pallas_call x1, Pallas kernels, prepare(): pl.pallas_call(functools.partial(prepare_kernel, parts, page_rows), in_sp...  3.71 us
    pallas_call x2, Pallas kernels, finish(): pl.pallas_call(functools.partial(finish_kernel, places, not before), in_s...  2.1 us
    pallas_call x1, Pallas kernels, query_gradient(): pl.pallas_call(functools.partial(query_kernel, counts, len(parts)), out_s...  1.92 us
    pallas_call x3, Pallas kernels, weight_partials(): pl.pallas_call(functools.partial(weights_kernel, True, len(parts), spans,...  1.91 us
  transfers between devices with their start and end apart: 15, of which 8 were waited for; matrix products, arithmetic and copies ran while one was open for 3% of the time, Pallas kernels for 22%

profile of v5, /device:TPU:0, one launch (start us, length us, event | category | flops | bytes accessed | tf_op | source)
XLA Modules:
  0.0 44.0 jit_solution(4642758082161641275)
XLA Ops:
  0.6 3.0 %collective-permute-start = (bf16[128,576]{1,0:T(8,128)(2,1)}, bf16[128,576]{1,0:T(8,128)(2,1)S(1)}, u32[]{:S(2)}, u32[]{:S(2)}) collective-permute-start(bf16[128,576]{1,0:T(8,128)(2,1)} %bitcast.15), channel_id=1, source_target_pairs={{0,2},{2,0},{1,3},{3,1},{4,6},{6,4},{5,7},{7,5},{8,10},{10,8},{9,1... | collective-permute-start | bytes 442376 | tf_op jit(solution)/shard_map/ppermute | solution.py:401
  3.7 3.7 %prepare.1 = (bf16[16,192,128]{2,1,0:T(8,128)(2,1)S(1)}, bf16[16,128,128]{2,1,0:T(8,128)(2,1)S(1)}, bf16[16,128,512]{2,1,0:T(8,128)(2,1)S(1)}, bf16[16,512,128]{...) custom-call(bf16[128,16,128]{2,1,0:T(8,128)(2,1)} %bitcast.11, ...), custom_call_target="tpu_custom_call" | custom-call | flops 600000000 | bytes 12000000 | tf_op jit(solution)/shard_map/prepare/pallas_call | solution.py:103
  7.4 0.7 %collective-permute-done.rest_1_.refs_1_.rest_3_ = bf16[128,576]{1,0:T(8,128)(2,1)S(1)} collective-permute-done((bf16[128,576]{1,0:T(8,128)(2,1)}, bf16[128,576]{1,0:T(8,128)(2,1)S(1)}, u32[]{:S(2)}, u32[]{:S(2)}) %collective-permute-start) | collective-permute-done | bytes 147488 | tf_op jit(solution)/shard_map/ppermute | solution.py:401
  8.1 1.7 %attend.3 = (bf16[4,256,128]{2,1,0:T(8,128)(2,1)S(1)}, bf16[4,256,128]{2,1,0:T(8,128)(2,1)S(1)}, bf16[4,2,128,128]{3,2,1,0:T(8,128)(2,1)S(1)}, bf16[4,2,128,128]...) custom-call(bf16[16,192,128]{2,1,0:T(8,128)(2,1)S(1)} %get-tuple-ele, ...), custom_call_target="tpu_custom_call" | custom-call | flops 1600000000 | bytes 2000000 | tf_op jit(solution)/shard_map/attend/pallas_call | solution.py:275
  9.9 1.3 %attend.4 = (bf16[4,256,128]{2,1,0:T(8,128)(2,1)S(1)}, bf16[4,256,128]{2,1,0:T(8,128)(2,1)S(1)}, bf16[256,512]{1,0:T(8,128)(2,1)S(1)}, f32[256,576]{1,0:T(8,128)S(1)}) custom-call(bf16[16,192,128]{2,1,0:T(8,128)(2,1)S(1)} %get-tuple-element.55.qt_ref, bf16[16,128,128]{2,1,0:T(8,128)(2,1)S(1)} %get-tuple-element.56.go_ref, ...), custom_call_target="tpu_custom_call" | custom-call | flops 1200000000 | bytes 2000000 | tf_op jit(solution)/shard_map/attend/pallas_call | solution.py:275
  11.2 0.2 collective-permute-done.1
  11.5 2.3 %attend.5 = (bf16[8,256,128]{2,1,0:T(8,128)(2,1)S(1)}, bf16[8,256,128]{2,1,0:T(8,128)(2,1)S(1)}, bf16[256,1024]{1,0:T(8,128)(2,1)S(1)}, bf16[128,576]{1,0:T(8,128)(2,1)S(1)}, bf16[128,576]{1,0:T(8,128)(2,1)S(1)}) custom-call(bf16[16,192,128]{2,1,0:T(8,128)(2,1)S(1)} %get-tuple-element.55.qt_ref, bf16[16,128,128]{2,1,0:T(8,128)(2,1)S(1)} %get-tuple-element.56.go_ref, ...), custom_call_target="tpu_custom_call" | custom-call | flops 2400000000 | bytes 4000000 | tf_op jit(solution)/shard_map/attend/pallas_call | solution.py:275
  13.8 1.8 %collective-permute-start.2 = (bf16[128,576]{1,0:T(8,128)(2,1)S(1)}, bf16[128,576]{1,0:T(8,128)(2,1)S(1)}, u32[]{:S(2)}, u32[]{:S(2)}) collective-permute-start(bf16[128,576]{1,0:T(8,128)(2,1)S(1)} %get-tuple-element.78), channel_id=1, source_target_pairs={{0,2},{2,0},{1,3},{3,1},{4,6},{6,4},{5,7},{7,5},{8,10},{10,8},{9,1... | collective-permute-start | bytes 442376 | tf_op jit(solution)/shard_map/ppermute | solution.py:401
  15.6 0.3 collective-permute-start.4
  15.9 0.6 %weight_partials.3 = (bf16[4,2,128,128]{3,2,1,0:T(8,128)(2,1)S(1)}, bf16[4,2,128,128]{3,2,1,0:T(8,128)(2,1)S(1)}, bf16[4,2,128,128]{3,2,1,0:T(8,128)(2,1)S(1)}, bf16[4,2,128,128]{3,2,1,0:T(8,128)(2,1)S(1)}) custom-call(bf16[16,192,128]{2,1,0:T(8,128)(2,1)S(1)} %get-tuple-element.55.qt_ref, bf16[4,256,128]{2,1,0:T(8,128)(2,1)S(1)} %get-tuple-element.81.refs_4_.rest_0_, ...), custom_call_target="tpu_custom_call" | custom-call | flops 400000000 | bytes 1600000 | tf_op jit(solution)/shard_map/weight_partials/pallas_call | solution.py:305
  16.6 0.6 %weight_partials.5 = (bf16[4,2,128,128]{3,2,1,0:T(8,128)(2,1)S(1)}, bf16[4,2,128,128]{3,2,1,0:T(8,128)(2,1)S(1)}, bf16[4,2,128,128]{3,2,1,0:T(8,128)(2,1)S(1)}, bf16[4,2,128,128]{3,2,1,0:T(8,128)(2,1)S(1)}) custom-call(bf16[16,192,128]{2,1,0:T(8,128)(2,1)S(1)} %get-tuple-element.55.qt_ref, bf16[8,256,128]{2,1,0:T(8,128)(2,1)S(1)} %get-tuple-element.71.refs_6_.rest_0_, ...), custom_call_target="tpu_custom_call" | custom-call | flops 400000000 | bytes 1600000 | tf_op jit(solution)/shard_map/weight_partials/pallas_call | solution.py:305
  17.3 0.6 %collective-permute-start.9 = (bf16[4,2,128,128]{3,2,1,0:T(8,128)(2,1)S(1)}, bf16[4,2,128,128]{3,2,1,0:T(8,128)(2,1)S(1)}, u32[]{:S(2)}, u32[]{:S(2)}) collective-permute-start(bf16[4,2,128,128]{3,2,1,0:T(8,128)(2,1)S(1)} %get-tuple-element.89), channel_id=1, source_target_pairs={{0,1},{1,0},{2,3},{3,2},{4,5},{5,4},{6,7},{7,6},{8,9},{9,8},{10,11... | collective-permute-start | bytes 786440 | tf_op jit(solution)/shard_map/ppermute | solution.py:401
  17.8 0.6 %weight_partials.4 = (bf16[4,2,128,128]{3,2,1,0:T(8,128)(2,1)S(1)}, bf16[4,2,128,128]{3,2,1,0:T(8,128)(2,1)S(1)}, bf16[4,2,128,128]{3,2,1,0:T(8,128)(2,1)S(1)}, bf16[4,2,128,128]{3,2,1,0:T(8,128)(2,1)S(1)}) custom-call(bf16[16,192,128]{2,1,0:T(8,128)(2,1)S(1)} %get-tuple-element.55.qt_ref, bf16[8,256,128]{2,1,0:T(8,128)(2,1)S(1)} %get-tuple-element.71.refs_6_.rest_0_, ...), custom_call_target="tpu_custom_call" | custom-call | flops 400000000 | bytes 1600000 | tf_op jit(solution)/shard_map/weight_partials/pallas_call | solution.py:305
  18.5 0.1 collective-permute-start.8
  18.6 2.3 %collective-permute-done.2 = bf16[128,576]{1,0:T(8,128)(2,1)S(1)} collective-permute-done((bf16[128,576]{1,0:T(8,128)(2,1)S(1)}, bf16[128,576]{1,0:T(8,128)(2,1)S(1)}, u32[]{:S(2)}, u32[]{:S(2)}) %collective-permute-start.2) | collective-permute-done | bytes 147488 | tf_op jit(solution)/shard_map/ppermute | solution.py:401
  20.9 1.8 %collective-permute-start.3 = (bf16[128,576]{1,0:T(8,128)(2,1)S(1)}, bf16[128,576]{1,0:T(8,128)(2,1)S(1)}, u32[]{:S(2)}, u32[]{:S(2)}) collective-permute-start(bf16[128,576]{1,0:T(8,128)(2,1)S(1)} %add_convert_fusion.6), channel_id=1, source_target_pairs={{0,4},{4,0},{8,12},{12,8},{16,20},{20,16},{24,28},{28,24},{1,5},{5... | collective-permute-start | bytes 442376 | tf_op jit(solution)/shard_map/ppermute | solution.py:401
  22.8 0.1 add_convert_fusion
  22.9 0.1 add_convert_fusion.1
  23.0 0.1 pad_maximum_fusion
  23.1 1.6 %collective-permute-start.10 = (bf16[12,2,128,128]{3,2,1,0:T(8,128)(2,1)S(1)}, bf16[12,2,128,128]{3,2,1,0:T(8,128)(2,1)S(1)}, u32[]{:S(2)}, u32[]{:S(2)}) collective-permute-start(bf16[12,2,128,128]{3,2,1,0:T(8,128)(2,1)S(1)} %pad_maximum_fusion), channel_id=1, source_target_pairs={{0,2},{2,0},{1,3},{3,1},{4,6},{6,4},{5,7},{7,5},{8,10},{10,8},{9,1... | collective-permute-start | bytes 2359304 | tf_op jit(solution)/shard_map/ppermute | solution.py:401
  24.7 1.7 %collective-permute-done.3 = bf16[128,576]{1,0:T(8,128)(2,1)S(1)} collective-permute-done((bf16[128,576]{1,0:T(8,128)(2,1)S(1)}, bf16[128,576]{1,0:T(8,128)(2,1)S(1)}, u32[]{:S(2)}, u32[]{:S(2)}) %collective-permute-start.3) | collective-permute-done | bytes 147488 | tf_op jit(solution)/shard_map/ppermute | solution.py:401
  26.4 0.1 collective-permute-done.4.far_ref
  26.5 1.8 %collective-permute-start.5 = (bf16[128,576]{1,0:T(8,128)(2,1)S(1)}, bf16[128,576]{1,0:T(8,128)(2,1)S(1)}, u32[]{:S(2)}, u32[]{:S(2)}) collective-permute-start(bf16[128,576]{1,0:T(8,128)(2,1)S(1)} %add_convert_fusion.5), channel_id=1, source_target_pairs={{0,8},{4,12},{8,0},{12,4},{16,24},{20,28},{24,16},{28,20},{1,9},{5... | collective-permute-start | bytes 442376 | tf_op jit(solution)/shard_map/ppermute | solution.py:401
  28.3 3.5 %collective-permute-done.5 = bf16[128,576]{1,0:T(8,128)(2,1)S(1)} collective-permute-done((bf16[128,576]{1,0:T(8,128)(2,1)S(1)}, bf16[128,576]{1,0:T(8,128)(2,1)S(1)}, u32[]{:S(2)}, u32[]{:S(2)}) %collective-permute-start.5) | collective-permute-done | bytes 147488 | tf_op jit(solution)/shard_map/ppermute | solution.py:401
  31.9 3.9 %collective-permute-start.6 = (bf16[128,576]{1,0:T(8,128)(2,1)S(1)}, bf16[128,576]{1,0:T(8,128)(2,1)S(1)}, u32[]{:S(2)}, u32[]{:S(2)}) collective-permute-start(bf16[128,576]{1,0:T(8,128)(2,1)S(1)} %add_convert_fusion.4), channel_id=1, source_target_pairs={{0,24},{4,28},{8,16},{12,20},{16,8},{20,12},{24,0},{28,4},{1,25},{... | collective-permute-start | bytes 442376 | tf_op jit(solution)/shard_map/ppermute | solution.py:401
  35.8 0.5 %collective-permute-start.13 = (bf16[4,2,128,128]{3,2,1,0:T(8,128)(2,1)S(1)}, bf16[4,2,128,128]{3,2,1,0:T(8,128)(2,1)S(1)}, u32[]{:S(2)}, u32[]{:S(2)}) collective-permute-start(bf16[4,2,128,128]{3,2,1,0:T(8,128)(2,1)S(1)} %get-tuple-element.95), channel_id=1, source_target_pairs={{0,1},{1,0},{2,3},{3,2},{4,5},{5,4},{6,7},{7,6},{8,9},{9,8},{10,11... | collective-permute-start | bytes 786440 | tf_op jit(solution)/shard_map/ppermute | solution.py:401
  36.3 1.9 %query_gradient.1 = (f32[2048,128]{1,0:T(8,128)}, f32[16,64,128]{2,1,0:T(8,128)}) custom-call(bf16[128,576]{1,0:T(8,128)(2,1)S(1)} %get-tuple-element.54.rest_0_.refs_0_.rest_2_, bf16[128,576]{1,0:T(8,128)(2,1)S(1)} %collective-permute-done.rest_1_.refs_1_.rest_3_, bf16[4,256,128]{2,1,0:T(8,128)(2,1)S(1)} %get-tuple-element.62.refs_2_, ...), custom_call_target="tpu_custom_call" | custom-call | flops 1000000000 | bytes 5000000 | tf_op jit(solution)/shard_map/query_gradient/pallas_call | solution.py:337
  38.2 0.8 %finish.2 = (f32[16,32,512]{2,1,0:T(8,128)}, f32[16,128,128]{2,1,0:T(8,128)}) custom-call(bf16[4,2,128,128]{3,2,1,0:T(8,128)(2,1)S(1)} %collective-permute-done.4.far_ref, bf16[4,2,128,128]{3,2,1,0:T(8,128)(2,1)S(1)} %get-tuple-element.97.rest_0_, bf16[4,2,128,128]{3,2,1,0:T(8,128)(2,1)S(1)} %collective-permute-done.14.rest_1_), custom_call_target="tpu_custom_call" | custom-call | flops 1000000 | bytes 1200000 | tf_op jit(solution)/shard_map/finish/pallas_call | solution.py:380
  39.1 0.1 collective-permute-done.6
  39.2 0.8 %convert_add_fusion = f32[128,576]{1,0:T(8,128)} fusion(bf16[128,576]{1,0:T(8,128)(2,1)S(1)} %collective-permute-done.6, bf16[128,576]{1,0:T(8,128)(2,1)S(1)} %add_convert_fusion.4), kind=kLoop, calls=%fused_computation.5 | loop fusion | flops 221184 | bytes 589824 | tf_op jit(solution)/shard_map/add | solution.py:518
  40.0 2.8 %collective-permute-done.10.far_ref = bf16[12,2,128,128]{3,2,1,0:T(8,128)(2,1)S(1)} collective-permute-done((bf16[12,2,128,128]{3,2,1,0:T(8,128)(2,1)S(1)}, bf16[12,2,128,128]{3,2,1,0:T(8,128)(2,1)S(1)}, u32[]{:S(2)}, u32[]{:S(2)}) %collective-permute-start.10) | collective-permute-done | bytes 786464 | tf_op jit(solution)/shard_map/ppermute | solution.py:401
  42.7 1.3 %finish.3 = (f32[16,32,512]{2,1,0:T(8,128)}, f32[16,128,128]{2,1,0:T(8,128)}) custom-call(bf16[12,2,128,128]{3,2,1,0:T(8,128)(2,1)S(1)} %collective-permute-done.10.far_ref, bf16[4,2,128,128]{3,2,1,0:T(8,128)(2,1)S(1)} %get-tuple-element.90.rest_0_, ...), custom_call_target="tpu_custom_call", output_to_operand_aliasing={{0}: (7, {}), {1}: (8, {})} | custom-call | flops 1000000 | bytes 3600000 | tf_op jit(solution)/shard_map/finish/pallas_call | solution.py:380
  (17 shorter events, 0.4 us)
Async XLA Ops:
  0.6 7.4 %collective-permute-start = (bf16[128,576]{1,0:T(8,128)(2,1)}, bf16[128,576]{1,0:T(8,128)(2,1)S(1)}, u32[]{:S(2)}, u32[]{:S(2)}) collective-permute-start(bf16[128,576]{1,0:T(8,128)(2,1)} %bitcast.15), channel_id=1, source_target_pairs={{0,2},{2,0},{1,3},{3,1},{4,6},{6,4},{5,7},{7,5},{8,10},{10,8},{9,1... | collective-permute-start | bytes 442376 | tf_op jit(solution)/shard_map/ppermute | solution.py:401
  9.8 1.6 %collective-permute-start.1 = (bf16[4,2,128,128]{3,2,1,0:T(8,128)(2,1)S(1)}, bf16[4,2,128,128]{3,2,1,0:T(8,128)(2,1)S(1)}, u32[]{:S(2)}, u32[]{:S(2)}) collective-permute-start(bf16[4,2,128,128]{3,2,1,0:T(8,128)(2,1)S(1)} %get-tuple-element.69), channel_id=1, source_target_pairs={{0,1},{1,0},{2,3},{3,2},{4,5},{5,4},{6,7},{7,6},{8,9},{9,8},{10,11... | collective-permute-start | bytes 786440 | tf_op jit(solution)/shard_map/ppermute | solution.py:401
  13.8 7.1 %collective-permute-start.2 = (bf16[128,576]{1,0:T(8,128)(2,1)S(1)}, bf16[128,576]{1,0:T(8,128)(2,1)S(1)}, u32[]{:S(2)}, u32[]{:S(2)}) collective-permute-start(bf16[128,576]{1,0:T(8,128)(2,1)S(1)} %get-tuple-element.78), channel_id=1, source_target_pairs={{0,2},{2,0},{1,3},{3,1},{4,6},{6,4},{5,7},{7,5},{8,10},{10,8},{9,1... | collective-permute-start | bytes 442376 | tf_op jit(solution)/shard_map/ppermute | solution.py:401
  15.6 10.9 %collective-permute-start.4 = (bf16[4,2,128,128]{3,2,1,0:T(8,128)(2,1)S(1)}, bf16[4,2,128,128]{3,2,1,0:T(8,128)(2,1)S(1)}, u32[]{:S(2)}, u32[]{:S(2)}) collective-permute-start(bf16[4,2,128,128]{3,2,1,0:T(8,128)(2,1)S(1)} %add_convert_fusion.3), channel_id=1, source_target_pairs={{0,2},{2,0},{1,3},{3,1},{4,6},{6,4},{5,7},{7,5},{8,10},{10,8},{9,1... | collective-permute-start | bytes 786440 | tf_op jit(solution)/shard_map/ppermute | solution.py:401
  16.5 6.2 %collective-permute-start.7 = (bf16[4,2,128,128]{3,2,1,0:T(8,128)(2,1)S(1)}, bf16[4,2,128,128]{3,2,1,0:T(8,128)(2,1)S(1)}, u32[]{:S(2)}, u32[]{:S(2)}) collective-permute-start(bf16[4,2,128,128]{3,2,1,0:T(8,128)(2,1)S(1)} %get-tuple-element.84), channel_id=1, source_target_pairs={{0,1},{1,0},{2,3},{3,2},{4,5},{5,4},{6,7},{7,6},{8,9},{9,8},{10,11... | collective-permute-start | bytes 786440 | tf_op jit(solution)/shard_map/ppermute | solution.py:401
  17.3 5.5 %collective-permute-start.9 = (bf16[4,2,128,128]{3,2,1,0:T(8,128)(2,1)S(1)}, bf16[4,2,128,128]{3,2,1,0:T(8,128)(2,1)S(1)}, u32[]{:S(2)}, u32[]{:S(2)}) collective-permute-start(bf16[4,2,128,128]{3,2,1,0:T(8,128)(2,1)S(1)} %get-tuple-element.89), channel_id=1, source_target_pairs={{0,1},{1,0},{2,3},{3,2},{4,5},{5,4},{6,7},{7,6},{8,9},{9,8},{10,11... | collective-permute-start | bytes 786440 | tf_op jit(solution)/shard_map/ppermute | solution.py:401
  18.5 4.4 %collective-permute-start.8 = (bf16[4,2,128,128]{3,2,1,0:T(8,128)(2,1)S(1)}, bf16[4,2,128,128]{3,2,1,0:T(8,128)(2,1)S(1)}, u32[]{:S(2)}, u32[]{:S(2)}) collective-permute-start(bf16[4,2,128,128]{3,2,1,0:T(8,128)(2,1)S(1)} %get-tuple-element.87), channel_id=1, source_target_pairs={{0,1},{1,0},{2,3},{3,2},{4,5},{5,4},{6,7},{7,6},{8,9},{9,8},{10,11... | collective-permute-start | bytes 786440 | tf_op jit(solution)/shard_map/ppermute | solution.py:401
  20.9 5.4 %collective-permute-start.3 = (bf16[128,576]{1,0:T(8,128)(2,1)S(1)}, bf16[128,576]{1,0:T(8,128)(2,1)S(1)}, u32[]{:S(2)}, u32[]{:S(2)}) collective-permute-start(bf16[128,576]{1,0:T(8,128)(2,1)S(1)} %add_convert_fusion.6), channel_id=1, source_target_pairs={{0,4},{4,0},{8,12},{12,8},{16,20},{20,16},{24,28},{28,24},{1,5},{5... | collective-permute-start | bytes 442376 | tf_op jit(solution)/shard_map/ppermute | solution.py:401
  23.1 19.6 %collective-permute-start.10 = (bf16[12,2,128,128]{3,2,1,0:T(8,128)(2,1)S(1)}, bf16[12,2,128,128]{3,2,1,0:T(8,128)(2,1)S(1)}, u32[]{:S(2)}, u32[]{:S(2)}) collective-permute-start(bf16[12,2,128,128]{3,2,1,0:T(8,128)(2,1)S(1)} %pad_maximum_fusion), channel_id=1, source_target_pairs={{0,2},{2,0},{1,3},{3,1},{4,6},{6,4},{5,7},{7,5},{8,10},{10,8},{9,1... | collective-permute-start | bytes 2359304 | tf_op jit(solution)/shard_map/ppermute | solution.py:401
  26.5 5.3 %collective-permute-start.5 = (bf16[128,576]{1,0:T(8,128)(2,1)S(1)}, bf16[128,576]{1,0:T(8,128)(2,1)S(1)}, u32[]{:S(2)}, u32[]{:S(2)}) collective-permute-start(bf16[128,576]{1,0:T(8,128)(2,1)S(1)} %add_convert_fusion.5), channel_id=1, source_target_pairs={{0,8},{4,12},{8,0},{12,4},{16,24},{20,28},{24,16},{28,20},{1,9},{5... | collective-permute-start | bytes 442376 | tf_op jit(solution)/shard_map/ppermute | solution.py:401
  28.3 8.0 %collective-permute-start.14 = (bf16[4,2,128,128]{3,2,1,0:T(8,128)(2,1)S(1)}, bf16[4,2,128,128]{3,2,1,0:T(8,128)(2,1)S(1)}, u32[]{:S(2)}, u32[]{:S(2)}) collective-permute-start(bf16[4,2,128,128]{3,2,1,0:T(8,128)(2,1)S(1)} %get-tuple-element.98), channel_id=1, source_target_pairs={{0,1},{1,0},{2,3},{3,2},{4,5},{5,4},{6,7},{7,6},{8,9},{9,8},{10,11... | collective-permute-start | bytes 786440 | tf_op jit(solution)/shard_map/ppermute | solution.py:401
  31.9 7.3 %collective-permute-start.6 = (bf16[128,576]{1,0:T(8,128)(2,1)S(1)}, bf16[128,576]{1,0:T(8,128)(2,1)S(1)}, u32[]{:S(2)}, u32[]{:S(2)}) collective-permute-start(bf16[128,576]{1,0:T(8,128)(2,1)S(1)} %add_convert_fusion.4), channel_id=1, source_target_pairs={{0,24},{4,28},{8,16},{12,20},{16,8},{20,12},{24,0},{28,4},{1,25},{... | collective-permute-start | bytes 442376 | tf_op jit(solution)/shard_map/ppermute | solution.py:401
  35.8 4.2 %collective-permute-start.11 = (bf16[4,2,128,128]{3,2,1,0:T(8,128)(2,1)S(1)}, bf16[4,2,128,128]{3,2,1,0:T(8,128)(2,1)S(1)}, u32[]{:S(2)}, u32[]{:S(2)}) collective-permute-start(bf16[4,2,128,128]{3,2,1,0:T(8,128)(2,1)S(1)} %get-tuple-element.91), channel_id=1, source_target_pairs={{0,1},{1,0},{2,3},{3,2},{4,5},{5,4},{6,7},{7,6},{8,9},{9,8},{10,11... | collective-permute-start | bytes 786440 | tf_op jit(solution)/shard_map/ppermute | solution.py:401
  35.8 4.2 %collective-permute-start.13 = (bf16[4,2,128,128]{3,2,1,0:T(8,128)(2,1)S(1)}, bf16[4,2,128,128]{3,2,1,0:T(8,128)(2,1)S(1)}, u32[]{:S(2)}, u32[]{:S(2)}) collective-permute-start(bf16[4,2,128,128]{3,2,1,0:T(8,128)(2,1)S(1)} %get-tuple-element.95), channel_id=1, source_target_pairs={{0,1},{1,0},{2,3},{3,2},{4,5},{5,4},{6,7},{7,6},{8,9},{9,8},{10,11... | collective-permute-start | bytes 786440 | tf_op jit(solution)/shard_map/ppermute | solution.py:401
  36.3 3.7 %collective-permute-start.12 = (bf16[4,2,128,128]{3,2,1,0:T(8,128)(2,1)S(1)}, bf16[4,2,128,128]{3,2,1,0:T(8,128)(2,1)S(1)}, u32[]{:S(2)}, u32[]{:S(2)}) collective-permute-start(bf16[4,2,128,128]{3,2,1,0:T(8,128)(2,1)S(1)} %get-tuple-element.93), channel_id=1, source_target_pairs={{0,1},{1,0},{2,3},{3,2},{4,5},{5,4},{6,7},{7,6},{8,9},{9,8},{10,11... | collective-permute-start | bytes 786440 | tf_op jit(solution)/shard_map/ppermute | solution.py:401

commit v6 on v5

--- a/solution.py
+++ b/solution.py
@@ -234,6 +234,17 @@
             weight_group(paired, g, [qt_ref[h, :nope_width] for h in heads], [d for _, d in soft], gv, latent, vt_ref, bp_ref, outs)
         else:
             gv_ref[:, g * value_width:(g + group) * value_width] = gv
+    if paired and final:
+        for n, ref in enumerate(total_refs):
+            rows = total_latent.shape[0] // parts
+            start, half = n * rows, rows // 2
+            blocks = latent_width // 128
+            for j in range(blocks):
+                ref[j * rows:(j + 1) * rows] = total_latent[start:start + rows, j * 128:(j + 1) * 128].astype(ref.dtype)
+            ref[blocks * rows:] = jnp.concatenate(
+                [total_rotary[start:start + half], total_rotary[start + half:start + rows]], axis=1
+            ).astype(ref.dtype)
+        return
     start = 0
     for ref in total_refs:
         stop = start + ref.shape[0]
@@ -270,7 +281,8 @@
         shapes += partial_shapes(paired, count, nope_width, latent_width, value_width)
     else:
         shapes += [out(key_count, count * value_width)]
-    shapes += [out(*p.shape) for p in parts] if final else [jax.ShapeDtypeStruct((key_count, row_width), F32)]
+    packed = lambda p: (p.shape[0] * p.shape[1] // 128, 128) if paired else p.shape
+    shapes += [out(*packed(p)) for p in parts] if final else [jax.ShapeDtypeStruct((key_count, row_width), F32)]
     group = min(4, count) if paired else 1
     return pl.pallas_call(
         functools.partial(attend_kernel, paired, before is None, final, weights, len(parts), begin, count, latent_width),
@@ -345,6 +357,27 @@
         name="query_gradient",
     )(*parts, *[x for pair in pairs for x in pair])
     return nope.reshape(1, query_count, heads, nope_width), jnp.transpose(rope, (2, 0, 1))[None]
+
+
+def unpack_kernel(one_ref, two_ref, out_ref):
+    total = one_ref[...].astype(F32) + two_ref[...].astype(F32)
+    rows, half = out_ref.shape[0], out_ref.shape[0] // 2
+    blocks = out_ref.shape[1] // 128
+    for j in range(blocks):
+        out_ref[:, j * 128:(j + 1) * 128] = total[j * rows:(j + 1) * rows]
+    rope = out_ref.shape[1] - blocks * 128
+    out_ref[:half, blocks * 128:] = total[blocks * rows:, :rope]
+    out_ref[half:, blocks * 128:] = total[blocks * rows:, rope:]
+
+
+def unpack(one, two, rows, row_width):
+    return pl.pallas_call(
+        unpack_kernel,
+        out_shape=jax.ShapeDtypeStruct((rows, row_width), F32),
+        compiler_params=params(8),
+        cost_estimate=cost(1_000_000, 600_000),
+        name="unpack",
+    )(one, two)
 
 
 def finish_kernel(places, first, far_ref, *rest):
@@ -417,6 +450,7 @@
     paired = (
         ctx_size == 2 and dp_size == 2 and latent_width == 4 * value_width and nope_width == value_width
         and nope_width % 64 == 0 and value_width % 128 == 0 and heads % 16 == 0
+        and 2 * (row_width - latent_width) == 128 and head_size > 1 and head_size & (head_size - 1) == 0
     )
     own_rows = latent_cache[0].reshape(-1, row_width)
     if ctx_size == 2:
@@ -517,6 +551,8 @@
             got = swap(rounded, "head", head_size, bits | (bits >> 1) if bits >= 4 else bits)
             share = rounded.astype(F32) + got.astype(F32)
             bits, n = bits * 2, n + 1
+        if paired:
+            share = unpack(rounded, got, *own_rows.shape)
     else:
         share = lax.psum(share.astype(BF16), "head").astype(F32)
     if paired:

time: 44.1 us -> 43.8 us (level)
  Pallas kernels: 15 us -> 15.8 us
  other arithmetic: 1.26 us -> 0.5 us
    pallas_call x0 -> x1, Pallas kernels: none -> 0.8 us  [unpack(): pl.pallas_call(unpack_kernel, out_shape=jax.ShapeDtypeStruct((rows, row_w...]
    add x1 -> x0, other arithmetic: 0.76 us -> none  [on_device(): share = rounded.astype(F32) + got.astype(F32)]
  transfers between devices with their start and end apart: 15 -> 15, of which waited for: 8 -> 8; matrix products, arithmetic and copies ran while one was open for 3% -> 1% of each run, Pallas kernels for 22% -> 24%
where the time goes in v6:
time: 43.8 us; the launch traced here: 43.6 us
  Pallas kernels  15.8 us (36%)
  starting transfers between devices  15.5 us (35%)
  waiting for transfers between devices  11.1 us (25%)
  between operations  0.79 us (2%)
  other arithmetic  0.5 us (1%)
    ppermute x15, starting transfers between devices, swap(): return lax.ppermute(x, axis, [(i, i ^ bits) for i in range(size)])  15.5 us
    ppermute x15, waiting for transfers between devices, swap(): return lax.ppermute(x, axis, [(i, i ^ bits) for i in range(size)])  11.1 us
    pallas_call x3, Pallas kernels, attend(): pl.pallas_call(functools.partial(attend_kernel, paired, before is None, f...  5.33 us
    pallas_call x1, Pallas kernels, prepare(): pl.pallas_call(functools.partial(prepare_kernel, parts, page_rows), in_sp...  3.71 us
    pallas_call x2, Pallas kernels, finish(): pl.pallas_call(functools.partial(finish_kernel, places, not before), in_s...  2.1 us
    pallas_call x1, Pallas kernels, query_gradient(): pl.pallas_call(functools.partial(query_kernel, counts, len(parts)), out_s...  1.92 us
    pallas_call x3, Pallas kernels, weight_partials(): pl.pallas_call(functools.partial(weights_kernel, True, len(parts), spans,...  1.92 us
  transfers between devices with their start and end apart: 15, of which 8 were waited for; matrix products, arithmetic and copies ran while one was open for 1% of the time, Pallas kernels for 24%

profile of v6, /device:TPU:0, one launch (start us, length us, event | category | flops | bytes accessed | tf_op | source)
XLA Modules:
  0.0 43.6 jit_solution(13558613033582515272)
XLA Ops:
  0.6 3.0 %collective-permute-start = (bf16[128,576]{1,0:T(8,128)(2,1)}, bf16[128,576]{1,0:T(8,128)(2,1)S(1)}, u32[]{:S(2)}, u32[]{:S(2)}) collective-permute-start(bf16[128,576]{1,0:T(8,128)(2,1)} %bitcast.15), channel_id=1, source_target_pairs={{0,2},{2,0},{1,3},{3,1},{4,6},{6,4},{5,7},{7,5},{8,10},{10,8},{9,1... | collective-permute-start | bytes 442376 | tf_op jit(solution)/shard_map/ppermute | solution.py:434
  3.7 3.7 %prepare.1 = (bf16[16,192,128]{2,1,0:T(8,128)(2,1)S(1)}, bf16[16,128,128]{2,1,0:T(8,128)(2,1)S(1)}, bf16[16,128,512]{2,1,0:T(8,128)(2,1)S(1)}, bf16[16,512,128]{...) custom-call(bf16[128,16,128]{2,1,0:T(8,128)(2,1)} %bitcast.11, ...), custom_call_target="tpu_custom_call" | custom-call | flops 600000000 | bytes 12000000 | tf_op jit(solution)/shard_map/prepare/pallas_call | solution.py:103
  7.4 0.7 %collective-permute-done.rest_1_.refs_1_.rest_3_ = bf16[128,576]{1,0:T(8,128)(2,1)S(1)} collective-permute-done((bf16[128,576]{1,0:T(8,128)(2,1)}, bf16[128,576]{1,0:T(8,128)(2,1)S(1)}, u32[]{:S(2)}, u32[]{:S(2)}) %collective-permute-start) | collective-permute-done | bytes 147488 | tf_op jit(solution)/shard_map/ppermute | solution.py:434
  8.1 1.7 %attend.3 = (bf16[4,256,128]{2,1,0:T(8,128)(2,1)S(1)}, bf16[4,256,128]{2,1,0:T(8,128)(2,1)S(1)}, bf16[4,2,128,128]{3,2,1,0:T(8,128)(2,1)S(1)}, bf16[4,2,128,128]...) custom-call(bf16[16,192,128]{2,1,0:T(8,128)(2,1)S(1)} %get-tuple-ele, ...), custom_call_target="tpu_custom_call" | custom-call | flops 1600000000 | bytes 2000000 | tf_op jit(solution)/shard_map/attend/pallas_call | solution.py:287
  9.9 1.3 %attend.4 = (bf16[4,256,128]{2,1,0:T(8,128)(2,1)S(1)}, bf16[4,256,128]{2,1,0:T(8,128)(2,1)S(1)}, bf16[256,512]{1,0:T(8,128)(2,1)S(1)}, f32[256,576]{1,0:T(8,128)S(1)}) custom-call(bf16[16,192,128]{2,1,0:T(8,128)(2,1)S(1)} %get-tuple-element.55.qt_ref, bf16[16,128,128]{2,1,0:T(8,128)(2,1)S(1)} %get-tuple-element.56.go_ref, ...), custom_call_target="tpu_custom_call" | custom-call | flops 1200000000 | bytes 2000000 | tf_op jit(solution)/shard_map/attend/pallas_call | solution.py:287
  11.2 0.2 collective-permute-done.1
  11.5 2.3 %attend.5 = (bf16[8,256,128]{2,1,0:T(8,128)(2,1)S(1)}, bf16[8,256,128]{2,1,0:T(8,128)(2,1)S(1)}, bf16[256,1024]{1,0:T(8,128)(2,1)S(1)}, bf16[576,128]{1,0:T(8,128)(2,1)S(1)}, bf16[576,128]{1,0:T(8,128)(2,1)S(1)}) custom-call(bf16[16,192,128]{2,1,0:T(8,128)(2,1)S(1)} %get-tuple-element.55.qt_ref, bf16[16,128,128]{2,1,0:T(8,128)(2,1)S(1)} %get-tuple-element.56.go_ref, ...), custom_call_target="tpu_custom_call" | custom-call | flops 2400000000 | bytes 4000000 | tf_op jit(solution)/shard_map/attend/pallas_call | solution.py:287
  13.8 1.8 %collective-permute-start.2 = (bf16[576,128]{1,0:T(8,128)(2,1)S(1)}, bf16[576,128]{1,0:T(8,128)(2,1)S(1)}, u32[]{:S(2)}, u32[]{:S(2)}) collective-permute-start(bf16[576,128]{1,0:T(8,128)(2,1)S(1)} %get-tuple-element.78), channel_id=1, source_target_pairs={{0,2},{2,0},{1,3},{3,1},{4,6},{6,4},{5,7},{7,5},{8,10},{10,8},{9,1... | collective-permute-start | bytes 442376 | tf_op jit(solution)/shard_map/ppermute | solution.py:434
  15.6 0.3 collective-permute-start.4
  15.9 0.6 %weight_partials.3 = (bf16[4,2,128,128]{3,2,1,0:T(8,128)(2,1)S(1)}, bf16[4,2,128,128]{3,2,1,0:T(8,128)(2,1)S(1)}, bf16[4,2,128,128]{3,2,1,0:T(8,128)(2,1)S(1)}, bf16[4,2,128,128]{3,2,1,0:T(8,128)(2,1)S(1)}) custom-call(bf16[16,192,128]{2,1,0:T(8,128)(2,1)S(1)} %get-tuple-element.55.qt_ref, bf16[4,256,128]{2,1,0:T(8,128)(2,1)S(1)} %get-tuple-element.81.refs_4_.rest_0_, ...), custom_call_target="tpu_custom_call" | custom-call | flops 400000000 | bytes 1600000 | tf_op jit(solution)/shard_map/weight_partials/pallas_call | solution.py:317
  16.6 0.6 %weight_partials.5 = (bf16[4,2,128,128]{3,2,1,0:T(8,128)(2,1)S(1)}, bf16[4,2,128,128]{3,2,1,0:T(8,128)(2,1)S(1)}, bf16[4,2,128,128]{3,2,1,0:T(8,128)(2,1)S(1)}, bf16[4,2,128,128]{3,2,1,0:T(8,128)(2,1)S(1)}) custom-call(bf16[16,192,128]{2,1,0:T(8,128)(2,1)S(1)} %get-tuple-element.55.qt_ref, bf16[8,256,128]{2,1,0:T(8,128)(2,1)S(1)} %get-tuple-element.71.refs_6_.rest_0_, ...), custom_call_target="tpu_custom_call" | custom-call | flops 400000000 | bytes 1600000 | tf_op jit(solution)/shard_map/weight_partials/pallas_call | solution.py:317
  17.3 0.6 %collective-permute-start.9 = (bf16[4,2,128,128]{3,2,1,0:T(8,128)(2,1)S(1)}, bf16[4,2,128,128]{3,2,1,0:T(8,128)(2,1)S(1)}, u32[]{:S(2)}, u32[]{:S(2)}) collective-permute-start(bf16[4,2,128,128]{3,2,1,0:T(8,128)(2,1)S(1)} %get-tuple-element.89), channel_id=1, source_target_pairs={{0,1},{1,0},{2,3},{3,2},{4,5},{5,4},{6,7},{7,6},{8,9},{9,8},{10,11... | collective-permute-start | bytes 786440 | tf_op jit(solution)/shard_map/ppermute | solution.py:434
  17.8 0.6 %weight_partials.4 = (bf16[4,2,128,128]{3,2,1,0:T(8,128)(2,1)S(1)}, bf16[4,2,128,128]{3,2,1,0:T(8,128)(2,1)S(1)}, bf16[4,2,128,128]{3,2,1,0:T(8,128)(2,1)S(1)}, bf16[4,2,128,128]{3,2,1,0:T(8,128)(2,1)S(1)}) custom-call(bf16[16,192,128]{2,1,0:T(8,128)(2,1)S(1)} %get-tuple-element.55.qt_ref, bf16[8,256,128]{2,1,0:T(8,128)(2,1)S(1)} %get-tuple-element.71.refs_6_.rest_0_, ...), custom_call_target="tpu_custom_call" | custom-call | flops 400000000 | bytes 1600000 | tf_op jit(solution)/shard_map/weight_partials/pallas_call | solution.py:317
  18.5 0.1 collective-permute-start.8
  18.6 2.0 %collective-permute-done.2 = bf16[576,128]{1,0:T(8,128)(2,1)S(1)} collective-permute-done((bf16[576,128]{1,0:T(8,128)(2,1)S(1)}, bf16[576,128]{1,0:T(8,128)(2,1)S(1)}, u32[]{:S(2)}, u32[]{:S(2)}) %collective-permute-start.2) | collective-permute-done | bytes 147488 | tf_op jit(solution)/shard_map/ppermute | solution.py:434
  20.6 1.8 %collective-permute-start.3 = (bf16[576,128]{1,0:T(8,128)(2,1)S(1)}, bf16[576,128]{1,0:T(8,128)(2,1)S(1)}, u32[]{:S(2)}, u32[]{:S(2)}) collective-permute-start(bf16[576,128]{1,0:T(8,128)(2,1)S(1)} %add_convert_fusion.6), channel_id=1, source_target_pairs={{0,4},{4,0},{8,12},{12,8},{16,20},{20,16},{24,28},{28,24},{1,5},{5... | collective-permute-start | bytes 442376 | tf_op jit(solution)/shard_map/ppermute | solution.py:434
  22.5 0.1 add_convert_fusion
  22.6 0.1 add_convert_fusion.1
  22.6 0.1 pad_maximum_fusion
  22.7 1.6 %collective-permute-start.10 = (bf16[12,2,128,128]{3,2,1,0:T(8,128)(2,1)S(1)}, bf16[12,2,128,128]{3,2,1,0:T(8,128)(2,1)S(1)}, u32[]{:S(2)}, u32[]{:S(2)}) collective-permute-start(bf16[12,2,128,128]{3,2,1,0:T(8,128)(2,1)S(1)} %pad_maximum_fusion), channel_id=1, source_target_pairs={{0,2},{2,0},{1,3},{3,1},{4,6},{6,4},{5,7},{7,5},{8,10},{10,8},{9,1... | collective-permute-start | bytes 2359304 | tf_op jit(solution)/shard_map/ppermute | solution.py:434
  24.3 1.5 %collective-permute-done.3 = bf16[576,128]{1,0:T(8,128)(2,1)S(1)} collective-permute-done((bf16[576,128]{1,0:T(8,128)(2,1)S(1)}, bf16[576,128]{1,0:T(8,128)(2,1)S(1)}, u32[]{:S(2)}, u32[]{:S(2)}) %collective-permute-start.3) | collective-permute-done | bytes 147488 | tf_op jit(solution)/shard_map/ppermute | solution.py:434
  25.9 0.3 collective-permute-done.4.far_ref
  26.2 1.8 %collective-permute-start.5 = (bf16[576,128]{1,0:T(8,128)(2,1)S(1)}, bf16[576,128]{1,0:T(8,128)(2,1)S(1)}, u32[]{:S(2)}, u32[]{:S(2)}) collective-permute-start(bf16[576,128]{1,0:T(8,128)(2,1)S(1)} %add_convert_fusion.5), channel_id=1, source_target_pairs={{0,8},{4,12},{8,0},{12,4},{16,24},{20,28},{24,16},{28,20},{1,9},{5... | collective-permute-start | bytes 442376 | tf_op jit(solution)/shard_map/ppermute | solution.py:434
  28.0 0.5 %collective-permute-start.11 = (bf16[4,2,128,128]{3,2,1,0:T(8,128)(2,1)S(1)}, bf16[4,2,128,128]{3,2,1,0:T(8,128)(2,1)S(1)}, u32[]{:S(2)}, u32[]{:S(2)}) collective-permute-start(bf16[4,2,128,128]{3,2,1,0:T(8,128)(2,1)S(1)} %get-tuple-element.91), channel_id=1, source_target_pairs={{0,1},{1,0},{2,3},{3,2},{4,5},{5,4},{6,7},{7,6},{8,9},{9,8},{10,11... | collective-permute-start | bytes 786440 | tf_op jit(solution)/shard_map/ppermute | solution.py:434
  28.5 2.8 %collective-permute-done.5 = bf16[576,128]{1,0:T(8,128)(2,1)S(1)} collective-permute-done((bf16[576,128]{1,0:T(8,128)(2,1)S(1)}, bf16[576,128]{1,0:T(8,128)(2,1)S(1)}, u32[]{:S(2)}, u32[]{:S(2)}) %collective-permute-start.5) | collective-permute-done | bytes 147488 | tf_op jit(solution)/shard_map/ppermute | solution.py:434
  31.4 3.9 %collective-permute-start.6 = (bf16[576,128]{1,0:T(8,128)(2,1)S(1)}, bf16[576,128]{1,0:T(8,128)(2,1)S(1)}, u32[]{:S(2)}, u32[]{:S(2)}) collective-permute-start(bf16[576,128]{1,0:T(8,128)(2,1)S(1)} %add_convert_fusion.4.one_ref), channel_id=1, source_target_pairs={{0,24},{4,28},{8,16},{12,20},{16,8},{20,12},{24,0},{28,4},{1,25},{... | collective-permute-start | bytes 442376 | tf_op jit(solution)/shard_map/ppermute | solution.py:434
  35.3 1.9 %query_gradient.1 = (f32[2048,128]{1,0:T(8,128)}, f32[16,64,128]{2,1,0:T(8,128)}) custom-call(bf16[128,576]{1,0:T(8,128)(2,1)S(1)} %get-tuple-element.54.rest_0_.refs_0_.rest_2_, bf16[128,576]{1,0:T(8,128)(2,1)S(1)} %collective-permute-done.rest_1_.refs_1_.rest_3_, bf16[4,256,128]{2,1,0:T(8,128)(2,1)S(1)} %get-tuple-element.62.refs_2_, ...), custom_call_target="tpu_custom_call" | custom-call | flops 1000000000 | bytes 5000000 | tf_op jit(solution)/shard_map/query_gradient/pallas_call | solution.py:349
  37.2 0.8 %finish.2 = (f32[16,32,512]{2,1,0:T(8,128)}, f32[16,128,128]{2,1,0:T(8,128)}) custom-call(bf16[4,2,128,128]{3,2,1,0:T(8,128)(2,1)S(1)} %collective-permute-done.4.far_ref, bf16[4,2,128,128]{3,2,1,0:T(8,128)(2,1)S(1)} %get-tuple-element.97.rest_0_, bf16[4,2,128,128]{3,2,1,0:T(8,128)(2,1)S(1)} %collective-permute-done.14.rest_1_), custom_call_target="tpu_custom_call" | custom-call | flops 1000000 | bytes 1200000 | tf_op jit(solution)/shard_map/finish/pallas_call | solution.py:413
  38.0 1.9 %collective-permute-done.6.two_ref = bf16[576,128]{1,0:T(8,128)(2,1)S(1)} collective-permute-done((bf16[576,128]{1,0:T(8,128)(2,1)S(1)}, bf16[576,128]{1,0:T(8,128)(2,1)S(1)}, u32[]{:S(2)}, u32[]{:S(2)}) %collective-permute-start.6) | collective-permute-done | bytes 147488 | tf_op jit(solution)/shard_map/ppermute | solution.py:434
  39.9 0.8 %unpack.1 = f32[128,576]{1,0:T(8,128)} custom-call(bf16[576,128]{1,0:T(8,128)(2,1)S(1)} %add_convert_fusion.4.one_ref, bf16[576,128]{1,0:T(8,128)(2,1)S(1)} %collective-permute-done.6.two_ref), custom_call_target="tpu_custom_call" | custom-call | flops 1000000 | bytes 600000 | tf_op jit(solution)/shard_map/unpack/pallas_call | solution.py:374
  40.7 1.7 %collective-permute-done.10.far_ref = bf16[12,2,128,128]{3,2,1,0:T(8,128)(2,1)S(1)} collective-permute-done((bf16[12,2,128,128]{3,2,1,0:T(8,128)(2,1)S(1)}, bf16[12,2,128,128]{3,2,1,0:T(8,128)(2,1)S(1)}, u32[]{:S(2)}, u32[]{:S(2)}) %collective-permute-start.10) | collective-permute-done | bytes 786464 | tf_op jit(solution)/shard_map/ppermute | solution.py:434
  42.4 1.3 %finish.3 = (f32[16,32,512]{2,1,0:T(8,128)}, f32[16,128,128]{2,1,0:T(8,128)}) custom-call(bf16[12,2,128,128]{3,2,1,0:T(8,128)(2,1)S(1)} %collective-permute-done.10.far_ref, bf16[4,2,128,128]{3,2,1,0:T(8,128)(2,1)S(1)} %get-tuple-element.90.rest_0_, ...), custom_call_target="tpu_custom_call", output_to_operand_aliasing={{0}: (7, {}), {1}: (8, {})} | custom-call | flops 1000000 | bytes 3600000 | tf_op jit(solution)/shard_map/finish/pallas_call | solution.py:413
  (17 shorter events, 0.4 us)
Async XLA Ops:
  0.6 7.4 %collective-permute-start = (bf16[128,576]{1,0:T(8,128)(2,1)}, bf16[128,576]{1,0:T(8,128)(2,1)S(1)}, u32[]{:S(2)}, u32[]{:S(2)}) collective-permute-start(bf16[128,576]{1,0:T(8,128)(2,1)} %bitcast.15), channel_id=1, source_target_pairs={{0,2},{2,0},{1,3},{3,1},{4,6},{6,4},{5,7},{7,5},{8,10},{10,8},{9,1... | collective-permute-start | bytes 442376 | tf_op jit(solution)/shard_map/ppermute | solution.py:434
  9.8 1.6 %collective-permute-start.1 = (bf16[4,2,128,128]{3,2,1,0:T(8,128)(2,1)S(1)}, bf16[4,2,128,128]{3,2,1,0:T(8,128)(2,1)S(1)}, u32[]{:S(2)}, u32[]{:S(2)}) collective-permute-start(bf16[4,2,128,128]{3,2,1,0:T(8,128)(2,1)S(1)} %get-tuple-element.69), channel_id=1, source_target_pairs={{0,1},{1,0},{2,3},{3,2},{4,5},{5,4},{6,7},{7,6},{8,9},{9,8},{10,11... | collective-permute-start | bytes 786440 | tf_op jit(solution)/shard_map/ppermute | solution.py:434
  13.8 6.7 %collective-permute-start.2 = (bf16[576,128]{1,0:T(8,128)(2,1)S(1)}, bf16[576,128]{1,0:T(8,128)(2,1)S(1)}, u32[]{:S(2)}, u32[]{:S(2)}) collective-permute-start(bf16[576,128]{1,0:T(8,128)(2,1)S(1)} %get-tuple-element.78), channel_id=1, source_target_pairs={{0,2},{2,0},{1,3},{3,1},{4,6},{6,4},{5,7},{7,5},{8,10},{10,8},{9,1... | collective-permute-start | bytes 442376 | tf_op jit(solution)/shard_map/ppermute | solution.py:434
  15.6 10.6 %collective-permute-start.4 = (bf16[4,2,128,128]{3,2,1,0:T(8,128)(2,1)S(1)}, bf16[4,2,128,128]{3,2,1,0:T(8,128)(2,1)S(1)}, u32[]{:S(2)}, u32[]{:S(2)}) collective-permute-start(bf16[4,2,128,128]{3,2,1,0:T(8,128)(2,1)S(1)} %add_convert_fusion.3), channel_id=1, source_target_pairs={{0,2},{2,0},{1,3},{3,1},{4,6},{6,4},{5,7},{7,5},{8,10},{10,8},{9,1... | collective-permute-start | bytes 786440 | tf_op jit(solution)/shard_map/ppermute | solution.py:434
  16.6 5.8 %collective-permute-start.7 = (bf16[4,2,128,128]{3,2,1,0:T(8,128)(2,1)S(1)}, bf16[4,2,128,128]{3,2,1,0:T(8,128)(2,1)S(1)}, u32[]{:S(2)}, u32[]{:S(2)}) collective-permute-start(bf16[4,2,128,128]{3,2,1,0:T(8,128)(2,1)S(1)} %get-tuple-element.84), channel_id=1, source_target_pairs={{0,1},{1,0},{2,3},{3,2},{4,5},{5,4},{6,7},{7,6},{8,9},{9,8},{10,11... | collective-permute-start | bytes 786440 | tf_op jit(solution)/shard_map/ppermute | solution.py:434
  17.3 5.2 %collective-permute-start.9 = (bf16[4,2,128,128]{3,2,1,0:T(8,128)(2,1)S(1)}, bf16[4,2,128,128]{3,2,1,0:T(8,128)(2,1)S(1)}, u32[]{:S(2)}, u32[]{:S(2)}) collective-permute-start(bf16[4,2,128,128]{3,2,1,0:T(8,128)(2,1)S(1)} %get-tuple-element.89), channel_id=1, source_target_pairs={{0,1},{1,0},{2,3},{3,2},{4,5},{5,4},{6,7},{7,6},{8,9},{9,8},{10,11... | collective-permute-start | bytes 786440 | tf_op jit(solution)/shard_map/ppermute | solution.py:434
  18.5 4.1 %collective-permute-start.8 = (bf16[4,2,128,128]{3,2,1,0:T(8,128)(2,1)S(1)}, bf16[4,2,128,128]{3,2,1,0:T(8,128)(2,1)S(1)}, u32[]{:S(2)}, u32[]{:S(2)}) collective-permute-start(bf16[4,2,128,128]{3,2,1,0:T(8,128)(2,1)S(1)} %get-tuple-element.87), channel_id=1, source_target_pairs={{0,1},{1,0},{2,3},{3,2},{4,5},{5,4},{6,7},{7,6},{8,9},{9,8},{10,11... | collective-permute-start | bytes 786440 | tf_op jit(solution)/shard_map/ppermute | solution.py:434
  20.6 5.2 %collective-permute-start.3 = (bf16[576,128]{1,0:T(8,128)(2,1)S(1)}, bf16[576,128]{1,0:T(8,128)(2,1)S(1)}, u32[]{:S(2)}, u32[]{:S(2)}) collective-permute-start(bf16[576,128]{1,0:T(8,128)(2,1)S(1)} %add_convert_fusion.6), channel_id=1, source_target_pairs={{0,4},{4,0},{8,12},{12,8},{16,20},{20,16},{24,28},{28,24},{1,5},{5... | collective-permute-start | bytes 442376 | tf_op jit(solution)/shard_map/ppermute | solution.py:434
  22.7 19.6 %collective-permute-start.10 = (bf16[12,2,128,128]{3,2,1,0:T(8,128)(2,1)S(1)}, bf16[12,2,128,128]{3,2,1,0:T(8,128)(2,1)S(1)}, u32[]{:S(2)}, u32[]{:S(2)}) collective-permute-start(bf16[12,2,128,128]{3,2,1,0:T(8,128)(2,1)S(1)} %pad_maximum_fusion), channel_id=1, source_target_pairs={{0,2},{2,0},{1,3},{3,1},{4,6},{6,4},{5,7},{7,5},{8,10},{10,8},{9,1... | collective-permute-start | bytes 2359304 | tf_op jit(solution)/shard_map/ppermute | solution.py:434
  26.2 5.1 %collective-permute-start.5 = (bf16[576,128]{1,0:T(8,128)(2,1)S(1)}, bf16[576,128]{1,0:T(8,128)(2,1)S(1)}, u32[]{:S(2)}, u32[]{:S(2)}) collective-permute-start(bf16[576,128]{1,0:T(8,128)(2,1)S(1)} %add_convert_fusion.5), channel_id=1, source_target_pairs={{0,8},{4,12},{8,0},{12,4},{16,24},{20,28},{24,16},{28,20},{1,9},{5... | collective-permute-start | bytes 442376 | tf_op jit(solution)/shard_map/ppermute | solution.py:434
  28.0 3.4 %collective-permute-start.14 = (bf16[4,2,128,128]{3,2,1,0:T(8,128)(2,1)S(1)}, bf16[4,2,128,128]{3,2,1,0:T(8,128)(2,1)S(1)}, u32[]{:S(2)}, u32[]{:S(2)}) collective-permute-start(bf16[4,2,128,128]{3,2,1,0:T(8,128)(2,1)S(1)} %get-tuple-element.98), channel_id=1, source_target_pairs={{0,1},{1,0},{2,3},{3,2},{4,5},{5,4},{6,7},{7,6},{8,9},{9,8},{10,11... | collective-permute-start | bytes 786440 | tf_op jit(solution)/shard_map/ppermute | solution.py:434
  28.0 12.7 %collective-permute-start.11 = (bf16[4,2,128,128]{3,2,1,0:T(8,128)(2,1)S(1)}, bf16[4,2,128,128]{3,2,1,0:T(8,128)(2,1)S(1)}, u32[]{:S(2)}, u32[]{:S(2)}) collective-permute-start(bf16[4,2,128,128]{3,2,1,0:T(8,128)(2,1)S(1)} %get-tuple-element.91), channel_id=1, source_target_pairs={{0,1},{1,0},{2,3},{3,2},{4,5},{5,4},{6,7},{7,6},{8,9},{9,8},{10,11... | collective-permute-start | bytes 786440 | tf_op jit(solution)/shard_map/ppermute | solution.py:434
  28.5 12.2 %collective-permute-start.13 = (bf16[4,2,128,128]{3,2,1,0:T(8,128)(2,1)S(1)}, bf16[4,2,128,128]{3,2,1,0:T(8,128)(2,1)S(1)}, u32[]{:S(2)}, u32[]{:S(2)}) collective-permute-start(bf16[4,2,128,128]{3,2,1,0:T(8,128)(2,1)S(1)} %get-tuple-element.95), channel_id=1, source_target_pairs={{0,1},{1,0},{2,3},{3,2},{4,5},{5,4},{6,7},{7,6},{8,9},{9,8},{10,11... | collective-permute-start | bytes 786440 | tf_op jit(solution)/shard_map/ppermute | solution.py:434
  31.3 9.4 %collective-permute-start.12 = (bf16[4,2,128,128]{3,2,1,0:T(8,128)(2,1)S(1)}, bf16[4,2,128,128]{3,2,1,0:T(8,128)(2,1)S(1)}, u32[]{:S(2)}, u32[]{:S(2)}) collective-permute-start(bf16[4,2,128,128]{3,2,1,0:T(8,128)(2,1)S(1)} %get-tuple-element.93), channel_id=1, source_target_pairs={{0,1},{1,0},{2,3},{3,2},{4,5},{5,4},{6,7},{7,6},{8,9},{9,8},{10,11... | collective-permute-start | bytes 786440 | tf_op jit(solution)/shard_map/ppermute | solution.py:434
  31.4 8.5 %collective-permute-start.6 = (bf16[576,128]{1,0:T(8,128)(2,1)S(1)}, bf16[576,128]{1,0:T(8,128)(2,1)S(1)}, u32[]{:S(2)}, u32[]{:S(2)}) collective-permute-start(bf16[576,128]{1,0:T(8,128)(2,1)S(1)} %add_convert_fusion.4.one_ref), channel_id=1, source_target_pairs={{0,24},{4,28},{8,16},{12,20},{16,8},{20,12},{24,0},{28,4},{1,25},{... | collective-permute-start | bytes 442376 | tf_op jit(solution)/shard_map/ppermute | solution.py:434

commit v7 on v6

--- a/solution.py
+++ b/solution.py
@@ -177,7 +177,7 @@
         turned_values(paired, latent, vt_ref)
         group = bp_ref.shape[1] * bp_ref.shape[0] // nope_width
     else:
-        group = min(4, count)
+        group = min(8, count)
     if not first:
         total = before_ref[...]
         total_latent, total_rotary = total[:, :latent_width], total[:, latent_width:]

time: 43.8 us -> 43.8 us (level)
  no operation moved by 1% of the time
where the time goes in v7:
time: 43.8 us; the launch traced here: 43.6 us
  Pallas kernels  15.7 us (36%)
  starting transfers between devices  15.5 us (35%)
  waiting for transfers between devices  11.1 us (25%)
  between operations  0.79 us (2%)
  other arithmetic  0.5 us (1%)
    ppermute x15, starting transfers between devices, swap(): return lax.ppermute(x, axis, [(i, i ^ bits) for i in range(size)])  15.5 us
    ppermute x15, waiting for transfers between devices, swap(): return lax.ppermute(x, axis, [(i, i ^ bits) for i in range(size)])  11.1 us
    pallas_call x3, Pallas kernels, attend(): pl.pallas_call(functools.partial(attend_kernel, paired, before is None, f...  5.3 us
    pallas_call x1, Pallas kernels, prepare(): pl.pallas_call(functools.partial(prepare_kernel, parts, page_rows), in_sp...  3.71 us
    pallas_call x2, Pallas kernels, finish(): pl.pallas_call(functools.partial(finish_kernel, places, not before), in_s...  2.1 us
    pallas_call x1, Pallas kernels, query_gradient(): pl.pallas_call(functools.partial(query_kernel, counts, len(parts)), out_s...  1.92 us
    pallas_call x3, Pallas kernels, weight_partials(): pl.pallas_call(functools.partial(weights_kernel, True, len(parts), spans,...  1.91 us
  transfers between devices with their start and end apart: 15, of which 8 were waited for; matrix products, arithmetic and copies ran while one was open for 1% of the time, Pallas kernels for 24%

profile of v7, /device:TPU:0, one launch (start us, length us, event | category | flops | bytes accessed | tf_op | source)
XLA Modules:
  0.0 43.6 jit_solution(6285006098915094386)
XLA Ops:
  0.6 3.0 %collective-permute-start = (bf16[128,576]{1,0:T(8,128)(2,1)}, bf16[128,576]{1,0:T(8,128)(2,1)S(1)}, u32[]{:S(2)}, u32[]{:S(2)}) collective-permute-start(bf16[128,576]{1,0:T(8,128)(2,1)} %bitcast.15), channel_id=1, source_target_pairs={{0,2},{2,0},{1,3},{3,1},{4,6},{6,4},{5,7},{7,5},{8,10},{10,8},{9,1... | collective-permute-start | bytes 442376 | tf_op jit(solution)/shard_map/ppermute | solution.py:434
  3.7 3.7 %prepare.1 = (bf16[16,192,128]{2,1,0:T(8,128)(2,1)S(1)}, bf16[16,128,128]{2,1,0:T(8,128)(2,1)S(1)}, bf16[16,128,512]{2,1,0:T(8,128)(2,1)S(1)}, bf16[16,512,128]{...) custom-call(bf16[128,16,128]{2,1,0:T(8,128)(2,1)} %bitcast.11, ...), custom_call_target="tpu_custom_call" | custom-call | flops 600000000 | bytes 12000000 | tf_op jit(solution)/shard_map/prepare/pallas_call | solution.py:103
  7.4 0.7 %collective-permute-done.rest_1_.refs_1_.rest_3_ = bf16[128,576]{1,0:T(8,128)(2,1)S(1)} collective-permute-done((bf16[128,576]{1,0:T(8,128)(2,1)}, bf16[128,576]{1,0:T(8,128)(2,1)S(1)}, u32[]{:S(2)}, u32[]{:S(2)}) %collective-permute-start) | collective-permute-done | bytes 147488 | tf_op jit(solution)/shard_map/ppermute | solution.py:434
  8.1 1.7 %attend.3 = (bf16[4,256,128]{2,1,0:T(8,128)(2,1)S(1)}, bf16[4,256,128]{2,1,0:T(8,128)(2,1)S(1)}, bf16[4,2,128,128]{3,2,1,0:T(8,128)(2,1)S(1)}, bf16[4,2,128,128]...) custom-call(bf16[16,192,128]{2,1,0:T(8,128)(2,1)S(1)} %get-tuple-ele, ...), custom_call_target="tpu_custom_call" | custom-call | flops 1600000000 | bytes 2000000 | tf_op jit(solution)/shard_map/attend/pallas_call | solution.py:287
  9.9 1.3 %attend.4 = (bf16[4,256,128]{2,1,0:T(8,128)(2,1)S(1)}, bf16[4,256,128]{2,1,0:T(8,128)(2,1)S(1)}, bf16[256,512]{1,0:T(8,128)(2,1)S(1)}, f32[256,576]{1,0:T(8,128)S(1)}) custom-call(bf16[16,192,128]{2,1,0:T(8,128)(2,1)S(1)} %get-tuple-element.55.qt_ref, bf16[16,128,128]{2,1,0:T(8,128)(2,1)S(1)} %get-tuple-element.56.go_ref, ...), custom_call_target="tpu_custom_call" | custom-call | flops 1200000000 | bytes 2000000 | tf_op jit(solution)/shard_map/attend/pallas_call | solution.py:287
  11.2 0.2 collective-permute-done.1
  11.5 2.3 %attend.5 = (bf16[8,256,128]{2,1,0:T(8,128)(2,1)S(1)}, bf16[8,256,128]{2,1,0:T(8,128)(2,1)S(1)}, bf16[256,1024]{1,0:T(8,128)(2,1)S(1)}, bf16[576,128]{1,0:T(8,128)(2,1)S(1)}, bf16[576,128]{1,0:T(8,128)(2,1)S(1)}) custom-call(bf16[16,192,128]{2,1,0:T(8,128)(2,1)S(1)} %get-tuple-element.55.qt_ref, bf16[16,128,128]{2,1,0:T(8,128)(2,1)S(1)} %get-tuple-element.56.go_ref, ...), custom_call_target="tpu_custom_call" | custom-call | flops 2400000000 | bytes 4000000 | tf_op jit(solution)/shard_map/attend/pallas_call | solution.py:287
  13.8 1.8 %collective-permute-start.2 = (bf16[576,128]{1,0:T(8,128)(2,1)S(1)}, bf16[576,128]{1,0:T(8,128)(2,1)S(1)}, u32[]{:S(2)}, u32[]{:S(2)}) collective-permute-start(bf16[576,128]{1,0:T(8,128)(2,1)S(1)} %get-tuple-element.78), channel_id=1, source_target_pairs={{0,2},{2,0},{1,3},{3,1},{4,6},{6,4},{5,7},{7,5},{8,10},{10,8},{9,1... | collective-permute-start | bytes 442376 | tf_op jit(solution)/shard_map/ppermute | solution.py:434
  15.6 0.3 collective-permute-start.4
  15.9 0.6 %weight_partials.3 = (bf16[4,2,128,128]{3,2,1,0:T(8,128)(2,1)S(1)}, bf16[4,2,128,128]{3,2,1,0:T(8,128)(2,1)S(1)}, bf16[4,2,128,128]{3,2,1,0:T(8,128)(2,1)S(1)}, bf16[4,2,128,128]{3,2,1,0:T(8,128)(2,1)S(1)}) custom-call(bf16[16,192,128]{2,1,0:T(8,128)(2,1)S(1)} %get-tuple-element.55.qt_ref, bf16[4,256,128]{2,1,0:T(8,128)(2,1)S(1)} %get-tuple-element.81.refs_4_.rest_0_, ...), custom_call_target="tpu_custom_call" | custom-call | flops 400000000 | bytes 1600000 | tf_op jit(solution)/shard_map/weight_partials/pallas_call | solution.py:317
  16.6 0.6 %weight_partials.5 = (bf16[4,2,128,128]{3,2,1,0:T(8,128)(2,1)S(1)}, bf16[4,2,128,128]{3,2,1,0:T(8,128)(2,1)S(1)}, bf16[4,2,128,128]{3,2,1,0:T(8,128)(2,1)S(1)}, bf16[4,2,128,128]{3,2,1,0:T(8,128)(2,1)S(1)}) custom-call(bf16[16,192,128]{2,1,0:T(8,128)(2,1)S(1)} %get-tuple-element.55.qt_ref, bf16[8,256,128]{2,1,0:T(8,128)(2,1)S(1)} %get-tuple-element.71.refs_6_.rest_0_, ...), custom_call_target="tpu_custom_call" | custom-call | flops 400000000 | bytes 1600000 | tf_op jit(solution)/shard_map/weight_partials/pallas_call | solution.py:317
  17.2 0.6 %collective-permute-start.9 = (bf16[4,2,128,128]{3,2,1,0:T(8,128)(2,1)S(1)}, bf16[4,2,128,128]{3,2,1,0:T(8,128)(2,1)S(1)}, u32[]{:S(2)}, u32[]{:S(2)}) collective-permute-start(bf16[4,2,128,128]{3,2,1,0:T(8,128)(2,1)S(1)} %get-tuple-element.89), channel_id=1, source_target_pairs={{0,1},{1,0},{2,3},{3,2},{4,5},{5,4},{6,7},{7,6},{8,9},{9,8},{10,11... | collective-permute-start | bytes 786440 | tf_op jit(solution)/shard_map/ppermute | solution.py:434
  17.8 0.6 %weight_partials.4 = (bf16[4,2,128,128]{3,2,1,0:T(8,128)(2,1)S(1)}, bf16[4,2,128,128]{3,2,1,0:T(8,128)(2,1)S(1)}, bf16[4,2,128,128]{3,2,1,0:T(8,128)(2,1)S(1)}, bf16[4,2,128,128]{3,2,1,0:T(8,128)(2,1)S(1)}) custom-call(bf16[16,192,128]{2,1,0:T(8,128)(2,1)S(1)} %get-tuple-element.55.qt_ref, bf16[8,256,128]{2,1,0:T(8,128)(2,1)S(1)} %get-tuple-element.71.refs_6_.rest_0_, ...), custom_call_target="tpu_custom_call" | custom-call | flops 400000000 | bytes 1600000 | tf_op jit(solution)/shard_map/weight_partials/pallas_call | solution.py:317
  18.4 0.1 collective-permute-start.8
  18.5 2.0 %collective-permute-done.2 = bf16[576,128]{1,0:T(8,128)(2,1)S(1)} collective-permute-done((bf16[576,128]{1,0:T(8,128)(2,1)S(1)}, bf16[576,128]{1,0:T(8,128)(2,1)S(1)}, u32[]{:S(2)}, u32[]{:S(2)}) %collective-permute-start.2) | collective-permute-done | bytes 147488 | tf_op jit(solution)/shard_map/ppermute | solution.py:434
  20.6 1.8 %collective-permute-start.3 = (bf16[576,128]{1,0:T(8,128)(2,1)S(1)}, bf16[576,128]{1,0:T(8,128)(2,1)S(1)}, u32[]{:S(2)}, u32[]{:S(2)}) collective-permute-start(bf16[576,128]{1,0:T(8,128)(2,1)S(1)} %add_convert_fusion.6), channel_id=1, source_target_pairs={{0,4},{4,0},{8,12},{12,8},{16,20},{20,16},{24,28},{28,24},{1,5},{5... | collective-permute-start | bytes 442376 | tf_op jit(solution)/shard_map/ppermute | solution.py:434
  22.4 0.1 add_convert_fusion
  22.5 0.1 add_convert_fusion.1
  22.6 0.1 pad_maximum_fusion
  22.7 1.6 %collective-permute-start.10 = (bf16[12,2,128,128]{3,2,1,0:T(8,128)(2,1)S(1)}, bf16[12,2,128,128]{3,2,1,0:T(8,128)(2,1)S(1)}, u32[]{:S(2)}, u32[]{:S(2)}) collective-permute-start(bf16[12,2,128,128]{3,2,1,0:T(8,128)(2,1)S(1)} %pad_maximum_fusion), channel_id=1, source_target_pairs={{0,2},{2,0},{1,3},{3,1},{4,6},{6,4},{5,7},{7,5},{8,10},{10,8},{9,1... | collective-permute-start | bytes 2359304 | tf_op jit(solution)/shard_map/ppermute | solution.py:434
  24.3 1.5 %collective-permute-done.3 = bf16[576,128]{1,0:T(8,128)(2,1)S(1)} collective-permute-done((bf16[576,128]{1,0:T(8,128)(2,1)S(1)}, bf16[576,128]{1,0:T(8,128)(2,1)S(1)}, u32[]{:S(2)}, u32[]{:S(2)}) %collective-permute-start.3) | collective-permute-done | bytes 147488 | tf_op jit(solution)/shard_map/ppermute | solution.py:434
  25.8 0.3 collective-permute-done.4.far_ref
  26.1 1.8 %collective-permute-start.5 = (bf16[576,128]{1,0:T(8,128)(2,1)S(1)}, bf16[576,128]{1,0:T(8,128)(2,1)S(1)}, u32[]{:S(2)}, u32[]{:S(2)}) collective-permute-start(bf16[576,128]{1,0:T(8,128)(2,1)S(1)} %add_convert_fusion.5), channel_id=1, source_target_pairs={{0,8},{4,12},{8,0},{12,4},{16,24},{20,28},{24,16},{28,20},{1,9},{5... | collective-permute-start | bytes 442376 | tf_op jit(solution)/shard_map/ppermute | solution.py:434
  27.9 0.5 %collective-permute-start.11 = (bf16[4,2,128,128]{3,2,1,0:T(8,128)(2,1)S(1)}, bf16[4,2,128,128]{3,2,1,0:T(8,128)(2,1)S(1)}, u32[]{:S(2)}, u32[]{:S(2)}) collective-permute-start(bf16[4,2,128,128]{3,2,1,0:T(8,128)(2,1)S(1)} %get-tuple-element.91), channel_id=1, source_target_pairs={{0,1},{1,0},{2,3},{3,2},{4,5},{5,4},{6,7},{7,6},{8,9},{9,8},{10,11... | collective-permute-start | bytes 786440 | tf_op jit(solution)/shard_map/ppermute | solution.py:434
  28.5 2.8 %collective-permute-done.5 = bf16[576,128]{1,0:T(8,128)(2,1)S(1)} collective-permute-done((bf16[576,128]{1,0:T(8,128)(2,1)S(1)}, bf16[576,128]{1,0:T(8,128)(2,1)S(1)}, u32[]{:S(2)}, u32[]{:S(2)}) %collective-permute-start.5) | collective-permute-done | bytes 147488 | tf_op jit(solution)/shard_map/ppermute | solution.py:434
  31.3 3.9 %collective-permute-start.6 = (bf16[576,128]{1,0:T(8,128)(2,1)S(1)}, bf16[576,128]{1,0:T(8,128)(2,1)S(1)}, u32[]{:S(2)}, u32[]{:S(2)}) collective-permute-start(bf16[576,128]{1,0:T(8,128)(2,1)S(1)} %add_convert_fusion.4.one_ref), channel_id=1, source_target_pairs={{0,24},{4,28},{8,16},{12,20},{16,8},{20,12},{24,0},{28,4},{1,25},{... | collective-permute-start | bytes 442376 | tf_op jit(solution)/shard_map/ppermute | solution.py:434
  35.2 1.9 %query_gradient.1 = (f32[2048,128]{1,0:T(8,128)}, f32[16,64,128]{2,1,0:T(8,128)}) custom-call(bf16[128,576]{1,0:T(8,128)(2,1)S(1)} %get-tuple-element.54.rest_0_.refs_0_.rest_2_, bf16[128,576]{1,0:T(8,128)(2,1)S(1)} %collective-permute-done.rest_1_.refs_1_.rest_3_, bf16[4,256,128]{2,1,0:T(8,128)(2,1)S(1)} %get-tuple-element.62.refs_2_, ...), custom_call_target="tpu_custom_call" | custom-call | flops 1000000000 | bytes 5000000 | tf_op jit(solution)/shard_map/query_gradient/pallas_call | solution.py:349
  37.2 0.8 %finish.2 = (f32[16,32,512]{2,1,0:T(8,128)}, f32[16,128,128]{2,1,0:T(8,128)}) custom-call(bf16[4,2,128,128]{3,2,1,0:T(8,128)(2,1)S(1)} %collective-permute-done.4.far_ref, bf16[4,2,128,128]{3,2,1,0:T(8,128)(2,1)S(1)} %get-tuple-element.97.rest_0_, bf16[4,2,128,128]{3,2,1,0:T(8,128)(2,1)S(1)} %collective-permute-done.14.rest_1_), custom_call_target="tpu_custom_call" | custom-call | flops 1000000 | bytes 1200000 | tf_op jit(solution)/shard_map/finish/pallas_call | solution.py:413
  38.0 1.9 %collective-permute-done.6.two_ref = bf16[576,128]{1,0:T(8,128)(2,1)S(1)} collective-permute-done((bf16[576,128]{1,0:T(8,128)(2,1)S(1)}, bf16[576,128]{1,0:T(8,128)(2,1)S(1)}, u32[]{:S(2)}, u32[]{:S(2)}) %collective-permute-start.6) | collective-permute-done | bytes 147488 | tf_op jit(solution)/shard_map/ppermute | solution.py:434
  39.9 0.8 %unpack.1 = f32[128,576]{1,0:T(8,128)} custom-call(bf16[576,128]{1,0:T(8,128)(2,1)S(1)} %add_convert_fusion.4.one_ref, bf16[576,128]{1,0:T(8,128)(2,1)S(1)} %collective-permute-done.6.two_ref), custom_call_target="tpu_custom_call" | custom-call | flops 1000000 | bytes 600000 | tf_op jit(solution)/shard_map/unpack/pallas_call | solution.py:374
  40.7 1.7 %collective-permute-done.10.far_ref = bf16[12,2,128,128]{3,2,1,0:T(8,128)(2,1)S(1)} collective-permute-done((bf16[12,2,128,128]{3,2,1,0:T(8,128)(2,1)S(1)}, bf16[12,2,128,128]{3,2,1,0:T(8,128)(2,1)S(1)}, u32[]{:S(2)}, u32[]{:S(2)}) %collective-permute-start.10) | collective-permute-done | bytes 786464 | tf_op jit(solution)/shard_map/ppermute | solution.py:434
  42.4 1.3 %finish.3 = (f32[16,32,512]{2,1,0:T(8,128)}, f32[16,128,128]{2,1,0:T(8,128)}) custom-call(bf16[12,2,128,128]{3,2,1,0:T(8,128)(2,1)S(1)} %collective-permute-done.10.far_ref, bf16[4,2,128,128]{3,2,1,0:T(8,128)(2,1)S(1)} %get-tuple-element.90.rest_0_, ...), custom_call_target="tpu_custom_call", output_to_operand_aliasing={{0}: (7, {}), {1}: (8, {})} | custom-call | flops 1000000 | bytes 3600000 | tf_op jit(solution)/shard_map/finish/pallas_call | solution.py:413
  (17 shorter events, 0.4 us)
Async XLA Ops:
  0.6 7.4 %collective-permute-start = (bf16[128,576]{1,0:T(8,128)(2,1)}, bf16[128,576]{1,0:T(8,128)(2,1)S(1)}, u32[]{:S(2)}, u32[]{:S(2)}) collective-permute-start(bf16[128,576]{1,0:T(8,128)(2,1)} %bitcast.15), channel_id=1, source_target_pairs={{0,2},{2,0},{1,3},{3,1},{4,6},{6,4},{5,7},{7,5},{8,10},{10,8},{9,1... | collective-permute-start | bytes 442376 | tf_op jit(solution)/shard_map/ppermute | solution.py:434
  9.8 1.6 %collective-permute-start.1 = (bf16[4,2,128,128]{3,2,1,0:T(8,128)(2,1)S(1)}, bf16[4,2,128,128]{3,2,1,0:T(8,128)(2,1)S(1)}, u32[]{:S(2)}, u32[]{:S(2)}) collective-permute-start(bf16[4,2,128,128]{3,2,1,0:T(8,128)(2,1)S(1)} %get-tuple-element.69), channel_id=1, source_target_pairs={{0,1},{1,0},{2,3},{3,2},{4,5},{5,4},{6,7},{7,6},{8,9},{9,8},{10,11... | collective-permute-start | bytes 786440 | tf_op jit(solution)/shard_map/ppermute | solution.py:434
  13.8 6.7 %collective-permute-start.2 = (bf16[576,128]{1,0:T(8,128)(2,1)S(1)}, bf16[576,128]{1,0:T(8,128)(2,1)S(1)}, u32[]{:S(2)}, u32[]{:S(2)}) collective-permute-start(bf16[576,128]{1,0:T(8,128)(2,1)S(1)} %get-tuple-element.78), channel_id=1, source_target_pairs={{0,2},{2,0},{1,3},{3,1},{4,6},{6,4},{5,7},{7,5},{8,10},{10,8},{9,1... | collective-permute-start | bytes 442376 | tf_op jit(solution)/shard_map/ppermute | solution.py:434
  15.6 10.6 %collective-permute-start.4 = (bf16[4,2,128,128]{3,2,1,0:T(8,128)(2,1)S(1)}, bf16[4,2,128,128]{3,2,1,0:T(8,128)(2,1)S(1)}, u32[]{:S(2)}, u32[]{:S(2)}) collective-permute-start(bf16[4,2,128,128]{3,2,1,0:T(8,128)(2,1)S(1)} %add_convert_fusion.3), channel_id=1, source_target_pairs={{0,2},{2,0},{1,3},{3,1},{4,6},{6,4},{5,7},{7,5},{8,10},{10,8},{9,1... | collective-permute-start | bytes 786440 | tf_op jit(solution)/shard_map/ppermute | solution.py:434
  16.5 5.8 %collective-permute-start.7 = (bf16[4,2,128,128]{3,2,1,0:T(8,128)(2,1)S(1)}, bf16[4,2,128,128]{3,2,1,0:T(8,128)(2,1)S(1)}, u32[]{:S(2)}, u32[]{:S(2)}) collective-permute-start(bf16[4,2,128,128]{3,2,1,0:T(8,128)(2,1)S(1)} %get-tuple-element.84), channel_id=1, source_target_pairs={{0,1},{1,0},{2,3},{3,2},{4,5},{5,4},{6,7},{7,6},{8,9},{9,8},{10,11... | collective-permute-start | bytes 786440 | tf_op jit(solution)/shard_map/ppermute | solution.py:434
  17.2 5.2 %collective-permute-start.9 = (bf16[4,2,128,128]{3,2,1,0:T(8,128)(2,1)S(1)}, bf16[4,2,128,128]{3,2,1,0:T(8,128)(2,1)S(1)}, u32[]{:S(2)}, u32[]{:S(2)}) collective-permute-start(bf16[4,2,128,128]{3,2,1,0:T(8,128)(2,1)S(1)} %get-tuple-element.89), channel_id=1, source_target_pairs={{0,1},{1,0},{2,3},{3,2},{4,5},{5,4},{6,7},{7,6},{8,9},{9,8},{10,11... | collective-permute-start | bytes 786440 | tf_op jit(solution)/shard_map/ppermute | solution.py:434
  18.4 4.1 %collective-permute-start.8 = (bf16[4,2,128,128]{3,2,1,0:T(8,128)(2,1)S(1)}, bf16[4,2,128,128]{3,2,1,0:T(8,128)(2,1)S(1)}, u32[]{:S(2)}, u32[]{:S(2)}) collective-permute-start(bf16[4,2,128,128]{3,2,1,0:T(8,128)(2,1)S(1)} %get-tuple-element.87), channel_id=1, source_target_pairs={{0,1},{1,0},{2,3},{3,2},{4,5},{5,4},{6,7},{7,6},{8,9},{9,8},{10,11... | collective-permute-start | bytes 786440 | tf_op jit(solution)/shard_map/ppermute | solution.py:434
  20.6 5.2 %collective-permute-start.3 = (bf16[576,128]{1,0:T(8,128)(2,1)S(1)}, bf16[576,128]{1,0:T(8,128)(2,1)S(1)}, u32[]{:S(2)}, u32[]{:S(2)}) collective-permute-start(bf16[576,128]{1,0:T(8,128)(2,1)S(1)} %add_convert_fusion.6), channel_id=1, source_target_pairs={{0,4},{4,0},{8,12},{12,8},{16,20},{20,16},{24,28},{28,24},{1,5},{5... | collective-permute-start | bytes 442376 | tf_op jit(solution)/shard_map/ppermute | solution.py:434
  22.7 19.6 %collective-permute-start.10 = (bf16[12,2,128,128]{3,2,1,0:T(8,128)(2,1)S(1)}, bf16[12,2,128,128]{3,2,1,0:T(8,128)(2,1)S(1)}, u32[]{:S(2)}, u32[]{:S(2)}) collective-permute-start(bf16[12,2,128,128]{3,2,1,0:T(8,128)(2,1)S(1)} %pad_maximum_fusion), channel_id=1, source_target_pairs={{0,2},{2,0},{1,3},{3,1},{4,6},{6,4},{5,7},{7,5},{8,10},{10,8},{9,1... | collective-permute-start | bytes 2359304 | tf_op jit(solution)/shard_map/ppermute | solution.py:434
  26.1 5.1 %collective-permute-start.5 = (bf16[576,128]{1,0:T(8,128)(2,1)S(1)}, bf16[576,128]{1,0:T(8,128)(2,1)S(1)}, u32[]{:S(2)}, u32[]{:S(2)}) collective-permute-start(bf16[576,128]{1,0:T(8,128)(2,1)S(1)} %add_convert_fusion.5), channel_id=1, source_target_pairs={{0,8},{4,12},{8,0},{12,4},{16,24},{20,28},{24,16},{28,20},{1,9},{5... | collective-permute-start | bytes 442376 | tf_op jit(solution)/shard_map/ppermute | solution.py:434
  27.9 3.4 %collective-permute-start.14 = (bf16[4,2,128,128]{3,2,1,0:T(8,128)(2,1)S(1)}, bf16[4,2,128,128]{3,2,1,0:T(8,128)(2,1)S(1)}, u32[]{:S(2)}, u32[]{:S(2)}) collective-permute-start(bf16[4,2,128,128]{3,2,1,0:T(8,128)(2,1)S(1)} %get-tuple-element.98), channel_id=1, source_target_pairs={{0,1},{1,0},{2,3},{3,2},{4,5},{5,4},{6,7},{7,6},{8,9},{9,8},{10,11... | collective-permute-start | bytes 786440 | tf_op jit(solution)/shard_map/ppermute | solution.py:434
  27.9 12.7 %collective-permute-start.11 = (bf16[4,2,128,128]{3,2,1,0:T(8,128)(2,1)S(1)}, bf16[4,2,128,128]{3,2,1,0:T(8,128)(2,1)S(1)}, u32[]{:S(2)}, u32[]{:S(2)}) collective-permute-start(bf16[4,2,128,128]{3,2,1,0:T(8,128)(2,1)S(1)} %get-tuple-element.91), channel_id=1, source_target_pairs={{0,1},{1,0},{2,3},{3,2},{4,5},{5,4},{6,7},{7,6},{8,9},{9,8},{10,11... | collective-permute-start | bytes 786440 | tf_op jit(solution)/shard_map/ppermute | solution.py:434
  28.5 12.2 %collective-permute-start.13 = (bf16[4,2,128,128]{3,2,1,0:T(8,128)(2,1)S(1)}, bf16[4,2,128,128]{3,2,1,0:T(8,128)(2,1)S(1)}, u32[]{:S(2)}, u32[]{:S(2)}) collective-permute-start(bf16[4,2,128,128]{3,2,1,0:T(8,128)(2,1)S(1)} %get-tuple-element.95), channel_id=1, source_target_pairs={{0,1},{1,0},{2,3},{3,2},{4,5},{5,4},{6,7},{7,6},{8,9},{9,8},{10,11... | collective-permute-start | bytes 786440 | tf_op jit(solution)/shard_map/ppermute | solution.py:434
  31.3 9.4 %collective-permute-start.12 = (bf16[4,2,128,128]{3,2,1,0:T(8,128)(2,1)S(1)}, bf16[4,2,128,128]{3,2,1,0:T(8,128)(2,1)S(1)}, u32[]{:S(2)}, u32[]{:S(2)}) collective-permute-start(bf16[4,2,128,128]{3,2,1,0:T(8,128)(2,1)S(1)} %get-tuple-element.93), channel_id=1, source_target_pairs={{0,1},{1,0},{2,3},{3,2},{4,5},{5,4},{6,7},{7,6},{8,9},{9,8},{10,11... | collective-permute-start | bytes 786440 | tf_op jit(solution)/shard_map/ppermute | solution.py:434
  31.3 8.5 %collective-permute-start.6 = (bf16[576,128]{1,0:T(8,128)(2,1)S(1)}, bf16[576,128]{1,0:T(8,128)(2,1)S(1)}, u32[]{:S(2)}, u32[]{:S(2)}) collective-permute-start(bf16[576,128]{1,0:T(8,128)(2,1)S(1)} %add_convert_fusion.4.one_ref), channel_id=1, source_target_pairs={{0,24},{4,28},{8,16},{12,20},{16,8},{20,12},{24,0},{28,4},{1,25},{... | collective-permute-start | bytes 442376 | tf_op jit(solution)/shard_map/ppermute | solution.py:434
